TPU v7x, 32 devices: a whole 2x2x4 slice. The times are simulated.
32 devices in a mesh: section: 4 (over y, x), row: 8 (over z, core).
Axes of the slice: x: 2, y: 2, z: 4, core: 2. Of those that a mesh axis runs over, the one named last changes fastest.
Arguments:
- features: bfloat16 [4, 4, 32, 256, 128], P('section', None, 'row'), may hold values from -6 to 6
- conv_weight: bfloat16 [4, 1152, 128], P('section'), may hold values from -0.1875 to 0.1875
- norm_gain: float32 [4, 128], P('section'), may hold values from 0.5 to 1.5
- norm_bias: float32 [4, 128], P('section'), may hold values from -3 to 3
- valid_mask: int32 [4, 4, 32, 256], P(None, None, 'row'), may hold values from 0 to 1
- out_cotangent: bfloat16 [4, 4, 32, 256, 128], P('section', None, 'row'), may hold values from -6 to 6
Outputs:
- neck_output: bfloat16 [4, 4, 32, 256, 128], P('section', None, 'row')
- feature_grad: bfloat16 [4, 4, 32, 256, 128], P('section', None, 'row')
- weight_grad: float32 [4, 1152, 128], P('section', 'row')
- gain_grad: float32 [4, 128], P('section')
- bias_grad: float32 [4, 128], P('section')
All inputs are finite; a program needn't handle non-finite values.
Results may differ from a plain program's by a relative error of at most 0.011.
Values may be sent and summed in bfloat16 or wider, within the bound.
No kernel may reach another device: no remote copies, remote signals or barrier semaphores. Data moves between devices by JAX's collectives and lax.ppermute only.
A program may use at most 128 MiB of HBM per device.

v0:
```python
import functools

import jax
import jax.numpy as jnp
from jax import lax
from jax.experimental import pallas as pl
from jax.experimental.pallas import tpu as pltpu
from jax.sharding import PartitionSpec as P

norm_eps = 1e-05
hole = -1e30
hole_edge = -1e29
f32 = jnp.float32
bf16 = jnp.bfloat16
VMEM_SPEC = pl.BlockSpec(memory_space=pltpu.VMEM)


class Place:
    def __init__(self):
        tile = lax.axis_index("row")
        self.section = lax.axis_index("section")
        self.core = lax.rem(tile, 2)
        self.even = self.core == 0
        self.chip = tile // 2
        outer = jnp.where(self.even, 0, lax.axis_size("row") - 1)
        self.inside = (tile != outer).astype(f32)

    def row(self, q, rows):
        return jnp.where(self.even, rows - 1 - q, q)

    def tap(self, i):
        return jnp.where(self.even, 2 - i, i)


def shifted(value, step):
    cols = value.shape[0]
    index = lax.broadcasted_iota(jnp.int32, value.shape, 0)
    edge = 0 if step == 1 else cols - 1
    return jnp.where(index == edge, 0.0, pltpu.roll(value, step % cols, 0))


def shifts(value, flip):
    left, right = shifted(value, 1).astype(bf16), shifted(value, -1).astype(bf16)
    return (right, value.astype(bf16), left) if flip else (left, value.astype(bf16), right)


def put_row(stack, scene, k, value, flip):
    ch = value.shape[1]
    for j, part in enumerate(shifts(value, flip)):
        stack[j, k // 2, scene, :, (k % 2) * ch : (k % 2 + 1) * ch] = part


def put_outer(outer, scene, value, flip):
    for j, part in enumerate(shifts(value, flip)):
        outer[j, scene] = part


def put_blocks(kernel_rows, blocks):
    ch = kernel_rows.shape[1]

    def tap(i, j):
        return kernel_rows[(3 * i + j) * ch : (3 * i + j + 1) * ch, :]

    zero = jnp.zeros((ch, ch), bf16)
    for j in range(3):
        blocks[2 * j, :ch, :ch] = tap(0, j)
        blocks[2 * j, :ch, ch:] = zero
        blocks[2 * j, ch:, :ch] = tap(1, j)
        blocks[2 * j, ch:, ch:] = tap(0, j)
        blocks[2 * j + 1, :ch, :ch] = tap(2, j)
        blocks[2 * j + 1, :ch, ch:] = tap(1, j)
        blocks[2 * j + 1, ch:, :ch] = zero
        blocks[2 * j + 1, ch:, ch:] = tap(2, j)


def operand(stack, outer, scene, j, pair):
    if outer is None or pair + 1 < stack.shape[1]:
        return stack[j, pair, scene]
    ch = outer.shape[-1]
    return jnp.concatenate([stack[j, pair, scene, :, :ch], outer[j, scene]], axis=1)


def conv_pair(stack, outer, blocks, scene, p):
    lhs = [operand(stack, outer, scene, j, p + h) for j in range(3) for h in range(2)]
    rhs = jnp.concatenate([blocks[n] for n in range(6)], axis=0)
    return jnp.dot(jnp.concatenate(lhs, axis=1), rhs, preferred_element_type=f32)


def conv_back_pair(stack, outer, blocks, scene, p):
    total = None
    for j in range(3):
        for h in range(2):
            term = lax.dot_general(
                operand(stack, outer, scene, j, p + h),
                blocks[2 * j + 1 - h],
                (((1,), (1,)), ((), ())),
                preferred_element_type=f32,
            )
            total = term if total is None else total + term
    return total


def summed(pieces):
    total = pieces[0][...]
    for piece in pieces[1:]:
        total = total + piece[...]
    return total


def norm_stats(total, count):
    count = total[2:3] if count is None else count
    mean = total[0:1] / count
    inv = lax.rsqrt(total[1:2] / count - mean * mean + norm_eps)
    return mean, inv, count


def half_affine(mean, inv, gb):
    scale = inv * gb[0:1]
    return 0.5 * scale, 0.5 * (gb[1:2] - mean * scale)


def twice_slope(half, t):
    return (1.0 + t) + half * (1.0 - t * t)


def fold(value):
    return jnp.sum(value.reshape(-1, 8, value.shape[-1]), axis=0)


def plus(total, term):
    return term if total is None else total + term


def sum_rows(first, second, third=None):
    ch = first.shape[1]
    rows = [jnp.sum(first, axis=0, keepdims=True), jnp.sum(second, axis=0, keepdims=True)]
    rows.append(jnp.zeros((1, ch), f32) if third is None else third)
    return jnp.concatenate(rows + [jnp.zeros((5, ch), f32)], axis=0)


def put_parts(out, start, total):
    hi = total.astype(bf16).astype(f32)
    left = total - hi
    mid = left.astype(bf16).astype(f32)
    parts = [hi, mid, left - mid, jnp.zeros_like(total)]
    out[start : start + 16, :] = jnp.concatenate(parts[:2], axis=0).astype(bf16)
    out[start + 16 : start + 32, :] = jnp.concatenate(parts[2:], axis=0).astype(bf16)


def put_sums(sums, near, total):
    sums[...] = total
    if near is not None:
        put_parts(near, near.shape[0] - 32, total)


def mask_columns(rows):
    count, cols = rows.shape
    filled = jnp.concatenate([rows, jnp.zeros((128 - count, cols), f32)], axis=0)
    return filled.T


def mask_rows(place, mask):
    scenes, rows = mask.shape[1:3]
    parts = []
    for s in range(scenes):
        parts += [mask[place.section, s, pl.ds(place.row(q, rows), 1), :].astype(f32) for q in range(rows)]
    return jnp.concatenate(parts, axis=0)


def prep_kernel(mask, features, cot, weight, gain, bias, near, far, out, held, rows_mask, both, sems):
    place = Place()
    scenes, rows, cols, ch = features.shape[1:]
    half = weight.shape[1] // 2
    mine = pl.ds(pl.multiple_of(place.core * half, 16), half)
    moves = [
        (weight.at[0, mine], out.at[pl.ds(0, half)]),
        (gain, both.at[pl.ds(0, 1)]),
        (bias, both.at[pl.ds(1, 1)]),
        (mask.at[pl.ds(place.section, 1)], rows_mask),
    ]
    for source in (features, cot):
        for q in (0, rows - 1):
            moves.append((source.at[0, :, place.row(q, rows)], held.at[len(moves) - 4]))
    copies = [pltpu.make_async_copy(a, b, sems.at[n]) for n, (a, b) in enumerate(moves)]
    for copy in copies:
        copy.start()
    both[2:8] = jnp.zeros((6, ch), f32)
    for copy in copies:
        copy.wait()
    put_parts(out, half, both[...])
    parts = []
    for s in range(scenes):
        for q in (0, rows - 1):
            parts.append(rows_mask[0, s, pl.ds(place.row(q, rows), 1), :].astype(f32))
    columns = mask_columns(jnp.concatenate(parts, axis=0))
    size = scenes * cols
    for s in range(scenes):
        here = slice(s * cols, (s + 1) * cols)
        there = slice(size + s * cols, size + (s + 1) * cols)
        for n, edge in enumerate((near, far)):
            at = 2 * s + n
            edge[here, :] = (held[n, s].astype(f32) * columns[:, at : at + 1]).astype(bf16)
            edge[there, :] = held[2 + n, s]


def gather_kernel(own, gain, bias, r1, r2, r3, other, weights, gbs):
    place = Place()
    taps, ch = own.shape[1:]
    piece = taps // 6

    def put(section, p, rows):
        at = (2 * place.tap(p // 2) + p % 2) * piece
        weights[section, pl.ds(pl.multiple_of(at, 16), piece), :] = rows

    for p in range(6):
        put(place.section, p, own[0, p * piece : (p + 1) * piece])
    gbs[place.section] = jnp.concatenate([gain[...], bias[...], jnp.zeros((6, ch), f32)], axis=0)
    for d, got in ((1, r1), (2, r2), (3, r3)):
        there = place.section ^ d
        for n in range(3):
            rows = slice(n * piece, (n + 1) * piece)
            put(there, 3 * place.core + n, got[rows])
            put(there, 3 * (1 - place.core) + n, other[d - 1, rows])
        parts = got[3 * piece :].astype(f32)
        gbs[there] = parts[0:8] + parts[8:16] + parts[16:24]


def far_kernel(rows_ref, far):
    scenes, rows, cols, ch = rows_ref.shape
    for s in range(scenes):
        far[s * cols : (s + 1) * cols, :] = rows_ref[s, rows - 1].astype(bf16)


def finish_forward(stack, blocks, pre, near, sums, make_rows, columns, third):
    scenes, rows, cols, ch = pre.shape
    first = second = None
    make_rows(0)
    for scene in range(scenes):
        if scene + 1 < scenes:
            make_rows(scene + 1)
        for p in range(rows // 2):
            both = conv_pair(stack, None, blocks, scene, p)
            for n in range(2):
                r = 2 * p + n
                kept = row = both[:, n * ch : (n + 1) * ch]
                if columns is not None:
                    at = scene * rows + r
                    inside = columns[:, at : at + 1] > 0.5
                    kept = jnp.where(inside, row, hole)
                    row = jnp.where(inside, row, 0.0)
                pre[scene, r] = kept
                if r == 0:
                    near[scene * cols : (scene + 1) * cols, :] = kept.astype(bf16)
                first = plus(first, fold(row))
                second = plus(second, fold(row * row))
    put_sums(sums, near, sum_rows(first, second, third))


def first_kernel(mask, features, near, far, weights, x, pre, near_out, sums, stack, blocks):
    scenes, rows, cols, ch = features.shape[1:]
    put_blocks(weights.at[0], blocks)
    place = Place()
    mask_now = mask_rows(place, mask)
    columns = mask_columns(mask_now)

    def make_rows(scene):
        here = slice(scene * cols, (scene + 1) * cols)
        for k in range(rows + 2):
            if k == 0:
                value = near[here, :].astype(f32)
            elif k == rows + 1:
                value = far[here, :].astype(f32)
            else:
                at = scene * rows + k - 1
                value = features[0, scene, place.row(k - 1, rows)].astype(f32) * columns[:, at : at + 1]
            x[scene, k] = value.astype(bf16)
            put_row(stack, scene, k, value, False)

    total = jnp.sum(jnp.sum(mask_now, axis=1, keepdims=True), axis=0, keepdims=True)
    third = jnp.broadcast_to(total, (1, ch))
    finish_forward(stack, blocks, pre, near_out, sums, make_rows, columns, third)


def next_kernel(section, count, n, x_in, pre_in, near, far, *rest):
    pieces, rest = rest[:n], rest[n:]
    gbs, weights, x, pre, near_out, sums, stack, blocks = rest
    scenes, rows, cols, ch = pre.shape
    put_blocks(weights.at[section], blocks)
    scale, offset = stat_affine(pieces, count, gbs[section - 1])
    inside = Place().inside

    def make_rows(scene):
        here = slice(scene * cols, (scene + 1) * cols)
        for k in range(rows + 2):
            if k == 0:
                act = act_of(near[here, :].astype(f32), scale, offset, count)
            elif k == rows + 1:
                act = inside * act_of(far[here, :].astype(f32), scale, offset, count)
            else:
                act = act_of(pre_in[scene, k - 1], scale, offset, count)
            value = x_in[scene, k].astype(f32) + act
            x[scene, k] = value.astype(bf16)
            put_row(stack, scene, k, value, False)

    finish_forward(stack, blocks, pre, near_out, sums, make_rows, None, None)


def stat_affine(pieces, count, gb):
    mean, inv, _ = norm_stats(summed(pieces), count)
    return half_affine(mean, inv, gb)


def act_of(value, scale, offset, count):
    half = value * scale + offset
    act = half * jnp.tanh(half) + half
    return jnp.where(value > hole_edge, act, 0.0) if count is None else act


def slope_of(value, scale, offset, count):
    half = value * scale + offset
    out = twice_slope(half, jnp.tanh(half))
    return jnp.where(value > hole_edge, out, 0.0) if count is None else out


def at_scene(scene, cols):
    start = scene * cols
    return pl.ds(start if isinstance(scene, int) else pl.multiple_of(start, 16), cols)


def slope_kernel(section, count, n, pre, near, *rest):
    pieces, (gbs, slope) = rest[:n], rest[n:]
    scenes, padded, cols, ch = slope.shape
    scale, offset = stat_affine(pieces, count, gbs[section])

    @pl.loop(0, scenes)
    def _(scene):
        for k in range(padded):
            value = pre[scene, k - 1] if k else near[at_scene(scene, cols), :].astype(f32)
            slope[scene, k] = slope_of(value, scale, offset, count)


def turn_kernel(count, n, section, pre, cot, *rest):
    pieces, (gbs, grad_u, sums) = rest[:n], rest[n:]
    scenes, rows, cols, ch = grad_u.shape
    mean, inv, _ = norm_stats(summed(pieces), count)
    scale, offset = half_affine(mean, inv, gbs[section])
    place = Place()

    def one(scene, total):
        first, second = total
        for q in range(rows):
            value = pre[scene, q]
            grad = cot[0, scene, place.row(q, rows)].astype(f32) * slope_of(value, scale, offset, count)
            grad_u[scene, q] = grad
            first = first + fold(grad * value)
            second = second + fold(grad)
        return first, second

    zero = jnp.zeros((8, ch), f32)
    first, second = lax.fori_loop(0, scenes, one, (zero, zero))
    put_sums(sums, None, grad_sums(first, second, mean, inv))


def grad_sums(by_pre, plain, mean, inv):
    by_pre = 0.5 * jnp.sum(by_pre, axis=0, keepdims=True)
    plain = 0.5 * jnp.sum(plain, axis=0, keepdims=True)
    return jnp.concatenate(
        [inv * (by_pre - mean * plain), plain, jnp.zeros((6, plain.shape[1]), f32)], axis=0
    )


def neck_kernel(count, n, section, x, pre, *rest):
    pieces, (gbs, neck) = rest[:n], rest[n:]
    scenes, rows = neck.shape[1:3]
    scale, offset = stat_affine(pieces, count, gbs[section])
    place = Place()

    @pl.loop(0, scenes)
    def _(scene):
        for q in range(rows):
            act = act_of(pre[scene, q], scale, offset, count)
            neck[0, scene, place.row(q, rows)] = (x[scene, q + 1].astype(f32) + act).astype(bf16)


def back_terms(section, count, pieces, grads, gbs):
    mean, inv, cells = norm_stats(summed(pieces), count)
    total = summed(grads)
    lead = inv * gbs[section][0:1]
    by_pre = -lead * inv * total[0:1] / cells
    constant = -lead * total[1:2] / cells - by_pre * mean
    return (0.5 * lead, by_pre, constant), total


def grad_pre(terms, lifted, value, count):
    lead, by_pre, constant = terms
    out = lead * lifted + (by_pre * value + constant)
    return jnp.where(value > hole_edge, out, 0.0) if count is None else out


def back_rows(count, last, terms, stack, grad_u, g1, pre, p1, slope):
    scenes, rows, cols, ch = grad_u.shape
    base = scenes * cols if last else 0

    def make_rows(scene):
        at = scene * cols
        for k in range(rows + 1):
            if k:
                value = pre[scene, k - 1]
                lifted = grad_u[scene, k - 1]
            else:
                value = p1[at : at + cols, :].astype(f32)
                lifted = g1[base + at : base + at + cols, :].astype(f32) * slope[scene, 0]
            put_row(stack, scene, k, grad_pre(terms, lifted, value, count), True)

    return make_rows


def back_outer_row(section, count, last, terms, g2, p2, pieces, gbs, cols):
    base = p2.shape[0] if last else 0
    scale, offset = stat_affine(pieces, count, gbs[section])
    inside = Place().inside

    def outer_row(scene):
        at = at_scene(scene, cols)
        value = p2[at, :].astype(f32)
        lifted = g2[pl.ds(base + at.start, cols), :].astype(f32) * slope_of(value, scale, offset, count)
        return inside * grad_pre(terms, lifted, value, count)

    return outer_row


def grad_row(grad_in, last, scene, q, rows):
    return grad_in[0, scene, Place().row(q, rows)] if last else grad_in[scene, q]


def back_kernel(section, count, count_below, last, n, *rest):
    pieces, rest = rest[:n], rest[n:]
    grads, rest = rest[:n], rest[n:]
    pieces_below, rest = rest[:n], rest[n:]
    pre_below, slope_below, grad_u, grad_in, g1, g2, pre, p1, p2, slope, gbs, weights, *rest = rest
    stack, grad_out, grad_u_below, near, sums, total_out, blocks = rest
    scenes, rows, cols, ch = grad_u.shape
    put_blocks(weights.at[section], blocks)
    terms, total = back_terms(section, count, pieces, grads, gbs)
    total_out[...] = total
    mean_below, inv_below, _ = norm_stats(summed(pieces_below), count_below)
    make_rows = back_rows(count, last, terms, stack, grad_u, g1, pre, p1, slope)
    outer_row = back_outer_row(section, count, last, terms, g2, p2, pieces, gbs, cols)

    def make_all(scene):
        make_rows(scene)
        put_row(stack, scene, rows + 1, outer_row(scene), True)

    first = second = None
    make_all(0)
    for scene in range(scenes):
        if scene + 1 < scenes:
            make_all(scene + 1)
        for p in range(rows // 2):
            both = conv_back_pair(stack, None, blocks, scene, p)
            for m in range(2):
                r = 2 * p + m
                grad = grad_row(grad_in, last, scene, r, rows).astype(f32)
                grad = (grad + both[:, m * ch : (m + 1) * ch]).astype(bf16)
                grad_out[scene, r] = grad
                if r == 0:
                    near[scene * cols : (scene + 1) * cols, :] = grad
                lifted = grad.astype(f32) * slope_below[scene, r + 1]
                grad_u_below[scene, r] = lifted
                first = plus(first, fold(lifted * pre_below[scene, r]))
                second = plus(second, fold(lifted))
    put_sums(sums, near, grad_sums(first, second, mean_below, inv_below))


def final_weight_kernel(section, count, last, n, *rest):
    pieces, rest = rest[:n], rest[n:]
    grads, rest = rest[:n], rest[n:]
    grad_u, g1, pre, p1, slope, gbs, x, stack, mine, theirs, total_out, whole = rest
    terms, total = back_terms(section, count, pieces, grads, gbs)
    total_out[...] = total
    make_rows = back_rows(count, last, terms, stack, grad_u, g1, pre, p1, slope)
    weight_body(x, stack, mine, theirs, whole, make_rows)


def final_grad_kernel(section, count, last, n, *rest):
    pieces, rest = rest[:n], rest[n:]
    grads, rest = rest[:n], rest[n:]
    grad_in, g2, pre, p2, gbs, weights, stack, grad_out, outer, blocks = rest
    scenes, rows, cols, ch = grad_out.shape[1:]
    put_blocks(weights.at[section], blocks)
    terms, _ = back_terms(section, count, pieces, grads, gbs)
    outer_row = back_outer_row(section, count, last, terms, g2, p2, pieces, gbs, cols)
    place = Place()

    @pl.loop(0, scenes)
    def _(scene):
        put_outer(outer, scene, outer_row(scene), True)
        for p in range(rows // 2):
            both = conv_back_pair(stack, outer, blocks, scene, p)
            for m in range(2):
                r = 2 * p + m
                grad = grad_row(grad_in, last, scene, r, rows).astype(f32)
                grad = grad + both[:, m * ch : (m + 1) * ch]
                if count is None:
                    grad = jnp.where(pre[scene, r] > hole_edge, grad, 0.0)
                grad_out[0, scene, place.row(r, rows)] = grad.astype(bf16)


def weight_kernel(x, stack, mine, theirs, whole):
    weight_body(x, stack, mine, theirs, whole, None)


def weight_body(x, stack, mine, theirs, whole, make_rows):
    scenes, padded, cols, ch = x.shape
    rows = padded - 2
    place = Place()
    total = None
    if make_rows:
        make_rows(0)
    for scene in range(scenes):
        if make_rows and scene + 1 < scenes:
            make_rows(scene + 1)
        lines = [x[scene, k] for k in range(rows + 2)]
        lhs = jnp.concatenate(
            [jnp.concatenate(lines[i : i + rows], axis=0) for i in range(3)], axis=1
        )
        rhs = jnp.concatenate(
            [
                jnp.concatenate(
                    [
                        stack[j, k // 2, scene, :, (k % 2) * ch : (k % 2 + 1) * ch]
                        for j in range(3)
                    ],
                    axis=1,
                )
                for k in range(1, rows + 1)
            ],
            axis=0,
        )
        term = lax.dot_general(lhs, rhs, (((0,), (0,)), ((), ())), preferred_element_type=f32)
        total = plus(total, term)
    for i in range(3):
        for j in range(3):
            at = pl.multiple_of((3 * place.tap(i) + j) * ch, 8)
            whole[pl.ds(at, ch), :] = total[i * ch : (i + 1) * ch, j * ch : (j + 1) * ch]
    chips, chunk = mine.shape[:2]
    for z in range(chips):
        at = pl.multiple_of((2 * z + place.core) * chunk, 8)
        mine[z] = whole[pl.ds(at, chunk), :]
        at = pl.multiple_of((2 * z + 1 - place.core) * chunk, 8)
        theirs[z] = whole[pl.ds(at, chunk), :].astype(bf16)


def chip_kernel(n, *refs):
    mine, refs = refs[:n], refs[n:]
    theirs, refs = refs[:n], refs[n:]
    totals, refs = refs[:n], refs[n:]
    outs, held, sums = refs[:4], refs[4], refs[5]
    here = Place().section
    chips, chunk, ch = mine[0].shape
    for s in range(n):
        for z in range(chips):
            held[s, z * chunk : (z + 1) * chunk] = mine[s][z] + theirs[s][z].astype(f32)
        sums[s] = totals[s][...]
    size = chips * chunk
    for d in range(4):
        if d:
            outs[d][:size] = held[here ^ d].astype(bf16)
            put_parts(outs[d], size, sums[here ^ d])
        else:
            outs[0][:size] = held[here]
            outs[0][size:] = sums[here]


def section_kernel(own, a, b, c, mine, one, two, three, sums, held):
    chips, chunk = held.shape[:2]
    size = chips * chunk
    for z in range(chips):
        at = slice(z * chunk, (z + 1) * chunk)
        held[z] = own[at] + a[at].astype(f32) + b[at].astype(f32) + c[at].astype(f32)
    total = own[size:]
    for got in (a, b, c):
        parts = got[size:].astype(f32)
        total = total + (parts[0:8] + parts[8:16] + parts[16:24])
    sums[...] = total
    chip = Place().chip
    mine[...] = held[chip]
    for k, out in ((1, one), (2, two), (3, three)):
        out[...] = held[chip ^ k].astype(bf16)


def last_kernel(mine, a, b, c, sums, weight, gain, bias):
    gain[...] = sums[0:1]
    bias[...] = sums[1:2]
    weight[0] = mine[...] + a[...].astype(f32) + b[...].astype(f32) + c[...].astype(f32)


def call(body, outs, ins, scratch=(), flops=0, name=None, hbm=()):
    specs = [VMEM_SPEC] * len(ins)
    for n in hbm:
        specs[n] = pl.BlockSpec(memory_space=pltpu.HBM)
    return pl.pallas_call(
        body,
        out_shape=[jax.ShapeDtypeStruct(s, d) for s, d in outs],
        in_specs=specs,
        out_specs=[VMEM_SPEC] * len(outs),
        scratch_shapes=list(scratch),
        compiler_params=pltpu.CompilerParams(vmem_limit_bytes=12 * 2**20),
        cost_estimate=pl.CostEstimate(flops=flops, bytes_accessed=0, transcendentals=0),
        name=name,
    )(*ins)


def swap(value, axis, step):
    count = lax.axis_size(axis)
    return lax.ppermute(value, axis, [(i, i ^ step) for i in range(count)])


def swap_next(value):
    pairs = []
    for i in range(1, lax.axis_size("row") - 1, 2):
        pairs += [(i, i + 1), (i + 1, i)]
    return lax.ppermute(value, "row", pairs)


def row_pieces(total):
    count = lax.axis_size("row")
    stride = 2
    while True:
        group = min(4, count // stride)
        pieces = [total] + [swap(total, "row", k * stride) for k in range(1, group)]
        stride *= group
        if stride >= count:
            return pieces
        total = sum(pieces[1:], pieces[0])


def after(value, signal):
    return lax.optimization_barrier((value, signal))[0]


def far_rows(rows_ref):
    scenes, _, cols, ch = rows_ref.shape
    (far,) = call(far_kernel, [((scenes * cols, ch), bf16)], (rows_ref,), name="far")
    return far


def exchange(sums, near, rows_ref):
    got = swap(near, "row", 1)
    far = swap_next(far_rows(rows_ref))
    parts = got[got.shape[0] - 32 :].astype(f32)
    total = sums + (parts[0:8] + parts[8:16] + parts[16:24])
    return got, far, row_pieces(total), total


def per_device(features, conv_weight, norm_gain, norm_bias, valid_mask, out_cotangent):
    sections = lax.axis_size("section")
    tiles = lax.axis_size("row")
    scenes, rows, cols, ch = features.shape[1:]
    taps = conv_weight.shape[1]
    cells = float(scenes * rows * cols * tiles)
    tile_shape = (scenes, rows, cols, ch)
    pad_shape = (scenes, rows + 2, cols, ch)
    slope_shape = (scenes, rows + 1, cols, ch)
    edge = scenes * cols
    near_shape = (edge + 32, ch)
    sum_shape = (8, ch)
    stack_shape = (3, rows // 2 + 1, scenes, cols, 2 * ch)
    blocks = pltpu.VMEM((6, 2 * ch, 2 * ch), bf16)
    outer = pltpu.VMEM((3, scenes, cols, ch), bf16)
    flops = 2 * scenes * rows * cols * taps * ch
    half = taps // 2
    chunk = taps // tiles
    direct = tiles == 8 and chunk % 16 == 0

    def in_hbm(*values):
        return [pltpu.with_memory_space_constraint(v, pltpu.HBM) for v in values]

    e1, e2, wsend = call(
        prep_kernel,
        [((2 * edge, ch), bf16), ((2 * edge, ch), bf16), ((half + 32, ch), bf16)],
        in_hbm(valid_mask, features, out_cotangent, conv_weight, norm_gain, norm_bias),
        [
            pltpu.VMEM((4, scenes, cols, ch), bf16),
            pltpu.VMEM((1, scenes, rows, cols), jnp.int32),
            pltpu.VMEM((8, ch), f32),
            pltpu.SemaphoreType.DMA((8,)),
        ],
        hbm=range(6),
        name="prep",
    )
    got = [swap(wsend, "section", d) for d in (1, 2, 3)]
    e1 = swap(e1, "row", 1)
    e2 = swap_next(e2)
    got[1] = after(got[1], e1)
    other = swap(jnp.stack(got), "row", 1)
    weights, gbs = call(
        gather_kernel,
        [((sections, taps, ch), bf16), ((sections, 8, ch), f32)],
        (conv_weight, norm_gain, norm_bias, *got, other),
        name="gather",
    )

    forward_outs = [(pad_shape, bf16), (tile_shape, f32), (near_shape, bf16), (sum_shape, f32)]
    scratch = [pltpu.VMEM(stack_shape, bf16), blocks]
    kept = []
    slopes = []
    x, pre, near, sums = call(
        first_kernel,
        forward_outs,
        (valid_mask, features, e1, e2, weights),
        scratch,
        flops=flops,
        name="forward",
    )
    for section in range(sections):
        count = None if section == 0 else cells
        near, far, pieces, total = exchange(sums, near, pre)
        if section > 0:
            _, below, below_near, _, below_pieces, below_count = kept[-1]
            slopes += call(
                functools.partial(slope_kernel, section - 1, below_count, len(pieces)),
                [(slope_shape, f32)],
                (after(below, total), below_near, *below_pieces, gbs),
                name="slope",
            )
            pieces[0] = after(pieces[0], slopes[-1])
        kept.append((x, pre, near, far, pieces, count))
        if section == sections - 1:
            break
        x, pre, near, sums = call(
            functools.partial(next_kernel, section + 1, count, len(pieces)),
            forward_outs,
            (x, pre, near, far, *pieces, gbs, weights),
            scratch,
            flops=flops,
            name="forward",
        )
    n = len(pieces)
    grad_u, sums = call(
        functools.partial(turn_kernel, count, n, sections - 1),
        [(tile_shape, f32), (sum_shape, f32)],
        (pre, out_cotangent, *pieces, gbs),
        name="turn",
    )
    total = sums + swap(sums, "row", 1)
    grads = row_pieces(total)
    slopes += call(
        functools.partial(slope_kernel, sections - 1, count, n),
        [(slope_shape, f32)],
        (after(pre, total), near, *pieces, gbs),
        name="slope",
    )
    grad, g1, g2 = out_cotangent, e1, e2
    parts = [None] * sections
    totals = [None] * sections
    part_shapes = [((tiles // 2, chunk, ch), f32), ((tiles // 2, chunk, ch), bf16)]
    whole = pltpu.VMEM((taps, ch), f32)
    for section in range(sections - 1, 0, -1):
        x, pre, p1, p2, pieces, count = kept[section]
        _, below, _, _, below_pieces, below_count = kept[section - 1]
        last = section == sections - 1
        stack, grad, grad_u, near, sums, totals[section] = call(
            functools.partial(back_kernel, section, count, below_count, last, n),
            [
                (stack_shape, bf16),
                (tile_shape, bf16),
                (tile_shape, f32),
                (near_shape, bf16),
                (sum_shape, f32),
                (sum_shape, f32),
            ],
            (
                *pieces,
                *grads,
                *below_pieces,
                below,
                slopes[section - 1],
                grad_u,
                grad,
                g1,
                g2,
                pre,
                p1,
                p2,
                slopes[section],
                gbs,
                weights,
            ),
            [blocks],
            flops=flops,
            name="backward",
        )
        g1, g2, grads, total = exchange(sums, near, grad)
        parts[section] = call(
            weight_kernel,
            part_shapes,
            (x, after(stack, total)),
            [whole],
            flops=flops,
            name="weight",
        )
        grads[0] = after(grads[0], parts[section][1])
    x, pre, p1, p2, pieces, count = kept[0]
    last = sections == 1
    stack, *parts[0], totals[0] = call(
        functools.partial(final_weight_kernel, 0, count, last, n),
        [(stack_shape, bf16), *part_shapes, (sum_shape, f32)],
        (*pieces, *grads, grad_u, g1, pre, p1, slopes[0], gbs, x),
        [whole],
        flops=flops,
        name="weight",
    )

    def finish(signal):
        (feature_grad,) = call(
            functools.partial(final_grad_kernel, 0, count, last, n),
            [((1,) + tile_shape, bf16)],
            (*pieces, *grads, grad, g2, pre, p2, gbs, weights, after(stack, signal)),
            [outer, blocks],
            flops=flops,
            name="final_grad",
        )
        last_x, last_pre, _, _, last_pieces, last_count = kept[-1]
        (neck,) = call(
            functools.partial(neck_kernel, last_count, n, sections - 1),
            [((1,) + tile_shape, bf16)],
            (last_x, after(last_pre, signal), *last_pieces, gbs),
            flops=flops,
            name="neck",
        )
        return neck, feature_grad

    m = sections
    if direct:
        size = taps // 2
        theirs = [swap(p[1], "row", 1) for p in parts]
        own, *sending = call(
            functools.partial(chip_kernel, m),
            [((size + 8, ch), f32)] + [((size + 32, ch), bf16)] * 3,
            (*[p[0] for p in parts], *theirs, *totals),
            [pltpu.VMEM((m, size, ch), f32), pltpu.VMEM((m, 8, ch), f32)],
            name="chips",
        )
        received = [swap(v, "section", d + 1) for d, v in enumerate(sending)]
        neck, feature_grad = finish(own)
        received[0] = after(received[0], (neck, feature_grad))
        mine, one, two, three, total = call(
            section_kernel,
            [((chunk, ch), f32)] + [((chunk, ch), bf16)] * 3 + [(sum_shape, f32)],
            (own, *received),
            [pltpu.VMEM((tiles // 2, chunk, ch), f32)],
            name="sections",
        )
        chunks = [swap(v, "row", 2 * (k + 1)) for k, v in enumerate((one, two, three))]
        weight_grad, gain_grad, bias_grad = call(
            last_kernel,
            [((1, chunk, ch), f32), ((1, ch), f32), ((1, ch), f32)],
            (mine, *chunks, total),
            name="last",
        )
    else:
        lanes = [list(range(c, tiles, 2)) for c in range(2)]
        here = lax.axis_index("section")
        chip_sums = jnp.stack([p[0] + swap(p[1], "row", 1).astype(f32) for p in parts])
        sums = jnp.stack(totals)

        def over_sections(stacked):
            total, *others = [
                lax.dynamic_index_in_dim(stacked, here ^ d, 0, keepdims=False) for d in range(4)
            ]
            for d, other in enumerate(others):
                total = total + swap(other, "section", d + 1)
            return total

        chip_sum, total = over_sections(chip_sums), over_sections(sums)
        weight_grad = lax.psum_scatter(
            chip_sum, "row", scatter_dimension=0, tiled=True, axis_index_groups=lanes
        )
        gain_grad, bias_grad = total[0:1], total[1:2]
        neck, feature_grad = finish(total)
    return neck, feature_grad, weight_grad, gain_grad, bias_grad


def solution(mesh):
    return jax.shard_map(
        per_device,
        mesh=mesh,
        in_specs=(
            P("section", None, "row", None, None),
            P("section", None, None),
            P("section", None),
            P("section", None),
            P(None, None, "row", None),
            P("section", None, "row", None, None),
        ),
        out_specs=(
            P("section", None, "row", None, None),
            P("section", None, "row", None, None),
            P("section", "row", None),
            P("section", None),
            P("section", None),
        ),
        check_vma=False,
    )
```

profile of v0, /device:TPU:0, one launch (start us, length us, event | category | flops | bytes accessed | tf_op | source)
XLA Modules:
  0.0 143.8 jit_solution(13952045866465476959)
XLA Ops:
  0.7 2.1 %prep.1 = (bf16[2048,128]{1,0:T(8,128)(2,1)S(1)}, bf16[2048,128]{1,0:T(8,128)(2,1)S(1)}, bf16[608,128]{1,0:T(8,128)(2,1)S(1)}) custom-call(s32[4,4,4,256]{3,2,1,0:T(4,128)} %mask.3, bf16[1,4,4,256,128]{4,3,2,1,0:T(8,128)(2,1)} %features.3, bf16[1,4,4,256,128]{4,3,2,1,0:T(8,128)(2,1)} %rest_15_.1, bf16[1,1152,128]{2,1,0:T(8,128)(2,1)} %own.1, f32[1,128]{1,0:T(1,128)} %gain.3, ...), custom_call_target="tpu_custom_call" | custom-call | tf_op jit(solution)/shard_map/prep/pallas_call | solution.py:602
  3.3 2.6 %collective-permute-start.3 = (bf16[608,128]{1,0:T(8,128)(2,1)S(1)}, bf16[608,128]{1,0:T(8,128)(2,1)S(1)}, u32[]{:S(2)}, u32[]{:S(2)}) collective-permute-start(bf16[608,128]{1,0:T(8,128)(2,1)S(1)} %get-tuple-element.87), channel_id=1, source_target_pairs={{0,16},{8,24},{16,0},{24,8},{1,17},{9,25},{17,1},{25,9},{2,18},{10... | collective-permute-start | bytes 466952 | tf_op jit(solution)/shard_map/ppermute | solution.py:616
  5.9 1.4 collective-permute-start.4
  7.4 0.7 collective-permute-start.1
  8.1 5.7 %collective-permute-done.3.r2 = bf16[608,128]{1,0:T(8,128)(2,1)S(1)} collective-permute-done((bf16[608,128]{1,0:T(8,128)(2,1)S(1)}, bf16[608,128]{1,0:T(8,128)(2,1)S(1)}, u32[]{:S(2)}, u32[]{:S(2)}) %collective-permute-start.3) | collective-permute-done | bytes 155680 | tf_op jit(solution)/shard_map/ppermute | solution.py:616
  13.8 1.3 collective-permute-done.2.r1
  15.2 1.8 %collective-permute-done.5.other = bf16[3,608,128]{2,1,0:T(8,128)(2,1)S(1)} collective-permute-done((bf16[3,608,128]{2,1,0:T(8,128)(2,1)S(1)}, bf16[3,608,128]{2,1,0:T(8,128)(2,1)S(1)}, u32[]{:S(2)}, u32[]{:S(2)}) %collective-permute-start.5) | collective-permute-done | bytes 466976 | tf_op jit(solution)/shard_map/ppermute | solution.py:616
  17.2 2.7 %forward.4 = (bf16[4,6,256,128]{3,2,1,0:T(8,128)(2,1)S(1)}, f32[4,4,256,128]{3,2,1,0:T(8,128)S(1)}, bf16[1056,128]{1,0:T(8,128)(2,1)S(1)}, f32[8,128]{1,0:T(8,128)S(1)}) custom-call(s32[4,4,4,256]{3,2,1,0:T(4,128)S(1)} %copy-done.3, bf16[1,4,4,256,128]{4,3,2,1,0:T(8,128)(2,1)S(1)} %copy-done.2, bf16[2048,128]{1,0:T(8,128)(2,1)S(1)} %collective-permute-done.near.rest_16_, ...), custom_call_target="tpu_custom_call" | custom-call | flops 1207959552 | tf_op jit(solution)/shard_map/forward/pallas_call | solution.py:602
  19.9 1.1 collective-permute-start.6
  21.0 0.7 collective-permute-start.7
  22.2 5.1 %collective-permute-start.10 = (f32[8,128]{1,0:T(8,128)S(1)}, f32[8,128]{1,0:T(8,128)S(1)}, u32[]{:S(2)}, u32[]{:S(2)}) collective-permute-start(f32[8,128]{1,0:T(8,128)S(1)} %fusion.6.rest_0_.rest_8_), channel_id=1, source_target_pairs={{0,6},{1,7},{2,4},{3,5},{4,2},{5,3},{6,0},{7,1},{8,14},{9,15},{10,... | collective-permute-start | bytes 12296 | tf_op jit(solution)/shard_map/ppermute | solution.py:616
  27.9 3.8 %collective-permute-done.10.rest_3_.rest_11_ = f32[8,128]{1,0:T(8,128)S(1)} collective-permute-done((f32[8,128]{1,0:T(8,128)S(1)}, f32[8,128]{1,0:T(8,128)S(1)}, u32[]{:S(2)}, u32[]{:S(2)}) %collective-permute-start.10) | collective-permute-done | bytes 4128 | tf_op jit(solution)/shard_map/ppermute | solution.py:616
  31.8 3.1 %forward.5 = (bf16[4,6,256,128]{3,2,1,0:T(8,128)(2,1)S(1)}, f32[4,4,256,128]{3,2,1,0:T(8,128)S(1)}, bf16[1056,128]{1,0:T(8,128)(2,1)S(1)}, f32[8,128]{1,0:T(8,128)S(1)}) custom-call(bf16[4,6,256,128]{3,2,1,0:T(8,128)(2,1)S(1)} %get-tuple-element.90.x_in.rest_14_, f32[4,4,256,128]{3,2,1,0:T(8,128)S(1)} %get-tuple-element.99.rows_ref.pre_in.pre.rest_12_.rest_10_, ...), custom_call_target="tpu_custom_call" | custom-call | flops 1207959552 | tf_op jit(solution)/shard_map/forward/pallas_call | solution.py:602
  35.0 0.7 collective-permute-start.12
  35.7 0.8 collective-permute-done.11.near.rest_19_
  36.5 4.1 %collective-permute-start.15 = (f32[8,128]{1,0:T(8,128)S(1)}, f32[8,128]{1,0:T(8,128)S(1)}, u32[]{:S(2)}, u32[]{:S(2)}) collective-permute-start(f32[8,128]{1,0:T(8,128)S(1)} %fusion.5.rest_0_.rest_8_), channel_id=1, source_target_pairs={{0,6},{1,7},{2,4},{3,5},{4,2},{5,3},{6,0},{7,1},{8,14},{9,15},{10,... | collective-permute-start | bytes 12296 | tf_op jit(solution)/shard_map/ppermute | solution.py:616
  41.3 0.9 slope.4.rest_13_.rest_12_
  42.2 2.8 %collective-permute-done.15.rest_3_.rest_11_ = f32[8,128]{1,0:T(8,128)S(1)} collective-permute-done((f32[8,128]{1,0:T(8,128)S(1)}, f32[8,128]{1,0:T(8,128)S(1)}, u32[]{:S(2)}, u32[]{:S(2)}) %collective-permute-start.15) | collective-permute-done | bytes 4128 | tf_op jit(solution)/shard_map/ppermute | solution.py:616
  45.1 2.9 %forward.6 = (bf16[4,6,256,128]{3,2,1,0:T(8,128)(2,1)S(1)}, f32[4,4,256,128]{3,2,1,0:T(8,128)S(1)}, bf16[1056,128]{1,0:T(8,128)(2,1)S(1)}, f32[8,128]{1,0:T(8,128)S(1)}) custom-call(bf16[4,6,256,128]{3,2,1,0:T(8,128)(2,1)S(1)} %get-tuple-element.95.x_in.x, f32[4,4,256,128]{3,2,1,0:T(8,128)S(1)} %get-tuple-element.105.rows_ref.pre_in.pre.rest_12_.rest_18_, ...), custom_call_target="tpu_custom_call" | custom-call | flops 1207959552 | tf_op jit(solution)/shard_map/forward/pallas_call | solution.py:602
  48.2 0.9 collective-permute-start.17
  49.7 4.3 %collective-permute-start.20 = (f32[8,128]{1,0:T(8,128)S(1)}, f32[8,128]{1,0:T(8,128)S(1)}, u32[]{:S(2)}, u32[]{:S(2)}) collective-permute-start(f32[8,128]{1,0:T(8,128)S(1)} %fusion.4.rest_0_.rest_8_), channel_id=1, source_target_pairs={{0,6},{1,7},{2,4},{3,5},{4,2},{5,3},{6,0},{7,1},{8,14},{9,15},{10,... | collective-permute-start | bytes 12296 | tf_op jit(solution)/shard_map/ppermute | solution.py:616
  54.6 0.7 slope.5.rest_13_.rest_21_
  55.4 2.8 %collective-permute-done.20.rest_3_.rest_11_ = f32[8,128]{1,0:T(8,128)S(1)} collective-permute-done((f32[8,128]{1,0:T(8,128)S(1)}, f32[8,128]{1,0:T(8,128)S(1)}, u32[]{:S(2)}, u32[]{:S(2)}) %collective-permute-start.20) | collective-permute-done | bytes 4128 | tf_op jit(solution)/shard_map/ppermute | solution.py:616
  58.5 2.9 %forward.7 = (bf16[4,6,256,128]{3,2,1,0:T(8,128)(2,1)S(1)}, f32[4,4,256,128]{3,2,1,0:T(8,128)S(1)}, bf16[1056,128]{1,0:T(8,128)(2,1)S(1)}, f32[8,128]{1,0:T(8,128)S(1)}) custom-call(bf16[4,6,256,128]{3,2,1,0:T(8,128)(2,1)S(1)} %get-tuple-element.101.x_in.x, f32[4,4,256,128]{3,2,1,0:T(8,128)S(1)} %get-tuple-element.111.rows_ref.pre_in.pre.rest_12_.rest_18_, ...), custom_call_target="tpu_custom_call" | custom-call | flops 1207959552 | tf_op jit(solution)/shard_map/forward/pallas_call | solution.py:602
  61.5 0.7 collective-permute-start.29
  62.2 0.8 collective-permute-done.21.near.rest_19_
  63.0 4.1 %collective-permute-start.24 = (f32[8,128]{1,0:T(8,128)S(1)}, f32[8,128]{1,0:T(8,128)S(1)}, u32[]{:S(2)}, u32[]{:S(2)}) collective-permute-start(f32[8,128]{1,0:T(8,128)S(1)} %fusion.3.rest_0_), channel_id=1, source_target_pairs={{0,6},{1,7},{2,4},{3,5},{4,2},{5,3},{6,0},{7,1},{8,14},{9,15},{10,... | collective-permute-start | bytes 12296 | tf_op jit(solution)/shard_map/ppermute | solution.py:616
  67.8 0.7 slope.6.rest_13_.rest_21_
  68.5 2.9 %collective-permute-done.24.rest_3_ = f32[8,128]{1,0:T(8,128)S(1)} collective-permute-done((f32[8,128]{1,0:T(8,128)S(1)}, f32[8,128]{1,0:T(8,128)S(1)}, u32[]{:S(2)}, u32[]{:S(2)}) %collective-permute-start.24) | collective-permute-done | bytes 4128 | tf_op jit(solution)/shard_map/ppermute | solution.py:616
  71.6 1.0 turn.1
  72.7 1.2 collective-permute-done.25
  73.9 1.5 %collective-permute-start.28 = (f32[8,128]{1,0:T(8,128)S(1)}, f32[8,128]{1,0:T(8,128)S(1)}, u32[]{:S(2)}, u32[]{:S(2)}) collective-permute-start(f32[8,128]{1,0:T(8,128)S(1)} %add.78.rest_4_), channel_id=1, source_target_pairs={{0,6},{1,7},{2,4},{3,5},{4,2},{5,3},{6,0},{7,1},{8,14},{9,15},{10,... | collective-permute-start | bytes 12296 | tf_op jit(solution)/shard_map/ppermute | solution.py:616
  75.9 2.4 %collective-permute-start.26 = (f32[8,128]{1,0:T(8,128)S(1)}, f32[8,128]{1,0:T(8,128)S(1)}, u32[]{:S(2)}, u32[]{:S(2)}) collective-permute-start(f32[8,128]{1,0:T(8,128)S(1)} %add.78.rest_4_), channel_id=1, source_target_pairs={{0,2},{1,3},{2,0},{3,1},{4,6},{5,7},{6,4},{7,5},{8,10},{9,11},{10,... | collective-permute-start | bytes 12296 | tf_op jit(solution)/shard_map/ppermute | solution.py:616
  78.2 0.7 slope.7.rest_21_
  79.9 3.1 %backward.3 = (bf16[3,3,4,256,256]{4,3,2,1,0:T(8,128)(2,1)S(1)}, bf16[4,4,256,128]{3,2,1,0:T(8,128)(2,1)S(1)}, f32[4,4,256,128]{3,2,1,0:T(8,128)S(1)}, bf16[1056...) custom-call(f32[8,128]{1,0:T(8,128)S(1)} %fusion.3.rest_0_, ...), custom_call_target="tpu_custom_call" | custom-call | flops 1207959552 | tf_op jit(solution)/shard_map/backward/pallas_call | solution.py:602
  83.1 0.7 collective-permute-start.34
  83.8 0.8 collective-permute-done.30.rest_16_
  84.6 4.0 %collective-permute-start.33 = (f32[8,128]{1,0:T(8,128)S(1)}, f32[8,128]{1,0:T(8,128)S(1)}, u32[]{:S(2)}, u32[]{:S(2)}) collective-permute-start(f32[8,128]{1,0:T(8,128)S(1)} %fusion.2.rest_4_), channel_id=1, source_target_pairs={{0,6},{1,7},{2,4},{3,5},{4,2},{5,3},{6,0},{7,1},{8,14},{9,15},{10,... | collective-permute-start | bytes 12296 | tf_op jit(solution)/shard_map/ppermute | solution.py:616
  89.3 1.9 %weight.6 = (f32[4,144,128]{2,1,0:T(8,128)S(1)}, bf16[4,144,128]{2,1,0:T(8,128)(2,1)S(1)}) custom-call(bf16[4,6,256,128]{3,2,1,0:T(8,128)(2,1)S(1)} %get-tuple-element.107.x, bf16[3,3,4,256,256]{4,3,2,1,0:T(8,128)(2,1)S(1)} %get-tuple-element.119.stack), custom_call_target="tpu_custom_call" | custom-call | flops 1207959552 | tf_op jit(solution)/shard_map/weight/pallas_call | solution.py:602
  91.2 1.9 %collective-permute-done.33.rest_7_ = f32[8,128]{1,0:T(8,128)S(1)} collective-permute-done((f32[8,128]{1,0:T(8,128)S(1)}, f32[8,128]{1,0:T(8,128)S(1)}, u32[]{:S(2)}, u32[]{:S(2)}) %collective-permute-start.33) | collective-permute-done | bytes 4128 | tf_op jit(solution)/shard_map/ppermute | solution.py:616
  93.2 3.0 %backward.4 = (bf16[3,3,4,256,256]{4,3,2,1,0:T(8,128)(2,1)S(1)}, bf16[4,4,256,128]{3,2,1,0:T(8,128)(2,1)S(1)}, f32[4,4,256,128]{3,2,1,0:T(8,128)S(1)}, bf16[1056...) custom-call(f32[8,128]{1,0:T(8,128)S(1)} %fusion.4.rest_0_.rest_8_, ...), custom_call_target="tpu_custom_call" | custom-call | flops 1207959552 | tf_op jit(solution)/shard_map/backward/pallas_call | solution.py:602
  96.3 0.9 collective-permute-start.39
  97.8 4.3 %collective-permute-start.38 = (f32[8,128]{1,0:T(8,128)S(1)}, f32[8,128]{1,0:T(8,128)S(1)}, u32[]{:S(2)}, u32[]{:S(2)}) collective-permute-start(f32[8,128]{1,0:T(8,128)S(1)} %fusion.1.rest_4_), channel_id=1, source_target_pairs={{0,6},{1,7},{2,4},{3,5},{4,2},{5,3},{6,0},{7,1},{8,14},{9,15},{10,... | collective-permute-start | bytes 12296 | tf_op jit(solution)/shard_map/ppermute | solution.py:616
  102.7 1.9 %weight.7 = (f32[4,144,128]{2,1,0:T(8,128)S(1)}, bf16[4,144,128]{2,1,0:T(8,128)(2,1)S(1)}) custom-call(bf16[4,6,256,128]{3,2,1,0:T(8,128)(2,1)S(1)} %get-tuple-element.101.x_in.x, bf16[3,3,4,256,256]{4,3,2,1,0:T(8,128)(2,1)S(1)} %get-tuple-element.127.stack), custom_call_target="tpu_custom_call" | custom-call | flops 1207959552 | tf_op jit(solution)/shard_map/weight/pallas_call | solution.py:602
  104.6 1.6 %collective-permute-done.38.rest_7_ = f32[8,128]{1,0:T(8,128)S(1)} collective-permute-done((f32[8,128]{1,0:T(8,128)S(1)}, f32[8,128]{1,0:T(8,128)S(1)}, u32[]{:S(2)}, u32[]{:S(2)}) %collective-permute-start.38) | collective-permute-done | bytes 4128 | tf_op jit(solution)/shard_map/ppermute | solution.py:616
  106.6 3.0 %backward.5 = (bf16[3,3,4,256,256]{4,3,2,1,0:T(8,128)(2,1)S(1)}, bf16[4,4,256,128]{3,2,1,0:T(8,128)(2,1)S(1)}, f32[4,4,256,128]{3,2,1,0:T(8,128)S(1)}, bf16[1056...) custom-call(f32[8,128]{1,0:T(8,128)S(1)} %fusion.5.rest_0_.rest_8_, ...), custom_call_target="tpu_custom_call" | custom-call | flops 1207959552 | tf_op jit(solution)/shard_map/backward/pallas_call | solution.py:602
  110.3 0.9 collective-permute-done.40.rest_9_
  111.2 1.8 %collective-permute-start.43 = (f32[8,128]{1,0:T(8,128)S(1)}, f32[8,128]{1,0:T(8,128)S(1)}, u32[]{:S(2)}, u32[]{:S(2)}) collective-permute-start(f32[8,128]{1,0:T(8,128)S(1)} %fusion.rest_4_), channel_id=1, source_target_pairs={{0,6},{1,7},{2,4},{3,5},{4,2},{5,3},{6,0},{7,1},{8,14},{9,15},{10,... | collective-permute-start | bytes 12296 | tf_op jit(solution)/shard_map/ppermute | solution.py:616
  113.3 2.3 %collective-permute-start.41 = (f32[8,128]{1,0:T(8,128)S(1)}, f32[8,128]{1,0:T(8,128)S(1)}, u32[]{:S(2)}, u32[]{:S(2)}) collective-permute-start(f32[8,128]{1,0:T(8,128)S(1)} %fusion.rest_4_), channel_id=1, source_target_pairs={{0,2},{1,3},{2,0},{3,1},{4,6},{5,7},{6,4},{7,5},{8,10},{9,11},{10,... | collective-permute-start | bytes 12296 | tf_op jit(solution)/shard_map/ppermute | solution.py:616
  115.6 1.9 %weight.8 = (f32[4,144,128]{2,1,0:T(8,128)S(1)}, bf16[4,144,128]{2,1,0:T(8,128)(2,1)S(1)}) custom-call(bf16[4,6,256,128]{3,2,1,0:T(8,128)(2,1)S(1)} %get-tuple-element.95.x_in.x, bf16[3,3,4,256,256]{4,3,2,1,0:T(8,128)(2,1)S(1)} %get-tuple-element.135.stack), custom_call_target="tpu_custom_call" | custom-call | flops 1207959552 | tf_op jit(solution)/shard_map/weight/pallas_call | solution.py:602
  117.5 0.7 collective-permute-start.48
  118.2 1.4 collective-permute-start.45
  119.6 2.6 %weight.9 = (bf16[3,3,4,256,256]{4,3,2,1,0:T(8,128)(2,1)S(1)}, f32[4,144,128]{2,1,0:T(8,128)S(1)}, bf16[4,144,128]{2,1,0:T(8,128)(2,1)S(1)}, f32[8,128]{1,0:T(8,128)S(1)}) custom-call(f32[8,128]{1,0:T(8,128)S(1)} %fusion.6.rest_0_.rest_8_, f32[8,128]{1,0:T(8,128)S(1)} %collective-permute-done.8.rest_1_.rest_9_, ...), custom_call_target="tpu_custom_call" | custom-call | flops 1207959552 | tf_op jit(solution)/shard_map/weight/pallas_call | solution.py:602
  122.4 1.3 collective-permute-done.44.refs_4_
  123.9 1.6 %collective-permute-start.49 = (bf16[608,128]{1,0:T(8,128)(2,1)S(1)}, bf16[608,128]{1,0:T(8,128)(2,1)S(1)}, u32[]{:S(2)}, u32[]{:S(2)}) collective-permute-start(bf16[608,128]{1,0:T(8,128)(2,1)S(1)} %get-tuple-element.153), channel_id=1, source_target_pairs={{0,8},{8,0},{16,24},{24,16},{1,9},{9,1},{17,25},{25,17},{2,10},{10... | collective-permute-start | bytes 466952 | tf_op jit(solution)/shard_map/ppermute | solution.py:616
  125.4 1.5 %collective-permute-start.50 = (bf16[608,128]{1,0:T(8,128)(2,1)S(1)}, bf16[608,128]{1,0:T(8,128)(2,1)S(1)}, u32[]{:S(2)}, u32[]{:S(2)}) collective-permute-start(bf16[608,128]{1,0:T(8,128)(2,1)S(1)} %get-tuple-element.155), channel_id=1, source_target_pairs={{0,16},{8,24},{16,0},{24,8},{1,17},{9,25},{17,1},{25,9},{2,18},{10... | collective-permute-start | bytes 466952 | tf_op jit(solution)/shard_map/ppermute | solution.py:616
  127.4 1.5 %neck.1 = bf16[1,4,4,256,128]{4,3,2,1,0:T(8,128)(2,1)} custom-call(bf16[4,6,256,128]{3,2,1,0:T(8,128)(2,1)S(1)} %get-tuple-element.107.x, f32[4,4,256,128]{3,2,1,0:T(8,128)S(1)} %get-tuple-element.149.pre.rows_ref.rest_18_, f32[8,128]{1,0:T(8,128)S(1)} %fusion.3.rest_0_, f32[8,128]{1,0:T(8,128)S(1)} %collective-permute-done.22.rest_1_, ...), custom_call_target="tpu_custom_call" | custom-call | flops 1207959552 | tf_op jit(solution)/shard_map/neck/pallas_call | solution.py:602
  129.0 3.6 %final_grad.1 = bf16[1,4,4,256,128]{4,3,2,1,0:T(8,128)(2,1)} custom-call(f32[8,128]{1,0:T(8,128)S(1)} %fusion.6.rest_0_.rest_8_, f32[8,128]{1,0:T(8,128)S(1)} %collective-permute-done.8.rest_1_.rest_9_, f32[8,128]{1,0:T(8,128)S(1)} %collective-permute-done.9.rest_2_.rest_10_, f32[8,128]{1,0:T(8,128)S(1)} %collective-permute-done.10.rest_3_.rest_11_, ...), custom_call_target="tpu_custom_call" | custom-call | flops 1207959552 | tf_op jit(solution)/shard_map/final_grad/pallas_call | solution.py:602
  132.6 2.0 %collective-permute-done.50.b = bf16[608,128]{1,0:T(8,128)(2,1)S(1)} collective-permute-done((bf16[608,128]{1,0:T(8,128)(2,1)S(1)}, bf16[608,128]{1,0:T(8,128)(2,1)S(1)}, u32[]{:S(2)}, u32[]{:S(2)}) %collective-permute-start.50) | collective-permute-done | bytes 155680 | tf_op jit(solution)/shard_map/ppermute | solution.py:616
  134.7 1.8 %collective-permute-start.52 = (bf16[144,128]{1,0:T(8,128)(2,1)S(1)}, bf16[144,128]{1,0:T(8,128)(2,1)S(1)}, u32[]{:S(2)}, u32[]{:S(2)}) collective-permute-start(bf16[144,128]{1,0:T(8,128)(2,1)S(1)} %get-tuple-element.158), channel_id=1, source_target_pairs={{0,2},{1,3},{2,0},{3,1},{4,6},{5,7},{6,4},{7,5},{8,10},{9,11},{10,... | collective-permute-start | bytes 110600 | tf_op jit(solution)/shard_map/ppermute | solution.py:616
  136.4 1.0 collective-permute-start.53
  137.4 1.7 %collective-permute-start.54 = (bf16[144,128]{1,0:T(8,128)(2,1)S(1)}, bf16[144,128]{1,0:T(8,128)(2,1)S(1)}, u32[]{:S(2)}, u32[]{:S(2)}) collective-permute-start(bf16[144,128]{1,0:T(8,128)(2,1)S(1)} %get-tuple-element.160), channel_id=1, source_target_pairs={{0,6},{1,7},{2,4},{3,5},{4,2},{5,3},{6,0},{7,1},{8,14},{9,15},{10,... | collective-permute-start | bytes 110600 | tf_op jit(solution)/shard_map/ppermute | solution.py:616
  139.1 2.6 %collective-permute-done.53.b = bf16[144,128]{1,0:T(8,128)(2,1)S(1)} collective-permute-done((bf16[144,128]{1,0:T(8,128)(2,1)S(1)}, bf16[144,128]{1,0:T(8,128)(2,1)S(1)}, u32[]{:S(2)}, u32[]{:S(2)}) %collective-permute-start.53) | collective-permute-done | bytes 36896 | tf_op jit(solution)/shard_map/ppermute | solution.py:616
  141.7 1.4 collective-permute-done.54.c
  (104 shorter events, 12.1 us)
Async XLA Ops:
  0.6 16.5 %copy-start.3 = (s32[4,4,4,256]{3,2,1,0:T(4,128)S(1)}, s32[4,4,4,256]{3,2,1,0:T(4,128)}, u32[]{:S(2)}) copy-start(s32[4,4,4,256]{3,2,1,0:T(4,128)} %mask.3) | copy-start | bytes 196612
  0.6 16.4 %copy-start.5 = (f32[1,128]{1,0:T(1,128)S(1)}, f32[1,128]{1,0:T(1,128)}, u32[]{:S(2)}) copy-start(f32[1,128]{1,0:T(1,128)} %bias.3) | copy-start | bytes 1540
  0.7 16.4 %copy-start.4 = (f32[1,128]{1,0:T(1,128)S(1)}, f32[1,128]{1,0:T(1,128)}, u32[]{:S(2)}) copy-start(f32[1,128]{1,0:T(1,128)} %gain.3) | copy-start | bytes 1540
  0.7 16.4 %copy-start.1 = (bf16[1,1152,128]{2,1,0:T(8,128)(2,1)S(1)}, bf16[1,1152,128]{2,1,0:T(8,128)(2,1)}, u32[]{:S(2)}) copy-start(bf16[1,1152,128]{2,1,0:T(8,128)(2,1)} %own.1) | copy-start | bytes 884740
  0.7 16.5 %copy-start.2 = (bf16[1,4,4,256,128]{4,3,2,1,0:T(8,128)(2,1)S(1)}, bf16[1,4,4,256,128]{4,3,2,1,0:T(8,128)(2,1)}, u32[]{:S(2)}) copy-start(bf16[1,4,4,256,128]{4,3,2,1,0:T(8,128)(2,1)} %features.3) | copy-start | bytes 3145732
  2.7 11.1 %collective-permute-start = (bf16[2048,128]{1,0:T(8,128)(2,1)S(1)}, bf16[2048,128]{1,0:T(8,128)(2,1)S(1)}, u32[]{:S(2)}, u32[]{:S(2)}) collective-permute-start(bf16[2048,128]{1,0:T(8,128)(2,1)S(1)} %get-tuple-element.85), channel_id=1, source_target_pairs={{0,1},{1,0},{2,3},{3,2},{4,5},{5,4},{6,7},{7,6},{8,9},{9,8},{10,11... | collective-permute-start | bytes 1572872 | tf_op jit(solution)/shard_map/ppermute | solution.py:616
  3.3 10.5 %collective-permute-start.3 = (bf16[608,128]{1,0:T(8,128)(2,1)S(1)}, bf16[608,128]{1,0:T(8,128)(2,1)S(1)}, u32[]{:S(2)}, u32[]{:S(2)}) collective-permute-start(bf16[608,128]{1,0:T(8,128)(2,1)S(1)} %get-tuple-element.87), channel_id=1, source_target_pairs={{0,16},{8,24},{16,0},{24,8},{1,17},{9,25},{17,1},{25,9},{2,18},{10... | collective-permute-start | bytes 466952 | tf_op jit(solution)/shard_map/ppermute | solution.py:616
  5.9 8.0 %collective-permute-start.4 = (bf16[608,128]{1,0:T(8,128)(2,1)S(1)}, bf16[608,128]{1,0:T(8,128)(2,1)S(1)}, u32[]{:S(2)}, u32[]{:S(2)}) collective-permute-start(bf16[608,128]{1,0:T(8,128)(2,1)S(1)} %get-tuple-element.87), channel_id=1, source_target_pairs={{0,24},{8,16},{16,8},{24,0},{1,25},{9,17},{17,9},{25,1},{2,26},{10... | collective-permute-start | bytes 466952 | tf_op jit(solution)/shard_map/ppermute | solution.py:616
  7.3 7.8 %collective-permute-start.2 = (bf16[608,128]{1,0:T(8,128)(2,1)S(1)}, bf16[608,128]{1,0:T(8,128)(2,1)S(1)}, u32[]{:S(2)}, u32[]{:S(2)}) collective-permute-start(bf16[608,128]{1,0:T(8,128)(2,1)S(1)} %get-tuple-element.87), channel_id=1, source_target_pairs={{0,8},{8,0},{16,24},{24,16},{1,9},{9,1},{17,25},{25,17},{2,10},{10... | collective-permute-start | bytes 466952 | tf_op jit(solution)/shard_map/ppermute | solution.py:616
  7.4 9.8 %collective-permute-start.1 = (bf16[2048,128]{1,0:T(8,128)(2,1)S(1)}, bf16[2048,128]{1,0:T(8,128)(2,1)S(1)}, u32[]{:S(2)}, u32[]{:S(2)}) collective-permute-start(bf16[2048,128]{1,0:T(8,128)(2,1)S(1)} %get-tuple-element.86), channel_id=1, source_target_pairs={{1,2},{2,1},{3,4},{4,3},{5,6},{6,5},{9,10},{10,9},{11,12},{12,11},... | collective-permute-start | bytes 1572872 | tf_op jit(solution)/shard_map/ppermute | solution.py:623
  15.1 1.9 %collective-permute-start.5 = (bf16[3,608,128]{2,1,0:T(8,128)(2,1)S(1)}, bf16[3,608,128]{2,1,0:T(8,128)(2,1)S(1)}, u32[]{:S(2)}, u32[]{:S(2)}) collective-permute-start(bf16[3,608,128]{2,1,0:T(8,128)(2,1)S(1)} %pad_maximum_fusion), channel_id=1, source_target_pairs={{0,1},{1,0},{2,3},{3,2},{4,5},{5,4},{6,7},{7,6},{8,9},{9,8},{10,11... | collective-permute-start | bytes 1400840 | tf_op jit(solution)/shard_map/ppermute | solution.py:616
  19.9 2.3 %collective-permute-start.6 = (bf16[1056,128]{1,0:T(8,128)(2,1)S(1)}, bf16[1056,128]{1,0:T(8,128)(2,1)S(1)}, u32[]{:S(2)}, u32[]{:S(2)}) collective-permute-start(bf16[1056,128]{1,0:T(8,128)(2,1)S(1)} %get-tuple-element.92), channel_id=1, source_target_pairs={{0,1},{1,0},{2,3},{3,2},{4,5},{5,4},{6,7},{7,6},{8,9},{9,8},{10,11... | collective-permute-start | bytes 811016 | tf_op jit(solution)/shard_map/ppermute | solution.py:616
  21.0 6.9 %collective-permute-start.7 = (bf16[1024,128]{1,0:T(8,128)(2,1)S(1)}, bf16[1024,128]{1,0:T(8,128)(2,1)S(1)}, u32[]{:S(2)}, u32[]{:S(2)}) collective-permute-start(bf16[1024,128]{1,0:T(8,128)(2,1)S(1)} %far.7), channel_id=1, source_target_pairs={{1,2},{2,1},{3,4},{4,3},{5,6},{6,5},{9,10},{10,9},{11,12},{12,11},... | collective-permute-start | bytes 786440 | tf_op jit(solution)/shard_map/ppermute | solution.py:623
  22.2 9.5 %collective-permute-start.10 = (f32[8,128]{1,0:T(8,128)S(1)}, f32[8,128]{1,0:T(8,128)S(1)}, u32[]{:S(2)}, u32[]{:S(2)}) collective-permute-start(f32[8,128]{1,0:T(8,128)S(1)} %fusion.6.rest_0_.rest_8_), channel_id=1, source_target_pairs={{0,6},{1,7},{2,4},{3,5},{4,2},{5,3},{6,0},{7,1},{8,14},{9,15},{10,... | collective-permute-start | bytes 12296 | tf_op jit(solution)/shard_map/ppermute | solution.py:616
  27.3 4.5 %collective-permute-start.9 = (f32[8,128]{1,0:T(8,128)S(1)}, f32[8,128]{1,0:T(8,128)S(1)}, u32[]{:S(2)}, u32[]{:S(2)}) collective-permute-start(f32[8,128]{1,0:T(8,128)S(1)} %fusion.6.rest_0_.rest_8_), channel_id=1, source_target_pairs={{0,4},{1,5},{2,6},{3,7},{4,0},{5,1},{6,2},{7,3},{8,12},{9,13},{10,... | collective-permute-start | bytes 12296 | tf_op jit(solution)/shard_map/ppermute | solution.py:616
  27.3 4.5 %collective-permute-start.8 = (f32[8,128]{1,0:T(8,128)S(1)}, f32[8,128]{1,0:T(8,128)S(1)}, u32[]{:S(2)}, u32[]{:S(2)}) collective-permute-start(f32[8,128]{1,0:T(8,128)S(1)} %fusion.6.rest_0_.rest_8_), channel_id=1, source_target_pairs={{0,2},{1,3},{2,0},{3,1},{4,6},{5,7},{6,4},{7,5},{8,10},{9,11},{10,... | collective-permute-start | bytes 12296 | tf_op jit(solution)/shard_map/ppermute | solution.py:616
  34.9 1.6 %collective-permute-start.11 = (bf16[1056,128]{1,0:T(8,128)(2,1)S(1)}, bf16[1056,128]{1,0:T(8,128)(2,1)S(1)}, u32[]{:S(2)}, u32[]{:S(2)}) collective-permute-start(bf16[1056,128]{1,0:T(8,128)(2,1)S(1)} %get-tuple-element.97), channel_id=1, source_target_pairs={{0,1},{1,0},{2,3},{3,2},{4,5},{5,4},{6,7},{7,6},{8,9},{9,8},{10,11... | collective-permute-start | bytes 811016 | tf_op jit(solution)/shard_map/ppermute | solution.py:616
  35.0 7.2 %collective-permute-start.12 = (bf16[1024,128]{1,0:T(8,128)(2,1)S(1)}, bf16[1024,128]{1,0:T(8,128)(2,1)S(1)}, u32[]{:S(2)}, u32[]{:S(2)}) collective-permute-start(bf16[1024,128]{1,0:T(8,128)(2,1)S(1)} %far.8), channel_id=1, source_target_pairs={{1,2},{2,1},{3,4},{4,3},{5,6},{6,5},{9,10},{10,9},{11,12},{12,11},... | collective-permute-start | bytes 786440 | tf_op jit(solution)/shard_map/ppermute | solution.py:623
  36.5 8.5 %collective-permute-start.15 = (f32[8,128]{1,0:T(8,128)S(1)}, f32[8,128]{1,0:T(8,128)S(1)}, u32[]{:S(2)}, u32[]{:S(2)}) collective-permute-start(f32[8,128]{1,0:T(8,128)S(1)} %fusion.5.rest_0_.rest_8_), channel_id=1, source_target_pairs={{0,6},{1,7},{2,4},{3,5},{4,2},{5,3},{6,0},{7,1},{8,14},{9,15},{10,... | collective-permute-start | bytes 12296 | tf_op jit(solution)/shard_map/ppermute | solution.py:616
  40.6 4.5 %collective-permute-start.14 = (f32[8,128]{1,0:T(8,128)S(1)}, f32[8,128]{1,0:T(8,128)S(1)}, u32[]{:S(2)}, u32[]{:S(2)}) collective-permute-start(f32[8,128]{1,0:T(8,128)S(1)} %fusion.5.rest_0_.rest_8_), channel_id=1, source_target_pairs={{0,4},{1,5},{2,6},{3,7},{4,0},{5,1},{6,2},{7,3},{8,12},{9,13},{10,... | collective-permute-start | bytes 12296 | tf_op jit(solution)/shard_map/ppermute | solution.py:616
  40.6 4.5 %collective-permute-start.13 = (f32[8,128]{1,0:T(8,128)S(1)}, f32[8,128]{1,0:T(8,128)S(1)}, u32[]{:S(2)}, u32[]{:S(2)}) collective-permute-start(f32[8,128]{1,0:T(8,128)S(1)} %fusion.5.rest_0_.rest_8_), channel_id=1, source_target_pairs={{0,2},{1,3},{2,0},{3,1},{4,6},{5,7},{6,4},{7,5},{8,10},{9,11},{10,... | collective-permute-start | bytes 12296 | tf_op jit(solution)/shard_map/ppermute | solution.py:616
  48.1 1.6 %collective-permute-start.16 = (bf16[1056,128]{1,0:T(8,128)(2,1)S(1)}, bf16[1056,128]{1,0:T(8,128)(2,1)S(1)}, u32[]{:S(2)}, u32[]{:S(2)}) collective-permute-start(bf16[1056,128]{1,0:T(8,128)(2,1)S(1)} %get-tuple-element.103), channel_id=1, source_target_pairs={{0,1},{1,0},{2,3},{3,2},{4,5},{5,4},{6,7},{7,6},{8,9},{9,8},{10,11... | collective-permute-start | bytes 811016 | tf_op jit(solution)/shard_map/ppermute | solution.py:616
  48.2 7.2 %collective-permute-start.17 = (bf16[1024,128]{1,0:T(8,128)(2,1)S(1)}, bf16[1024,128]{1,0:T(8,128)(2,1)S(1)}, u32[]{:S(2)}, u32[]{:S(2)}) collective-permute-start(bf16[1024,128]{1,0:T(8,128)(2,1)S(1)} %far.9), channel_id=1, source_target_pairs={{1,2},{2,1},{3,4},{4,3},{5,6},{6,5},{9,10},{10,9},{11,12},{12,11},... | collective-permute-start | bytes 786440 | tf_op jit(solution)/shard_map/ppermute | solution.py:623
  49.7 8.5 %collective-permute-start.20 = (f32[8,128]{1,0:T(8,128)S(1)}, f32[8,128]{1,0:T(8,128)S(1)}, u32[]{:S(2)}, u32[]{:S(2)}) collective-permute-start(f32[8,128]{1,0:T(8,128)S(1)} %fusion.4.rest_0_.rest_8_), channel_id=1, source_target_pairs={{0,6},{1,7},{2,4},{3,5},{4,2},{5,3},{6,0},{7,1},{8,14},{9,15},{10,... | collective-permute-start | bytes 12296 | tf_op jit(solution)/shard_map/ppermute | solution.py:616
  53.9 4.5 %collective-permute-start.19 = (f32[8,128]{1,0:T(8,128)S(1)}, f32[8,128]{1,0:T(8,128)S(1)}, u32[]{:S(2)}, u32[]{:S(2)}) collective-permute-start(f32[8,128]{1,0:T(8,128)S(1)} %fusion.4.rest_0_.rest_8_), channel_id=1, source_target_pairs={{0,4},{1,5},{2,6},{3,7},{4,0},{5,1},{6,2},{7,3},{8,12},{9,13},{10,... | collective-permute-start | bytes 12296 | tf_op jit(solution)/shard_map/ppermute | solution.py:616
  53.9 4.5 %collective-permute-start.18 = (f32[8,128]{1,0:T(8,128)S(1)}, f32[8,128]{1,0:T(8,128)S(1)}, u32[]{:S(2)}, u32[]{:S(2)}) collective-permute-start(f32[8,128]{1,0:T(8,128)S(1)} %fusion.4.rest_0_.rest_8_), channel_id=1, source_target_pairs={{0,2},{1,3},{2,0},{3,1},{4,6},{5,7},{6,4},{7,5},{8,10},{9,11},{10,... | collective-permute-start | bytes 12296 | tf_op jit(solution)/shard_map/ppermute | solution.py:616
  61.4 1.6 %collective-permute-start.21 = (bf16[1056,128]{1,0:T(8,128)(2,1)S(1)}, bf16[1056,128]{1,0:T(8,128)(2,1)S(1)}, u32[]{:S(2)}, u32[]{:S(2)}) collective-permute-start(bf16[1056,128]{1,0:T(8,128)(2,1)S(1)} %get-tuple-element.110), channel_id=1, source_target_pairs={{0,1},{1,0},{2,3},{3,2},{4,5},{5,4},{6,7},{7,6},{8,9},{9,8},{10,11... | collective-permute-start | bytes 811016 | tf_op jit(solution)/shard_map/ppermute | solution.py:616
  61.5 17.5 %collective-permute-start.29 = (bf16[1024,128]{1,0:T(8,128)(2,1)S(1)}, bf16[1024,128]{1,0:T(8,128)(2,1)S(1)}, u32[]{:S(2)}, u32[]{:S(2)}) collective-permute-start(bf16[1024,128]{1,0:T(8,128)(2,1)S(1)} %far.10), channel_id=1, source_target_pairs={{1,2},{2,1},{3,4},{4,3},{5,6},{6,5},{9,10},{10,9},{11,12},{12,11},... | collective-permute-start | bytes 786440 | tf_op jit(solution)/shard_map/ppermute | solution.py:623
  63.0 8.6 %copy-start = (bf16[1,4,4,256,128]{4,3,2,1,0:T(8,128)(2,1)S(1)}, bf16[1,4,4,256,128]{4,3,2,1,0:T(8,128)(2,1)}, u32[]{:S(2)}) copy-start(bf16[1,4,4,256,128]{4,3,2,1,0:T(8,128)(2,1)} %rest_15_.1) | copy-start | bytes 3145732
  63.0 8.4 %collective-permute-start.24 = (f32[8,128]{1,0:T(8,128)S(1)}, f32[8,128]{1,0:T(8,128)S(1)}, u32[]{:S(2)}, u32[]{:S(2)}) collective-permute-start(f32[8,128]{1,0:T(8,128)S(1)} %fusion.3.rest_0_), channel_id=1, source_target_pairs={{0,6},{1,7},{2,4},{3,5},{4,2},{5,3},{6,0},{7,1},{8,14},{9,15},{10,... | collective-permute-start | bytes 12296 | tf_op jit(solution)/shard_map/ppermute | solution.py:616
  67.1 4.5 %collective-permute-start.23 = (f32[8,128]{1,0:T(8,128)S(1)}, f32[8,128]{1,0:T(8,128)S(1)}, u32[]{:S(2)}, u32[]{:S(2)}) collective-permute-start(f32[8,128]{1,0:T(8,128)S(1)} %fusion.3.rest_0_), channel_id=1, source_target_pairs={{0,4},{1,5},{2,6},{3,7},{4,0},{5,1},{6,2},{7,3},{8,12},{9,13},{10,... | collective-permute-start | bytes 12296 | tf_op jit(solution)/shard_map/ppermute | solution.py:616
  67.1 4.5 %collective-permute-start.22 = (f32[8,128]{1,0:T(8,128)S(1)}, f32[8,128]{1,0:T(8,128)S(1)}, u32[]{:S(2)}, u32[]{:S(2)}) collective-permute-start(f32[8,128]{1,0:T(8,128)S(1)} %fusion.3.rest_0_), channel_id=1, source_target_pairs={{0,2},{1,3},{2,0},{3,1},{4,6},{5,7},{6,4},{7,5},{8,10},{9,11},{10,... | collective-permute-start | bytes 12296 | tf_op jit(solution)/shard_map/ppermute | solution.py:616
  72.6 1.2 collective-permute-start.25
  73.9 5.4 %collective-permute-start.28 = (f32[8,128]{1,0:T(8,128)S(1)}, f32[8,128]{1,0:T(8,128)S(1)}, u32[]{:S(2)}, u32[]{:S(2)}) collective-permute-start(f32[8,128]{1,0:T(8,128)S(1)} %add.78.rest_4_), channel_id=1, source_target_pairs={{0,6},{1,7},{2,4},{3,5},{4,2},{5,3},{6,0},{7,1},{8,14},{9,15},{10,... | collective-permute-start | bytes 12296 | tf_op jit(solution)/shard_map/ppermute | solution.py:616
  75.3 4.5 %collective-permute-start.27 = (f32[8,128]{1,0:T(8,128)S(1)}, f32[8,128]{1,0:T(8,128)S(1)}, u32[]{:S(2)}, u32[]{:S(2)}) collective-permute-start(f32[8,128]{1,0:T(8,128)S(1)} %add.78.rest_4_), channel_id=1, source_target_pairs={{0,4},{1,5},{2,6},{3,7},{4,0},{5,1},{6,2},{7,3},{8,12},{9,13},{10,... | collective-permute-start | bytes 12296 | tf_op jit(solution)/shard_map/ppermute | solution.py:616
  75.9 4.0 %collective-permute-start.26 = (f32[8,128]{1,0:T(8,128)S(1)}, f32[8,128]{1,0:T(8,128)S(1)}, u32[]{:S(2)}, u32[]{:S(2)}) collective-permute-start(f32[8,128]{1,0:T(8,128)S(1)} %add.78.rest_4_), channel_id=1, source_target_pairs={{0,2},{1,3},{2,0},{3,1},{4,6},{5,7},{6,4},{7,5},{8,10},{9,11},{10,... | collective-permute-start | bytes 12296 | tf_op jit(solution)/shard_map/ppermute | solution.py:616
  83.0 1.6 %collective-permute-start.30 = (bf16[1056,128]{1,0:T(8,128)(2,1)S(1)}, bf16[1056,128]{1,0:T(8,128)(2,1)S(1)}, u32[]{:S(2)}, u32[]{:S(2)}) collective-permute-start(bf16[1056,128]{1,0:T(8,128)(2,1)S(1)} %get-tuple-element.117), channel_id=1, source_target_pairs={{0,1},{1,0},{2,3},{3,2},{4,5},{5,4},{6,7},{7,6},{8,9},{9,8},{10,11... | collective-permute-start | bytes 811016 | tf_op jit(solution)/shard_map/ppermute | solution.py:616
  83.1 8.1 %collective-permute-start.34 = (bf16[1024,128]{1,0:T(8,128)(2,1)S(1)}, bf16[1024,128]{1,0:T(8,128)(2,1)S(1)}, u32[]{:S(2)}, u32[]{:S(2)}) collective-permute-start(bf16[1024,128]{1,0:T(8,128)(2,1)S(1)} %far.11), channel_id=1, source_target_pairs={{1,2},{2,1},{3,4},{4,3},{5,6},{6,5},{9,10},{10,9},{11,12},{12,11},... | collective-permute-start | bytes 786440 | tf_op jit(solution)/shard_map/ppermute | solution.py:623
  84.6 8.5 %collective-permute-start.33 = (f32[8,128]{1,0:T(8,128)S(1)}, f32[8,128]{1,0:T(8,128)S(1)}, u32[]{:S(2)}, u32[]{:S(2)}) collective-permute-start(f32[8,128]{1,0:T(8,128)S(1)} %fusion.2.rest_4_), channel_id=1, source_target_pairs={{0,6},{1,7},{2,4},{3,5},{4,2},{5,3},{6,0},{7,1},{8,14},{9,15},{10,... | collective-permute-start | bytes 12296 | tf_op jit(solution)/shard_map/ppermute | solution.py:616
  88.6 4.5 %collective-permute-start.32 = (f32[8,128]{1,0:T(8,128)S(1)}, f32[8,128]{1,0:T(8,128)S(1)}, u32[]{:S(2)}, u32[]{:S(2)}) collective-permute-start(f32[8,128]{1,0:T(8,128)S(1)} %fusion.2.rest_4_), channel_id=1, source_target_pairs={{0,4},{1,5},{2,6},{3,7},{4,0},{5,1},{6,2},{7,3},{8,12},{9,13},{10,... | collective-permute-start | bytes 12296 | tf_op jit(solution)/shard_map/ppermute | solution.py:616
  88.7 4.5 %collective-permute-start.31 = (f32[8,128]{1,0:T(8,128)S(1)}, f32[8,128]{1,0:T(8,128)S(1)}, u32[]{:S(2)}, u32[]{:S(2)}) collective-permute-start(f32[8,128]{1,0:T(8,128)S(1)} %fusion.2.rest_4_), channel_id=1, source_target_pairs={{0,2},{1,3},{2,0},{3,1},{4,6},{5,7},{6,4},{7,5},{8,10},{9,11},{10,... | collective-permute-start | bytes 12296 | tf_op jit(solution)/shard_map/ppermute | solution.py:616
  96.2 1.6 %collective-permute-start.35 = (bf16[1056,128]{1,0:T(8,128)(2,1)S(1)}, bf16[1056,128]{1,0:T(8,128)(2,1)S(1)}, u32[]{:S(2)}, u32[]{:S(2)}) collective-permute-start(bf16[1056,128]{1,0:T(8,128)(2,1)S(1)} %get-tuple-element.125), channel_id=1, source_target_pairs={{0,1},{1,0},{2,3},{3,2},{4,5},{5,4},{6,7},{7,6},{8,9},{9,8},{10,11... | collective-permute-start | bytes 811016 | tf_op jit(solution)/shard_map/ppermute | solution.py:616
  96.3 8.3 %collective-permute-start.39 = (bf16[1024,128]{1,0:T(8,128)(2,1)S(1)}, bf16[1024,128]{1,0:T(8,128)(2,1)S(1)}, u32[]{:S(2)}, u32[]{:S(2)}) collective-permute-start(bf16[1024,128]{1,0:T(8,128)(2,1)S(1)} %far.12), channel_id=1, source_target_pairs={{1,2},{2,1},{3,4},{4,3},{5,6},{6,5},{9,10},{10,9},{11,12},{12,11},... | collective-permute-start | bytes 786440 | tf_op jit(solution)/shard_map/ppermute | solution.py:623
  97.8 8.4 %collective-permute-start.38 = (f32[8,128]{1,0:T(8,128)S(1)}, f32[8,128]{1,0:T(8,128)S(1)}, u32[]{:S(2)}, u32[]{:S(2)}) collective-permute-start(f32[8,128]{1,0:T(8,128)S(1)} %fusion.1.rest_4_), channel_id=1, source_target_pairs={{0,6},{1,7},{2,4},{3,5},{4,2},{5,3},{6,0},{7,1},{8,14},{9,15},{10,... | collective-permute-start | bytes 12296 | tf_op jit(solution)/shard_map/ppermute | solution.py:616
  102.1 4.5 %collective-permute-start.37 = (f32[8,128]{1,0:T(8,128)S(1)}, f32[8,128]{1,0:T(8,128)S(1)}, u32[]{:S(2)}, u32[]{:S(2)}) collective-permute-start(f32[8,128]{1,0:T(8,128)S(1)} %fusion.1.rest_4_), channel_id=1, source_target_pairs={{0,4},{1,5},{2,6},{3,7},{4,0},{5,1},{6,2},{7,3},{8,12},{9,13},{10,... | collective-permute-start | bytes 12296 | tf_op jit(solution)/shard_map/ppermute | solution.py:616
  102.1 4.5 %collective-permute-start.36 = (f32[8,128]{1,0:T(8,128)S(1)}, f32[8,128]{1,0:T(8,128)S(1)}, u32[]{:S(2)}, u32[]{:S(2)}) collective-permute-start(f32[8,128]{1,0:T(8,128)S(1)} %fusion.1.rest_4_), channel_id=1, source_target_pairs={{0,2},{1,3},{2,0},{3,1},{4,6},{5,7},{6,4},{7,5},{8,10},{9,11},{10,... | collective-permute-start | bytes 12296 | tf_op jit(solution)/shard_map/ppermute | solution.py:616
  109.6 1.6 %collective-permute-start.40 = (bf16[1056,128]{1,0:T(8,128)(2,1)S(1)}, bf16[1056,128]{1,0:T(8,128)(2,1)S(1)}, u32[]{:S(2)}, u32[]{:S(2)}) collective-permute-start(bf16[1056,128]{1,0:T(8,128)(2,1)S(1)} %get-tuple-element.133), channel_id=1, source_target_pairs={{0,1},{1,0},{2,3},{3,2},{4,5},{5,4},{6,7},{7,6},{8,9},{9,8},{10,11... | collective-permute-start | bytes 811016 | tf_op jit(solution)/shard_map/ppermute | solution.py:616
  109.7 12.7 %collective-permute-start.47 = (bf16[4,144,128]{2,1,0:T(8,128)(2,1)S(1)}, bf16[4,144,128]{2,1,0:T(8,128)(2,1)S(1)}, u32[]{:S(2)}, u32[]{:S(2)}) collective-permute-start(bf16[4,144,128]{2,1,0:T(8,128)(2,1)S(1)} %get-tuple-element.120), channel_id=1, source_target_pairs={{0,1},{1,0},{2,3},{3,2},{4,5},{5,4},{6,7},{7,6},{8,9},{9,8},{10,11... | collective-permute-start | bytes 442376 | tf_op jit(solution)/shard_map/ppermute | solution.py:616
  110.2 12.2 %collective-permute-start.46 = (bf16[4,144,128]{2,1,0:T(8,128)(2,1)S(1)}, bf16[4,144,128]{2,1,0:T(8,128)(2,1)S(1)}, u32[]{:S(2)}, u32[]{:S(2)}) collective-permute-start(bf16[4,144,128]{2,1,0:T(8,128)(2,1)S(1)} %get-tuple-element.128), channel_id=1, source_target_pairs={{0,1},{1,0},{2,3},{3,2},{4,5},{5,4},{6,7},{7,6},{8,9},{9,8},{10,11... | collective-permute-start | bytes 442376 | tf_op jit(solution)/shard_map/ppermute | solution.py:616
  111.2 6.3 %collective-permute-start.43 = (f32[8,128]{1,0:T(8,128)S(1)}, f32[8,128]{1,0:T(8,128)S(1)}, u32[]{:S(2)}, u32[]{:S(2)}) collective-permute-start(f32[8,128]{1,0:T(8,128)S(1)} %fusion.rest_4_), channel_id=1, source_target_pairs={{0,6},{1,7},{2,4},{3,5},{4,2},{5,3},{6,0},{7,1},{8,14},{9,15},{10,... | collective-permute-start | bytes 12296 | tf_op jit(solution)/shard_map/ppermute | solution.py:616
  113.0 5.2 %collective-permute-start.42 = (f32[8,128]{1,0:T(8,128)S(1)}, f32[8,128]{1,0:T(8,128)S(1)}, u32[]{:S(2)}, u32[]{:S(2)}) collective-permute-start(f32[8,128]{1,0:T(8,128)S(1)} %fusion.rest_4_), channel_id=1, source_target_pairs={{0,4},{1,5},{2,6},{3,7},{4,0},{5,1},{6,2},{7,3},{8,12},{9,13},{10,... | collective-permute-start | bytes 12296 | tf_op jit(solution)/shard_map/ppermute | solution.py:616
  113.3 6.3 %collective-permute-start.41 = (f32[8,128]{1,0:T(8,128)S(1)}, f32[8,128]{1,0:T(8,128)S(1)}, u32[]{:S(2)}, u32[]{:S(2)}) collective-permute-start(f32[8,128]{1,0:T(8,128)S(1)} %fusion.rest_4_), channel_id=1, source_target_pairs={{0,2},{1,3},{2,0},{3,1},{4,6},{5,7},{6,4},{7,5},{8,10},{9,11},{10,... | collective-permute-start | bytes 12296 | tf_op jit(solution)/shard_map/ppermute | solution.py:616
  117.5 11.5 %collective-permute-start.48 = (bf16[1024,128]{1,0:T(8,128)(2,1)S(1)}, bf16[1024,128]{1,0:T(8,128)(2,1)S(1)}, u32[]{:S(2)}, u32[]{:S(2)}) collective-permute-start(bf16[1024,128]{1,0:T(8,128)(2,1)S(1)} %far.13), channel_id=1, source_target_pairs={{1,2},{2,1},{3,4},{4,3},{5,6},{6,5},{9,10},{10,9},{11,12},{12,11},... | collective-permute-start | bytes 786440 | tf_op jit(solution)/shard_map/ppermute | solution.py:623
  118.2 4.2 %collective-permute-start.45 = (bf16[4,144,128]{2,1,0:T(8,128)(2,1)S(1)}, bf16[4,144,128]{2,1,0:T(8,128)(2,1)S(1)}, u32[]{:S(2)}, u32[]{:S(2)}) collective-permute-start(bf16[4,144,128]{2,1,0:T(8,128)(2,1)S(1)} %get-tuple-element.136), channel_id=1, source_target_pairs={{0,1},{1,0},{2,3},{3,2},{4,5},{5,4},{6,7},{7,6},{8,9},{9,8},{10,11... | collective-permute-start | bytes 442376 | tf_op jit(solution)/shard_map/ppermute | solution.py:616
  122.3 1.4 collective-permute-start.44
  123.9 8.7 %collective-permute-start.49 = (bf16[608,128]{1,0:T(8,128)(2,1)S(1)}, bf16[608,128]{1,0:T(8,128)(2,1)S(1)}, u32[]{:S(2)}, u32[]{:S(2)}) collective-permute-start(bf16[608,128]{1,0:T(8,128)(2,1)S(1)} %get-tuple-element.153), channel_id=1, source_target_pairs={{0,8},{8,0},{16,24},{24,16},{1,9},{9,1},{17,25},{25,17},{2,10},{10... | collective-permute-start | bytes 466952 | tf_op jit(solution)/shard_map/ppermute | solution.py:616
  125.4 9.1 %collective-permute-start.50 = (bf16[608,128]{1,0:T(8,128)(2,1)S(1)}, bf16[608,128]{1,0:T(8,128)(2,1)S(1)}, u32[]{:S(2)}, u32[]{:S(2)}) collective-permute-start(bf16[608,128]{1,0:T(8,128)(2,1)S(1)} %get-tuple-element.155), channel_id=1, source_target_pairs={{0,16},{8,24},{16,0},{24,8},{1,17},{9,25},{17,1},{25,9},{2,18},{10... | collective-permute-start | bytes 466952 | tf_op jit(solution)/shard_map/ppermute | solution.py:616
  127.0 7.6 %collective-permute-start.51 = (bf16[608,128]{1,0:T(8,128)(2,1)S(1)}, bf16[608,128]{1,0:T(8,128)(2,1)S(1)}, u32[]{:S(2)}, u32[]{:S(2)}) collective-permute-start(bf16[608,128]{1,0:T(8,128)(2,1)S(1)} %get-tuple-element.156), channel_id=1, source_target_pairs={{0,24},{8,16},{16,8},{24,0},{1,25},{9,17},{17,9},{25,1},{2,26},{10... | collective-permute-start | bytes 466952 | tf_op jit(solution)/shard_map/ppermute | solution.py:616
  134.7 4.5 %collective-permute-start.52 = (bf16[144,128]{1,0:T(8,128)(2,1)S(1)}, bf16[144,128]{1,0:T(8,128)(2,1)S(1)}, u32[]{:S(2)}, u32[]{:S(2)}) collective-permute-start(bf16[144,128]{1,0:T(8,128)(2,1)S(1)} %get-tuple-element.158), channel_id=1, source_target_pairs={{0,2},{1,3},{2,0},{3,1},{4,6},{5,7},{6,4},{7,5},{8,10},{9,11},{10,... | collective-permute-start | bytes 110600 | tf_op jit(solution)/shard_map/ppermute | solution.py:616
  136.4 5.3 %collective-permute-start.53 = (bf16[144,128]{1,0:T(8,128)(2,1)S(1)}, bf16[144,128]{1,0:T(8,128)(2,1)S(1)}, u32[]{:S(2)}, u32[]{:S(2)}) collective-permute-start(bf16[144,128]{1,0:T(8,128)(2,1)S(1)} %get-tuple-element.159), channel_id=1, source_target_pairs={{0,4},{1,5},{2,6},{3,7},{4,0},{5,1},{6,2},{7,3},{8,12},{9,13},{10,... | collective-permute-start | bytes 110600 | tf_op jit(solution)/shard_map/ppermute | solution.py:616
  137.4 5.8 %collective-permute-start.54 = (bf16[144,128]{1,0:T(8,128)(2,1)S(1)}, bf16[144,128]{1,0:T(8,128)(2,1)S(1)}, u32[]{:S(2)}, u32[]{:S(2)}) collective-permute-start(bf16[144,128]{1,0:T(8,128)(2,1)S(1)} %get-tuple-element.160), channel_id=1, source_target_pairs={{0,6},{1,7},{2,4},{3,5},{4,2},{5,3},{6,0},{7,1},{8,14},{9,15},{10,... | collective-permute-start | bytes 110600 | tf_op jit(solution)/shard_map/ppermute | solution.py:616
where the time goes:
time: 144 us
  starting transfers between devices  60.7 us (42%)
  Pallas kernels  41.6 us (29%)
  waiting for transfers between devices  40.2 us (28%)
    ppermute x47, starting transfers between devices, swap(): return lax.ppermute(value, axis, [(i, i ^ step) for i in range(count)])  54.9 us
    pallas_call x30, Pallas kernels, call(): pl.pallas_call(body, out_shape=[jax.ShapeDtypeStruct(s, d) for s, d in ou...  41.6 us
    ppermute x47, waiting for transfers between devices, swap(): return lax.ppermute(value, axis, [(i, i ^ step) for i in range(count)])  40.2 us
    ppermute x8, starting transfers between devices, swap_next(): return lax.ppermute(value, 'row', pairs)  5.82 us
  transfers between devices with their start and end apart: 55, of which 29 were waited for; matrix products, arithmetic and copies ran while one was open for 0% of the time, Pallas kernels for 13%

commit v1 on v0

--- a/solution.py
+++ b/solution.py
@@ -628,7 +628,7 @@
     stride = 2
     while True:
         group = min(4, count // stride)
-        pieces = [total] + [swap(total, "row", k * stride) for k in range(1, group)]
+        pieces = [total] + [swap(total, "row", k * stride + (stride == 2)) for k in range(1, group)]
         stride *= group
         if stride >= count:
             return pieces

time: 144 us -> 139 us (0.965)
  waiting for transfers between devices: 40.2 us -> 24.2 us
  starting transfers between devices: 60.7 us -> 71.2 us
    ppermute x47, waiting for transfers between devices: 40.2 us -> 24.2 us  [swap(): return lax.ppermute(value, axis, [(i, i ^ step) for i in range(count)])]
    ppermute x47, starting transfers between devices: 54.9 us -> 65.4 us  [swap(): return lax.ppermute(value, axis, [(i, i ^ step) for i in range(count)])]
  transfers between devices with their start and end apart: 55 -> 55, of which waited for: 29 -> 22; matrix products, arithmetic and copies ran while one was open for 0% -> 0% of each run, Pallas kernels for 13% -> 13%
where the time goes in v1:
time: 139 us; the launch traced here: 138 us
  starting transfers between devices  71.2 us (51%)
  Pallas kernels  41.6 us (30%)
  waiting for transfers between devices  24.2 us (17%)
    ppermute x47, starting transfers between devices, swap(): return lax.ppermute(value, axis, [(i, i ^ step) for i in range(count)])  65.4 us
    pallas_call x30, Pallas kernels, call(): pl.pallas_call(body, out_shape=[jax.ShapeDtypeStruct(s, d) for s, d in ou...  41.6 us
    ppermute x47, waiting for transfers between devices, swap(): return lax.ppermute(value, axis, [(i, i ^ step) for i in range(count)])  24.2 us
    ppermute x8, starting transfers between devices, swap_next(): return lax.ppermute(value, 'row', pairs)  5.82 us
  transfers between devices with their start and end apart: 55, of which 22 were waited for; matrix products, arithmetic and copies ran while one was open for 0% of the time, Pallas kernels for 13%

profile of v1, /device:TPU:0, one launch (start us, length us, event | category | flops | bytes accessed | tf_op | source)
XLA Modules:
  0.0 138.2 jit_solution(16270581613955872171)
XLA Ops:
  0.7 2.1 %prep.1 = (bf16[2048,128]{1,0:T(8,128)(2,1)S(1)}, bf16[2048,128]{1,0:T(8,128)(2,1)S(1)}, bf16[608,128]{1,0:T(8,128)(2,1)S(1)}) custom-call(s32[4,4,4,256]{3,2,1,0:T(4,128)} %mask.3, bf16[1,4,4,256,128]{4,3,2,1,0:T(8,128)(2,1)} %features.3, bf16[1,4,4,256,128]{4,3,2,1,0:T(8,128)(2,1)} %rest_15_.1, bf16[1,1152,128]{2,1,0:T(8,128)(2,1)} %own.1, f32[1,128]{1,0:T(1,128)} %gain.3, ...), custom_call_target="tpu_custom_call" | custom-call | tf_op jit(solution)/shard_map/prep/pallas_call | solution.py:602
  3.3 2.6 %collective-permute-start.3 = (bf16[608,128]{1,0:T(8,128)(2,1)S(1)}, bf16[608,128]{1,0:T(8,128)(2,1)S(1)}, u32[]{:S(2)}, u32[]{:S(2)}) collective-permute-start(bf16[608,128]{1,0:T(8,128)(2,1)S(1)} %get-tuple-element.87), channel_id=1, source_target_pairs={{0,16},{8,24},{16,0},{24,8},{1,17},{9,25},{17,1},{25,9},{2,18},{10... | collective-permute-start | bytes 466952 | tf_op jit(solution)/shard_map/ppermute | solution.py:616
  5.9 1.4 %collective-permute-start.4 = (bf16[608,128]{1,0:T(8,128)(2,1)S(1)}, bf16[608,128]{1,0:T(8,128)(2,1)S(1)}, u32[]{:S(2)}, u32[]{:S(2)}) collective-permute-start(bf16[608,128]{1,0:T(8,128)(2,1)S(1)} %get-tuple-element.87), channel_id=1, source_target_pairs={{0,24},{8,16},{16,8},{24,0},{1,25},{9,17},{17,9},{25,1},{2,26},{10... | collective-permute-start | bytes 466952 | tf_op jit(solution)/shard_map/ppermute | solution.py:616
  8.1 5.7 %collective-permute-done.3.r2 = bf16[608,128]{1,0:T(8,128)(2,1)S(1)} collective-permute-done((bf16[608,128]{1,0:T(8,128)(2,1)S(1)}, bf16[608,128]{1,0:T(8,128)(2,1)S(1)}, u32[]{:S(2)}, u32[]{:S(2)}) %collective-permute-start.3) | collective-permute-done | bytes 155680 | tf_op jit(solution)/shard_map/ppermute | solution.py:616
  13.8 1.3 collective-permute-done.2.r1
  15.2 1.8 %collective-permute-done.5.other = bf16[3,608,128]{2,1,0:T(8,128)(2,1)S(1)} collective-permute-done((bf16[3,608,128]{2,1,0:T(8,128)(2,1)S(1)}, bf16[3,608,128]{2,1,0:T(8,128)(2,1)S(1)}, u32[]{:S(2)}, u32[]{:S(2)}) %collective-permute-start.5) | collective-permute-done | bytes 466976 | tf_op jit(solution)/shard_map/ppermute | solution.py:616
  17.2 2.7 %forward.4 = (bf16[4,6,256,128]{3,2,1,0:T(8,128)(2,1)S(1)}, f32[4,4,256,128]{3,2,1,0:T(8,128)S(1)}, bf16[1056,128]{1,0:T(8,128)(2,1)S(1)}, f32[8,128]{1,0:T(8,128)S(1)}) custom-call(s32[4,4,4,256]{3,2,1,0:T(4,128)S(1)} %copy-done.3, bf16[1,4,4,256,128]{4,3,2,1,0:T(8,128)(2,1)S(1)} %copy-done.2, bf16[2048,128]{1,0:T(8,128)(2,1)S(1)} %collective-permute-done.near.rest_16_, ...), custom_call_target="tpu_custom_call" | custom-call | flops 1207959552 | tf_op jit(solution)/shard_map/forward/pallas_call | solution.py:602
  19.9 1.1 collective-permute-start.6
  22.2 3.8 %collective-permute-start.10 = (f32[8,128]{1,0:T(8,128)S(1)}, f32[8,128]{1,0:T(8,128)S(1)}, u32[]{:S(2)}, u32[]{:S(2)}) collective-permute-start(f32[8,128]{1,0:T(8,128)S(1)} %fusion.6.rest_0_.rest_8_), channel_id=1, source_target_pairs={{0,7},{1,6},{2,5},{3,4},{4,3},{5,2},{6,1},{7,0},{8,15},{9,14},{10,... | collective-permute-start | bytes 12296 | tf_op jit(solution)/shard_map/ppermute | solution.py:616
  26.0 1.1 collective-permute-start.9
  27.1 1.5 %collective-permute-start.8 = (f32[8,128]{1,0:T(8,128)S(1)}, f32[8,128]{1,0:T(8,128)S(1)}, u32[]{:S(2)}, u32[]{:S(2)}) collective-permute-start(f32[8,128]{1,0:T(8,128)S(1)} %fusion.6.rest_0_.rest_8_), channel_id=1, source_target_pairs={{0,3},{1,2},{2,1},{3,0},{4,7},{5,6},{6,5},{7,4},{8,11},{9,10},{10,... | collective-permute-start | bytes 12296 | tf_op jit(solution)/shard_map/ppermute | solution.py:616
  28.6 1.4 collective-permute-done.9.rest_2_.rest_10_
  30.1 3.1 %forward.5 = (bf16[4,6,256,128]{3,2,1,0:T(8,128)(2,1)S(1)}, f32[4,4,256,128]{3,2,1,0:T(8,128)S(1)}, bf16[1056,128]{1,0:T(8,128)(2,1)S(1)}, f32[8,128]{1,0:T(8,128)S(1)}) custom-call(bf16[4,6,256,128]{3,2,1,0:T(8,128)(2,1)S(1)} %get-tuple-element.90.x_in.rest_14_, f32[4,4,256,128]{3,2,1,0:T(8,128)S(1)} %get-tuple-element.99.rows_ref.pre_in.pre.rest_12_.rest_10_, ...), custom_call_target="tpu_custom_call" | custom-call | flops 1207959552 | tf_op jit(solution)/shard_map/forward/pallas_call | solution.py:602
  33.3 1.4 collective-permute-start.11
  35.8 1.6 %collective-permute-start.15 = (f32[8,128]{1,0:T(8,128)S(1)}, f32[8,128]{1,0:T(8,128)S(1)}, u32[]{:S(2)}, u32[]{:S(2)}) collective-permute-start(f32[8,128]{1,0:T(8,128)S(1)} %fusion.5.rest_0_.rest_8_), channel_id=1, source_target_pairs={{0,7},{1,6},{2,5},{3,4},{4,3},{5,2},{6,1},{7,0},{8,15},{9,14},{10,... | collective-permute-start | bytes 12296 | tf_op jit(solution)/shard_map/ppermute | solution.py:616
  37.4 2.0 %collective-permute-start.14 = (f32[8,128]{1,0:T(8,128)S(1)}, f32[8,128]{1,0:T(8,128)S(1)}, u32[]{:S(2)}, u32[]{:S(2)}) collective-permute-start(f32[8,128]{1,0:T(8,128)S(1)} %fusion.5.rest_0_.rest_8_), channel_id=1, source_target_pairs={{0,5},{1,4},{2,7},{3,6},{4,1},{5,0},{6,3},{7,2},{8,13},{9,12},{10,... | collective-permute-start | bytes 12296 | tf_op jit(solution)/shard_map/ppermute | solution.py:616
  39.5 1.6 %collective-permute-start.13 = (f32[8,128]{1,0:T(8,128)S(1)}, f32[8,128]{1,0:T(8,128)S(1)}, u32[]{:S(2)}, u32[]{:S(2)}) collective-permute-start(f32[8,128]{1,0:T(8,128)S(1)} %fusion.5.rest_0_.rest_8_), channel_id=1, source_target_pairs={{0,3},{1,2},{2,1},{3,0},{4,7},{5,6},{6,5},{7,4},{8,11},{9,10},{10,... | collective-permute-start | bytes 12296 | tf_op jit(solution)/shard_map/ppermute | solution.py:616
  41.1 0.9 slope.4.rest_13_.rest_12_
  42.6 2.9 %forward.6 = (bf16[4,6,256,128]{3,2,1,0:T(8,128)(2,1)S(1)}, f32[4,4,256,128]{3,2,1,0:T(8,128)S(1)}, bf16[1056,128]{1,0:T(8,128)(2,1)S(1)}, f32[8,128]{1,0:T(8,128)S(1)}) custom-call(bf16[4,6,256,128]{3,2,1,0:T(8,128)(2,1)S(1)} %get-tuple-element.95.x_in.x, f32[4,4,256,128]{3,2,1,0:T(8,128)S(1)} %get-tuple-element.105.rows_ref.pre_in.pre.rest_12_.rest_18_, ...), custom_call_target="tpu_custom_call" | custom-call | flops 1207959552 | tf_op jit(solution)/shard_map/forward/pallas_call | solution.py:602
  45.5 1.4 collective-permute-start.16
  46.9 0.9 collective-permute-start.17
  48.1 1.3 collective-permute-start.20
  49.4 2.5 %collective-permute-start.19 = (f32[8,128]{1,0:T(8,128)S(1)}, f32[8,128]{1,0:T(8,128)S(1)}, u32[]{:S(2)}, u32[]{:S(2)}) collective-permute-start(f32[8,128]{1,0:T(8,128)S(1)} %fusion.4.rest_0_.rest_8_), channel_id=1, source_target_pairs={{0,5},{1,4},{2,7},{3,6},{4,1},{5,0},{6,3},{7,2},{8,13},{9,12},{10,... | collective-permute-start | bytes 12296 | tf_op jit(solution)/shard_map/ppermute | solution.py:616
  52.0 1.6 %collective-permute-start.18 = (f32[8,128]{1,0:T(8,128)S(1)}, f32[8,128]{1,0:T(8,128)S(1)}, u32[]{:S(2)}, u32[]{:S(2)}) collective-permute-start(f32[8,128]{1,0:T(8,128)S(1)} %fusion.4.rest_0_.rest_8_), channel_id=1, source_target_pairs={{0,3},{1,2},{2,1},{3,0},{4,7},{5,6},{6,5},{7,4},{8,11},{9,10},{10,... | collective-permute-start | bytes 12296 | tf_op jit(solution)/shard_map/ppermute | solution.py:616
  53.6 0.7 slope.5.rest_13_.rest_21_
  55.0 2.9 %forward.7 = (bf16[4,6,256,128]{3,2,1,0:T(8,128)(2,1)S(1)}, f32[4,4,256,128]{3,2,1,0:T(8,128)S(1)}, bf16[1056,128]{1,0:T(8,128)(2,1)S(1)}, f32[8,128]{1,0:T(8,128)S(1)}) custom-call(bf16[4,6,256,128]{3,2,1,0:T(8,128)(2,1)S(1)} %get-tuple-element.101.x_in.x, f32[4,4,256,128]{3,2,1,0:T(8,128)S(1)} %get-tuple-element.111.rows_ref.pre_in.pre.rest_12_.rest_18_, ...), custom_call_target="tpu_custom_call" | custom-call | flops 1207959552 | tf_op jit(solution)/shard_map/forward/pallas_call | solution.py:602
  57.9 1.4 collective-permute-start.21
  60.5 1.5 %collective-permute-start.24 = (f32[8,128]{1,0:T(8,128)S(1)}, f32[8,128]{1,0:T(8,128)S(1)}, u32[]{:S(2)}, u32[]{:S(2)}) collective-permute-start(f32[8,128]{1,0:T(8,128)S(1)} %fusion.3.rest_0_), channel_id=1, source_target_pairs={{0,7},{1,6},{2,5},{3,4},{4,3},{5,2},{6,1},{7,0},{8,15},{9,14},{10,... | collective-permute-start | bytes 12296 | tf_op jit(solution)/shard_map/ppermute | solution.py:616
  62.0 2.2 %collective-permute-start.23 = (f32[8,128]{1,0:T(8,128)S(1)}, f32[8,128]{1,0:T(8,128)S(1)}, u32[]{:S(2)}, u32[]{:S(2)}) collective-permute-start(f32[8,128]{1,0:T(8,128)S(1)} %fusion.3.rest_0_), channel_id=1, source_target_pairs={{0,5},{1,4},{2,7},{3,6},{4,1},{5,0},{6,3},{7,2},{8,13},{9,12},{10,... | collective-permute-start | bytes 12296 | tf_op jit(solution)/shard_map/ppermute | solution.py:616
  64.2 1.7 %collective-permute-start.22 = (f32[8,128]{1,0:T(8,128)S(1)}, f32[8,128]{1,0:T(8,128)S(1)}, u32[]{:S(2)}, u32[]{:S(2)}) collective-permute-start(f32[8,128]{1,0:T(8,128)S(1)} %fusion.3.rest_0_), channel_id=1, source_target_pairs={{0,3},{1,2},{2,1},{3,0},{4,7},{5,6},{6,5},{7,4},{8,11},{9,10},{10,... | collective-permute-start | bytes 12296 | tf_op jit(solution)/shard_map/ppermute | solution.py:616
  67.3 1.0 turn.1
  68.3 1.4 %collective-permute-start.25 = (f32[8,128]{1,0:T(8,128)S(1)}, f32[8,128]{1,0:T(8,128)S(1)}, u32[]{:S(2)}, u32[]{:S(2)}) collective-permute-start(f32[8,128]{1,0:T(8,128)S(1)} %get-tuple-element.113), channel_id=1, source_target_pairs={{0,1},{1,0},{2,3},{3,2},{4,5},{5,4},{6,7},{7,6},{8,9},{9,8},{10,11... | collective-permute-start | bytes 12296 | tf_op jit(solution)/shard_map/ppermute | solution.py:616
  69.7 0.8 collective-permute-done.25
  70.6 1.3 collective-permute-start.28
  72.4 2.2 %collective-permute-start.26 = (f32[8,128]{1,0:T(8,128)S(1)}, f32[8,128]{1,0:T(8,128)S(1)}, u32[]{:S(2)}, u32[]{:S(2)}) collective-permute-start(f32[8,128]{1,0:T(8,128)S(1)} %add.78.rest_4_), channel_id=1, source_target_pairs={{0,3},{1,2},{2,1},{3,0},{4,7},{5,6},{6,5},{7,4},{8,11},{9,10},{10,... | collective-permute-start | bytes 12296 | tf_op jit(solution)/shard_map/ppermute | solution.py:616
  76.0 3.1 %backward.3 = (bf16[3,3,4,256,256]{4,3,2,1,0:T(8,128)(2,1)S(1)}, bf16[4,4,256,128]{3,2,1,0:T(8,128)(2,1)S(1)}, f32[4,4,256,128]{3,2,1,0:T(8,128)S(1)}, bf16[1056...) custom-call(f32[8,128]{1,0:T(8,128)S(1)} %fusion.3.rest_0_, ...), custom_call_target="tpu_custom_call" | custom-call | flops 1207959552 | tf_op jit(solution)/shard_map/backward/pallas_call | solution.py:602
  80.7 2.1 %collective-permute-start.33 = (f32[8,128]{1,0:T(8,128)S(1)}, f32[8,128]{1,0:T(8,128)S(1)}, u32[]{:S(2)}, u32[]{:S(2)}) collective-permute-start(f32[8,128]{1,0:T(8,128)S(1)} %fusion.2.rest_4_), channel_id=1, source_target_pairs={{0,7},{1,6},{2,5},{3,4},{4,3},{5,2},{6,1},{7,0},{8,15},{9,14},{10,... | collective-permute-start | bytes 12296 | tf_op jit(solution)/shard_map/ppermute | solution.py:616
  82.8 1.7 %collective-permute-start.32 = (f32[8,128]{1,0:T(8,128)S(1)}, f32[8,128]{1,0:T(8,128)S(1)}, u32[]{:S(2)}, u32[]{:S(2)}) collective-permute-start(f32[8,128]{1,0:T(8,128)S(1)} %fusion.2.rest_4_), channel_id=1, source_target_pairs={{0,5},{1,4},{2,7},{3,6},{4,1},{5,0},{6,3},{7,2},{8,13},{9,12},{10,... | collective-permute-start | bytes 12296 | tf_op jit(solution)/shard_map/ppermute | solution.py:616
  84.5 2.6 %collective-permute-start.31 = (f32[8,128]{1,0:T(8,128)S(1)}, f32[8,128]{1,0:T(8,128)S(1)}, u32[]{:S(2)}, u32[]{:S(2)}) collective-permute-start(f32[8,128]{1,0:T(8,128)S(1)} %fusion.2.rest_4_), channel_id=1, source_target_pairs={{0,3},{1,2},{2,1},{3,0},{4,7},{5,6},{6,5},{7,4},{8,11},{9,10},{10,... | collective-permute-start | bytes 12296 | tf_op jit(solution)/shard_map/ppermute | solution.py:616
  87.1 1.9 %weight.6 = (f32[4,144,128]{2,1,0:T(8,128)S(1)}, bf16[4,144,128]{2,1,0:T(8,128)(2,1)S(1)}) custom-call(bf16[4,6,256,128]{3,2,1,0:T(8,128)(2,1)S(1)} %get-tuple-element.107.x, bf16[3,3,4,256,256]{4,3,2,1,0:T(8,128)(2,1)S(1)} %get-tuple-element.119.stack), custom_call_target="tpu_custom_call" | custom-call | flops 1207959552 | tf_op jit(solution)/shard_map/weight/pallas_call | solution.py:602
  89.0 3.0 %backward.4 = (bf16[3,3,4,256,256]{4,3,2,1,0:T(8,128)(2,1)S(1)}, bf16[4,4,256,128]{3,2,1,0:T(8,128)(2,1)S(1)}, f32[4,4,256,128]{3,2,1,0:T(8,128)S(1)}, bf16[1056...) custom-call(f32[8,128]{1,0:T(8,128)S(1)} %fusion.4.rest_0_.rest_8_, ...), custom_call_target="tpu_custom_call" | custom-call | flops 1207959552 | tf_op jit(solution)/shard_map/backward/pallas_call | solution.py:602
  92.2 0.9 collective-permute-start.39
  93.7 1.6 %collective-permute-start.38 = (f32[8,128]{1,0:T(8,128)S(1)}, f32[8,128]{1,0:T(8,128)S(1)}, u32[]{:S(2)}, u32[]{:S(2)}) collective-permute-start(f32[8,128]{1,0:T(8,128)S(1)} %fusion.1.rest_4_), channel_id=1, source_target_pairs={{0,7},{1,6},{2,5},{3,4},{4,3},{5,2},{6,1},{7,0},{8,15},{9,14},{10,... | collective-permute-start | bytes 12296 | tf_op jit(solution)/shard_map/ppermute | solution.py:616
  95.3 2.4 %collective-permute-start.37 = (f32[8,128]{1,0:T(8,128)S(1)}, f32[8,128]{1,0:T(8,128)S(1)}, u32[]{:S(2)}, u32[]{:S(2)}) collective-permute-start(f32[8,128]{1,0:T(8,128)S(1)} %fusion.1.rest_4_), channel_id=1, source_target_pairs={{0,5},{1,4},{2,7},{3,6},{4,1},{5,0},{6,3},{7,2},{8,13},{9,12},{10,... | collective-permute-start | bytes 12296 | tf_op jit(solution)/shard_map/ppermute | solution.py:616
  97.7 2.0 %collective-permute-start.36 = (f32[8,128]{1,0:T(8,128)S(1)}, f32[8,128]{1,0:T(8,128)S(1)}, u32[]{:S(2)}, u32[]{:S(2)}) collective-permute-start(f32[8,128]{1,0:T(8,128)S(1)} %fusion.1.rest_4_), channel_id=1, source_target_pairs={{0,3},{1,2},{2,1},{3,0},{4,7},{5,6},{6,5},{7,4},{8,11},{9,10},{10,... | collective-permute-start | bytes 12296 | tf_op jit(solution)/shard_map/ppermute | solution.py:616
  99.7 1.9 %weight.7 = (f32[4,144,128]{2,1,0:T(8,128)S(1)}, bf16[4,144,128]{2,1,0:T(8,128)(2,1)S(1)}) custom-call(bf16[4,6,256,128]{3,2,1,0:T(8,128)(2,1)S(1)} %get-tuple-element.101.x_in.x, bf16[3,3,4,256,256]{4,3,2,1,0:T(8,128)(2,1)S(1)} %get-tuple-element.127.stack), custom_call_target="tpu_custom_call" | custom-call | flops 1207959552 | tf_op jit(solution)/shard_map/weight/pallas_call | solution.py:602
  101.6 3.0 %backward.5 = (bf16[3,3,4,256,256]{4,3,2,1,0:T(8,128)(2,1)S(1)}, bf16[4,4,256,128]{3,2,1,0:T(8,128)(2,1)S(1)}, f32[4,4,256,128]{3,2,1,0:T(8,128)S(1)}, bf16[1056...) custom-call(f32[8,128]{1,0:T(8,128)S(1)} %fusion.5.rest_0_.rest_8_, ...), custom_call_target="tpu_custom_call" | custom-call | flops 1207959552 | tf_op jit(solution)/shard_map/backward/pallas_call | solution.py:602
  105.3 0.9 collective-permute-done.40.rest_9_
  106.3 1.5 %collective-permute-start.43 = (f32[8,128]{1,0:T(8,128)S(1)}, f32[8,128]{1,0:T(8,128)S(1)}, u32[]{:S(2)}, u32[]{:S(2)}) collective-permute-start(f32[8,128]{1,0:T(8,128)S(1)} %fusion.rest_4_), channel_id=1, source_target_pairs={{0,7},{1,6},{2,5},{3,4},{4,3},{5,2},{6,1},{7,0},{8,15},{9,14},{10,... | collective-permute-start | bytes 12296 | tf_op jit(solution)/shard_map/ppermute | solution.py:616
  107.7 0.9 collective-permute-start.42
  108.6 1.6 %collective-permute-start.41 = (f32[8,128]{1,0:T(8,128)S(1)}, f32[8,128]{1,0:T(8,128)S(1)}, u32[]{:S(2)}, u32[]{:S(2)}) collective-permute-start(f32[8,128]{1,0:T(8,128)S(1)} %fusion.rest_4_), channel_id=1, source_target_pairs={{0,3},{1,2},{2,1},{3,0},{4,7},{5,6},{6,5},{7,4},{8,11},{9,10},{10,... | collective-permute-start | bytes 12296 | tf_op jit(solution)/shard_map/ppermute | solution.py:616
  110.1 1.9 %weight.8 = (f32[4,144,128]{2,1,0:T(8,128)S(1)}, bf16[4,144,128]{2,1,0:T(8,128)(2,1)S(1)}) custom-call(bf16[4,6,256,128]{3,2,1,0:T(8,128)(2,1)S(1)} %get-tuple-element.95.x_in.x, bf16[3,3,4,256,256]{4,3,2,1,0:T(8,128)(2,1)S(1)} %get-tuple-element.135.stack), custom_call_target="tpu_custom_call" | custom-call | flops 1207959552 | tf_op jit(solution)/shard_map/weight/pallas_call | solution.py:602
  112.7 1.9 %collective-permute-start.45 = (bf16[4,144,128]{2,1,0:T(8,128)(2,1)S(1)}, bf16[4,144,128]{2,1,0:T(8,128)(2,1)S(1)}, u32[]{:S(2)}, u32[]{:S(2)}) collective-permute-start(bf16[4,144,128]{2,1,0:T(8,128)(2,1)S(1)} %get-tuple-element.136), channel_id=1, source_target_pairs={{0,1},{1,0},{2,3},{3,2},{4,5},{5,4},{6,7},{7,6},{8,9},{9,8},{10,11... | collective-permute-start | bytes 442376 | tf_op jit(solution)/shard_map/ppermute | solution.py:616
  114.6 2.6 %weight.9 = (bf16[3,3,4,256,256]{4,3,2,1,0:T(8,128)(2,1)S(1)}, f32[4,144,128]{2,1,0:T(8,128)S(1)}, bf16[4,144,128]{2,1,0:T(8,128)(2,1)S(1)}, f32[8,128]{1,0:T(8,128)S(1)}) custom-call(f32[8,128]{1,0:T(8,128)S(1)} %fusion.6.rest_0_.rest_8_, f32[8,128]{1,0:T(8,128)S(1)} %collective-permute-done.8.rest_1_.rest_9_, ...), custom_call_target="tpu_custom_call" | custom-call | flops 1207959552 | tf_op jit(solution)/shard_map/weight/pallas_call | solution.py:602
  117.3 1.3 collective-permute-done.44.refs_4_
  118.8 1.6 %collective-permute-start.49 = (bf16[608,128]{1,0:T(8,128)(2,1)S(1)}, bf16[608,128]{1,0:T(8,128)(2,1)S(1)}, u32[]{:S(2)}, u32[]{:S(2)}) collective-permute-start(bf16[608,128]{1,0:T(8,128)(2,1)S(1)} %get-tuple-element.153), channel_id=1, source_target_pairs={{0,8},{8,0},{16,24},{24,16},{1,9},{9,1},{17,25},{25,17},{2,10},{10... | collective-permute-start | bytes 466952 | tf_op jit(solution)/shard_map/ppermute | solution.py:616
  120.4 1.5 %collective-permute-start.50 = (bf16[608,128]{1,0:T(8,128)(2,1)S(1)}, bf16[608,128]{1,0:T(8,128)(2,1)S(1)}, u32[]{:S(2)}, u32[]{:S(2)}) collective-permute-start(bf16[608,128]{1,0:T(8,128)(2,1)S(1)} %get-tuple-element.155), channel_id=1, source_target_pairs={{0,16},{8,24},{16,0},{24,8},{1,17},{9,25},{17,1},{25,9},{2,18},{10... | collective-permute-start | bytes 466952 | tf_op jit(solution)/shard_map/ppermute | solution.py:616
  122.4 1.5 %neck.1 = bf16[1,4,4,256,128]{4,3,2,1,0:T(8,128)(2,1)} custom-call(bf16[4,6,256,128]{3,2,1,0:T(8,128)(2,1)S(1)} %get-tuple-element.107.x, f32[4,4,256,128]{3,2,1,0:T(8,128)S(1)} %get-tuple-element.149.pre.rows_ref.rest_18_, f32[8,128]{1,0:T(8,128)S(1)} %fusion.3.rest_0_, f32[8,128]{1,0:T(8,128)S(1)} %collective-permute-done.22.rest_1_, ...), custom_call_target="tpu_custom_call" | custom-call | flops 1207959552 | tf_op jit(solution)/shard_map/neck/pallas_call | solution.py:602
  123.9 3.6 %final_grad.1 = bf16[1,4,4,256,128]{4,3,2,1,0:T(8,128)(2,1)} custom-call(f32[8,128]{1,0:T(8,128)S(1)} %fusion.6.rest_0_.rest_8_, f32[8,128]{1,0:T(8,128)S(1)} %collective-permute-done.8.rest_1_.rest_9_, f32[8,128]{1,0:T(8,128)S(1)} %collective-permute-done.9.rest_2_.rest_10_, f32[8,128]{1,0:T(8,128)S(1)} %collective-permute-done.10.rest_3_.rest_11_, ...), custom_call_target="tpu_custom_call" | custom-call | flops 1207959552 | tf_op jit(solution)/shard_map/final_grad/pallas_call | solution.py:602
  127.5 2.0 %collective-permute-done.50.b = bf16[608,128]{1,0:T(8,128)(2,1)S(1)} collective-permute-done((bf16[608,128]{1,0:T(8,128)(2,1)S(1)}, bf16[608,128]{1,0:T(8,128)(2,1)S(1)}, u32[]{:S(2)}, u32[]{:S(2)}) %collective-permute-start.50) | collective-permute-done | bytes 155680 | tf_op jit(solution)/shard_map/ppermute | solution.py:616
  129.6 1.9 %collective-permute-start.52 = (bf16[144,128]{1,0:T(8,128)(2,1)S(1)}, bf16[144,128]{1,0:T(8,128)(2,1)S(1)}, u32[]{:S(2)}, u32[]{:S(2)}) collective-permute-start(bf16[144,128]{1,0:T(8,128)(2,1)S(1)} %get-tuple-element.158), channel_id=1, source_target_pairs={{0,2},{1,3},{2,0},{3,1},{4,6},{5,7},{6,4},{7,5},{8,10},{9,11},{10,... | collective-permute-start | bytes 110600 | tf_op jit(solution)/shard_map/ppermute | solution.py:616
  131.8 2.2 %collective-permute-start.54 = (bf16[144,128]{1,0:T(8,128)(2,1)S(1)}, bf16[144,128]{1,0:T(8,128)(2,1)S(1)}, u32[]{:S(2)}, u32[]{:S(2)}) collective-permute-start(bf16[144,128]{1,0:T(8,128)(2,1)S(1)} %get-tuple-element.160), channel_id=1, source_target_pairs={{0,6},{1,7},{2,4},{3,5},{4,2},{5,3},{6,0},{7,1},{8,14},{9,15},{10,... | collective-permute-start | bytes 110600 | tf_op jit(solution)/shard_map/ppermute | solution.py:616
  134.1 2.3 %collective-permute-done.53.b = bf16[144,128]{1,0:T(8,128)(2,1)S(1)} collective-permute-done((bf16[144,128]{1,0:T(8,128)(2,1)S(1)}, bf16[144,128]{1,0:T(8,128)(2,1)S(1)}, u32[]{:S(2)}, u32[]{:S(2)}) %collective-permute-start.53) | collective-permute-done | bytes 36896 | tf_op jit(solution)/shard_map/ppermute | solution.py:616
  136.4 1.2 collective-permute-done.54.c
  (104 shorter events, 15.5 us)
Async XLA Ops:
  0.6 16.5 %copy-start.3 = (s32[4,4,4,256]{3,2,1,0:T(4,128)S(1)}, s32[4,4,4,256]{3,2,1,0:T(4,128)}, u32[]{:S(2)}) copy-start(s32[4,4,4,256]{3,2,1,0:T(4,128)} %mask.3) | copy-start | bytes 196612
  0.6 16.4 %copy-start.5 = (f32[1,128]{1,0:T(1,128)S(1)}, f32[1,128]{1,0:T(1,128)}, u32[]{:S(2)}) copy-start(f32[1,128]{1,0:T(1,128)} %bias.3) | copy-start | bytes 1540
  0.7 16.4 %copy-start.4 = (f32[1,128]{1,0:T(1,128)S(1)}, f32[1,128]{1,0:T(1,128)}, u32[]{:S(2)}) copy-start(f32[1,128]{1,0:T(1,128)} %gain.3) | copy-start | bytes 1540
  0.7 16.4 %copy-start.1 = (bf16[1,1152,128]{2,1,0:T(8,128)(2,1)S(1)}, bf16[1,1152,128]{2,1,0:T(8,128)(2,1)}, u32[]{:S(2)}) copy-start(bf16[1,1152,128]{2,1,0:T(8,128)(2,1)} %own.1) | copy-start | bytes 884740
  0.7 16.5 %copy-start.2 = (bf16[1,4,4,256,128]{4,3,2,1,0:T(8,128)(2,1)S(1)}, bf16[1,4,4,256,128]{4,3,2,1,0:T(8,128)(2,1)}, u32[]{:S(2)}) copy-start(bf16[1,4,4,256,128]{4,3,2,1,0:T(8,128)(2,1)} %features.3) | copy-start | bytes 3145732
  2.7 11.1 %collective-permute-start = (bf16[2048,128]{1,0:T(8,128)(2,1)S(1)}, bf16[2048,128]{1,0:T(8,128)(2,1)S(1)}, u32[]{:S(2)}, u32[]{:S(2)}) collective-permute-start(bf16[2048,128]{1,0:T(8,128)(2,1)S(1)} %get-tuple-element.85), channel_id=1, source_target_pairs={{0,1},{1,0},{2,3},{3,2},{4,5},{5,4},{6,7},{7,6},{8,9},{9,8},{10,11... | collective-permute-start | bytes 1572872 | tf_op jit(solution)/shard_map/ppermute | solution.py:616
  3.3 10.5 %collective-permute-start.3 = (bf16[608,128]{1,0:T(8,128)(2,1)S(1)}, bf16[608,128]{1,0:T(8,128)(2,1)S(1)}, u32[]{:S(2)}, u32[]{:S(2)}) collective-permute-start(bf16[608,128]{1,0:T(8,128)(2,1)S(1)} %get-tuple-element.87), channel_id=1, source_target_pairs={{0,16},{8,24},{16,0},{24,8},{1,17},{9,25},{17,1},{25,9},{2,18},{10... | collective-permute-start | bytes 466952 | tf_op jit(solution)/shard_map/ppermute | solution.py:616
  5.9 8.0 %collective-permute-start.4 = (bf16[608,128]{1,0:T(8,128)(2,1)S(1)}, bf16[608,128]{1,0:T(8,128)(2,1)S(1)}, u32[]{:S(2)}, u32[]{:S(2)}) collective-permute-start(bf16[608,128]{1,0:T(8,128)(2,1)S(1)} %get-tuple-element.87), channel_id=1, source_target_pairs={{0,24},{8,16},{16,8},{24,0},{1,25},{9,17},{17,9},{25,1},{2,26},{10... | collective-permute-start | bytes 466952 | tf_op jit(solution)/shard_map/ppermute | solution.py:616
  7.3 7.8 %collective-permute-start.2 = (bf16[608,128]{1,0:T(8,128)(2,1)S(1)}, bf16[608,128]{1,0:T(8,128)(2,1)S(1)}, u32[]{:S(2)}, u32[]{:S(2)}) collective-permute-start(bf16[608,128]{1,0:T(8,128)(2,1)S(1)} %get-tuple-element.87), channel_id=1, source_target_pairs={{0,8},{8,0},{16,24},{24,16},{1,9},{9,1},{17,25},{25,17},{2,10},{10... | collective-permute-start | bytes 466952 | tf_op jit(solution)/shard_map/ppermute | solution.py:616
  7.4 9.8 %collective-permute-start.1 = (bf16[2048,128]{1,0:T(8,128)(2,1)S(1)}, bf16[2048,128]{1,0:T(8,128)(2,1)S(1)}, u32[]{:S(2)}, u32[]{:S(2)}) collective-permute-start(bf16[2048,128]{1,0:T(8,128)(2,1)S(1)} %get-tuple-element.86), channel_id=1, source_target_pairs={{1,2},{2,1},{3,4},{4,3},{5,6},{6,5},{9,10},{10,9},{11,12},{12,11},... | collective-permute-start | bytes 1572872 | tf_op jit(solution)/shard_map/ppermute | solution.py:623
  15.1 1.9 %collective-permute-start.5 = (bf16[3,608,128]{2,1,0:T(8,128)(2,1)S(1)}, bf16[3,608,128]{2,1,0:T(8,128)(2,1)S(1)}, u32[]{:S(2)}, u32[]{:S(2)}) collective-permute-start(bf16[3,608,128]{2,1,0:T(8,128)(2,1)S(1)} %pad_maximum_fusion), channel_id=1, source_target_pairs={{0,1},{1,0},{2,3},{3,2},{4,5},{5,4},{6,7},{7,6},{8,9},{9,8},{10,11... | collective-permute-start | bytes 1400840 | tf_op jit(solution)/shard_map/ppermute | solution.py:616
  19.9 2.3 %collective-permute-start.6 = (bf16[1056,128]{1,0:T(8,128)(2,1)S(1)}, bf16[1056,128]{1,0:T(8,128)(2,1)S(1)}, u32[]{:S(2)}, u32[]{:S(2)}) collective-permute-start(bf16[1056,128]{1,0:T(8,128)(2,1)S(1)} %get-tuple-element.92), channel_id=1, source_target_pairs={{0,1},{1,0},{2,3},{3,2},{4,5},{5,4},{6,7},{7,6},{8,9},{9,8},{10,11... | collective-permute-start | bytes 811016 | tf_op jit(solution)/shard_map/ppermute | solution.py:616
  21.0 7.6 %collective-permute-start.7 = (bf16[1024,128]{1,0:T(8,128)(2,1)S(1)}, bf16[1024,128]{1,0:T(8,128)(2,1)S(1)}, u32[]{:S(2)}, u32[]{:S(2)}) collective-permute-start(bf16[1024,128]{1,0:T(8,128)(2,1)S(1)} %far.7), channel_id=1, source_target_pairs={{1,2},{2,1},{3,4},{4,3},{5,6},{6,5},{9,10},{10,9},{11,12},{12,11},... | collective-permute-start | bytes 786440 | tf_op jit(solution)/shard_map/ppermute | solution.py:623
  22.2 6.4 %collective-permute-start.10 = (f32[8,128]{1,0:T(8,128)S(1)}, f32[8,128]{1,0:T(8,128)S(1)}, u32[]{:S(2)}, u32[]{:S(2)}) collective-permute-start(f32[8,128]{1,0:T(8,128)S(1)} %fusion.6.rest_0_.rest_8_), channel_id=1, source_target_pairs={{0,7},{1,6},{2,5},{3,4},{4,3},{5,2},{6,1},{7,0},{8,15},{9,14},{10,... | collective-permute-start | bytes 12296 | tf_op jit(solution)/shard_map/ppermute | solution.py:616
  26.0 4.0 %collective-permute-start.9 = (f32[8,128]{1,0:T(8,128)S(1)}, f32[8,128]{1,0:T(8,128)S(1)}, u32[]{:S(2)}, u32[]{:S(2)}) collective-permute-start(f32[8,128]{1,0:T(8,128)S(1)} %fusion.6.rest_0_.rest_8_), channel_id=1, source_target_pairs={{0,5},{1,4},{2,7},{3,6},{4,1},{5,0},{6,3},{7,2},{8,13},{9,12},{10,... | collective-permute-start | bytes 12296 | tf_op jit(solution)/shard_map/ppermute | solution.py:616
  27.1 3.0 %collective-permute-start.8 = (f32[8,128]{1,0:T(8,128)S(1)}, f32[8,128]{1,0:T(8,128)S(1)}, u32[]{:S(2)}, u32[]{:S(2)}) collective-permute-start(f32[8,128]{1,0:T(8,128)S(1)} %fusion.6.rest_0_.rest_8_), channel_id=1, source_target_pairs={{0,3},{1,2},{2,1},{3,0},{4,7},{5,6},{6,5},{7,4},{8,11},{9,10},{10,... | collective-permute-start | bytes 12296 | tf_op jit(solution)/shard_map/ppermute | solution.py:616
  33.3 2.5 %collective-permute-start.11 = (bf16[1056,128]{1,0:T(8,128)(2,1)S(1)}, bf16[1056,128]{1,0:T(8,128)(2,1)S(1)}, u32[]{:S(2)}, u32[]{:S(2)}) collective-permute-start(bf16[1056,128]{1,0:T(8,128)(2,1)S(1)} %get-tuple-element.97), channel_id=1, source_target_pairs={{0,1},{1,0},{2,3},{3,2},{4,5},{5,4},{6,7},{7,6},{8,9},{9,8},{10,11... | collective-permute-start | bytes 811016 | tf_op jit(solution)/shard_map/ppermute | solution.py:616
  34.6 7.4 %collective-permute-start.12 = (bf16[1024,128]{1,0:T(8,128)(2,1)S(1)}, bf16[1024,128]{1,0:T(8,128)(2,1)S(1)}, u32[]{:S(2)}, u32[]{:S(2)}) collective-permute-start(bf16[1024,128]{1,0:T(8,128)(2,1)S(1)} %far.8), channel_id=1, source_target_pairs={{1,2},{2,1},{3,4},{4,3},{5,6},{6,5},{9,10},{10,9},{11,12},{12,11},... | collective-permute-start | bytes 786440 | tf_op jit(solution)/shard_map/ppermute | solution.py:623
  35.8 6.3 %collective-permute-start.15 = (f32[8,128]{1,0:T(8,128)S(1)}, f32[8,128]{1,0:T(8,128)S(1)}, u32[]{:S(2)}, u32[]{:S(2)}) collective-permute-start(f32[8,128]{1,0:T(8,128)S(1)} %fusion.5.rest_0_.rest_8_), channel_id=1, source_target_pairs={{0,7},{1,6},{2,5},{3,4},{4,3},{5,2},{6,1},{7,0},{8,15},{9,14},{10,... | collective-permute-start | bytes 12296 | tf_op jit(solution)/shard_map/ppermute | solution.py:616
  37.4 4.6 %collective-permute-start.14 = (f32[8,128]{1,0:T(8,128)S(1)}, f32[8,128]{1,0:T(8,128)S(1)}, u32[]{:S(2)}, u32[]{:S(2)}) collective-permute-start(f32[8,128]{1,0:T(8,128)S(1)} %fusion.5.rest_0_.rest_8_), channel_id=1, source_target_pairs={{0,5},{1,4},{2,7},{3,6},{4,1},{5,0},{6,3},{7,2},{8,13},{9,12},{10,... | collective-permute-start | bytes 12296 | tf_op jit(solution)/shard_map/ppermute | solution.py:616
  39.5 3.1 %collective-permute-start.13 = (f32[8,128]{1,0:T(8,128)S(1)}, f32[8,128]{1,0:T(8,128)S(1)}, u32[]{:S(2)}, u32[]{:S(2)}) collective-permute-start(f32[8,128]{1,0:T(8,128)S(1)} %fusion.5.rest_0_.rest_8_), channel_id=1, source_target_pairs={{0,3},{1,2},{2,1},{3,0},{4,7},{5,6},{6,5},{7,4},{8,11},{9,10},{10,... | collective-permute-start | bytes 12296 | tf_op jit(solution)/shard_map/ppermute | solution.py:616
  45.5 2.5 %collective-permute-start.16 = (bf16[1056,128]{1,0:T(8,128)(2,1)S(1)}, bf16[1056,128]{1,0:T(8,128)(2,1)S(1)}, u32[]{:S(2)}, u32[]{:S(2)}) collective-permute-start(bf16[1056,128]{1,0:T(8,128)(2,1)S(1)} %get-tuple-element.103), channel_id=1, source_target_pairs={{0,1},{1,0},{2,3},{3,2},{4,5},{5,4},{6,7},{7,6},{8,9},{9,8},{10,11... | collective-permute-start | bytes 811016 | tf_op jit(solution)/shard_map/ppermute | solution.py:616
  46.9 7.4 %collective-permute-start.17 = (bf16[1024,128]{1,0:T(8,128)(2,1)S(1)}, bf16[1024,128]{1,0:T(8,128)(2,1)S(1)}, u32[]{:S(2)}, u32[]{:S(2)}) collective-permute-start(bf16[1024,128]{1,0:T(8,128)(2,1)S(1)} %far.9), channel_id=1, source_target_pairs={{1,2},{2,1},{3,4},{4,3},{5,6},{6,5},{9,10},{10,9},{11,12},{12,11},... | collective-permute-start | bytes 786440 | tf_op jit(solution)/shard_map/ppermute | solution.py:623
  48.1 6.3 %collective-permute-start.20 = (f32[8,128]{1,0:T(8,128)S(1)}, f32[8,128]{1,0:T(8,128)S(1)}, u32[]{:S(2)}, u32[]{:S(2)}) collective-permute-start(f32[8,128]{1,0:T(8,128)S(1)} %fusion.4.rest_0_.rest_8_), channel_id=1, source_target_pairs={{0,7},{1,6},{2,5},{3,4},{4,3},{5,2},{6,1},{7,0},{8,15},{9,14},{10,... | collective-permute-start | bytes 12296 | tf_op jit(solution)/shard_map/ppermute | solution.py:616
  49.4 4.9 %collective-permute-start.19 = (f32[8,128]{1,0:T(8,128)S(1)}, f32[8,128]{1,0:T(8,128)S(1)}, u32[]{:S(2)}, u32[]{:S(2)}) collective-permute-start(f32[8,128]{1,0:T(8,128)S(1)} %fusion.4.rest_0_.rest_8_), channel_id=1, source_target_pairs={{0,5},{1,4},{2,7},{3,6},{4,1},{5,0},{6,3},{7,2},{8,13},{9,12},{10,... | collective-permute-start | bytes 12296 | tf_op jit(solution)/shard_map/ppermute | solution.py:616
  52.0 3.0 %collective-permute-start.18 = (f32[8,128]{1,0:T(8,128)S(1)}, f32[8,128]{1,0:T(8,128)S(1)}, u32[]{:S(2)}, u32[]{:S(2)}) collective-permute-start(f32[8,128]{1,0:T(8,128)S(1)} %fusion.4.rest_0_.rest_8_), channel_id=1, source_target_pairs={{0,3},{1,2},{2,1},{3,0},{4,7},{5,6},{6,5},{7,4},{8,11},{9,10},{10,... | collective-permute-start | bytes 12296 | tf_op jit(solution)/shard_map/ppermute | solution.py:616
  57.9 2.5 %collective-permute-start.21 = (bf16[1056,128]{1,0:T(8,128)(2,1)S(1)}, bf16[1056,128]{1,0:T(8,128)(2,1)S(1)}, u32[]{:S(2)}, u32[]{:S(2)}) collective-permute-start(bf16[1056,128]{1,0:T(8,128)(2,1)S(1)} %get-tuple-element.110), channel_id=1, source_target_pairs={{0,1},{1,0},{2,3},{3,2},{4,5},{5,4},{6,7},{7,6},{8,9},{9,8},{10,11... | collective-permute-start | bytes 811016 | tf_op jit(solution)/shard_map/ppermute | solution.py:616
  59.3 16.1 %collective-permute-start.29 = (bf16[1024,128]{1,0:T(8,128)(2,1)S(1)}, bf16[1024,128]{1,0:T(8,128)(2,1)S(1)}, u32[]{:S(2)}, u32[]{:S(2)}) collective-permute-start(bf16[1024,128]{1,0:T(8,128)(2,1)S(1)} %far.10), channel_id=1, source_target_pairs={{1,2},{2,1},{3,4},{4,3},{5,6},{6,5},{9,10},{10,9},{11,12},{12,11},... | collective-permute-start | bytes 786440 | tf_op jit(solution)/shard_map/ppermute | solution.py:623
  60.5 6.8 %copy-start = (bf16[1,4,4,256,128]{4,3,2,1,0:T(8,128)(2,1)S(1)}, bf16[1,4,4,256,128]{4,3,2,1,0:T(8,128)(2,1)}, u32[]{:S(2)}) copy-start(bf16[1,4,4,256,128]{4,3,2,1,0:T(8,128)(2,1)} %rest_15_.1) | copy-start | bytes 3145732
  60.5 6.2 %collective-permute-start.24 = (f32[8,128]{1,0:T(8,128)S(1)}, f32[8,128]{1,0:T(8,128)S(1)}, u32[]{:S(2)}, u32[]{:S(2)}) collective-permute-start(f32[8,128]{1,0:T(8,128)S(1)} %fusion.3.rest_0_), channel_id=1, source_target_pairs={{0,7},{1,6},{2,5},{3,4},{4,3},{5,2},{6,1},{7,0},{8,15},{9,14},{10,... | collective-permute-start | bytes 12296 | tf_op jit(solution)/shard_map/ppermute | solution.py:616
  62.0 4.7 %collective-permute-start.23 = (f32[8,128]{1,0:T(8,128)S(1)}, f32[8,128]{1,0:T(8,128)S(1)}, u32[]{:S(2)}, u32[]{:S(2)}) collective-permute-start(f32[8,128]{1,0:T(8,128)S(1)} %fusion.3.rest_0_), channel_id=1, source_target_pairs={{0,5},{1,4},{2,7},{3,6},{4,1},{5,0},{6,3},{7,2},{8,13},{9,12},{10,... | collective-permute-start | bytes 12296 | tf_op jit(solution)/shard_map/ppermute | solution.py:616
  64.2 3.1 %collective-permute-start.22 = (f32[8,128]{1,0:T(8,128)S(1)}, f32[8,128]{1,0:T(8,128)S(1)}, u32[]{:S(2)}, u32[]{:S(2)}) collective-permute-start(f32[8,128]{1,0:T(8,128)S(1)} %fusion.3.rest_0_), channel_id=1, source_target_pairs={{0,3},{1,2},{2,1},{3,0},{4,7},{5,6},{6,5},{7,4},{8,11},{9,10},{10,... | collective-permute-start | bytes 12296 | tf_op jit(solution)/shard_map/ppermute | solution.py:616
  68.3 2.3 %collective-permute-start.25 = (f32[8,128]{1,0:T(8,128)S(1)}, f32[8,128]{1,0:T(8,128)S(1)}, u32[]{:S(2)}, u32[]{:S(2)}) collective-permute-start(f32[8,128]{1,0:T(8,128)S(1)} %get-tuple-element.113), channel_id=1, source_target_pairs={{0,1},{1,0},{2,3},{3,2},{4,5},{5,4},{6,7},{7,6},{8,9},{9,8},{10,11... | collective-permute-start | bytes 12296 | tf_op jit(solution)/shard_map/ppermute | solution.py:616
  70.6 4.8 %collective-permute-start.28 = (f32[8,128]{1,0:T(8,128)S(1)}, f32[8,128]{1,0:T(8,128)S(1)}, u32[]{:S(2)}, u32[]{:S(2)}) collective-permute-start(f32[8,128]{1,0:T(8,128)S(1)} %add.78.rest_4_), channel_id=1, source_target_pairs={{0,7},{1,6},{2,5},{3,4},{4,3},{5,2},{6,1},{7,0},{8,15},{9,14},{10,... | collective-permute-start | bytes 12296 | tf_op jit(solution)/shard_map/ppermute | solution.py:616
  71.9 3.9 %collective-permute-start.27 = (f32[8,128]{1,0:T(8,128)S(1)}, f32[8,128]{1,0:T(8,128)S(1)}, u32[]{:S(2)}, u32[]{:S(2)}) collective-permute-start(f32[8,128]{1,0:T(8,128)S(1)} %add.78.rest_4_), channel_id=1, source_target_pairs={{0,5},{1,4},{2,7},{3,6},{4,1},{5,0},{6,3},{7,2},{8,13},{9,12},{10,... | collective-permute-start | bytes 12296 | tf_op jit(solution)/shard_map/ppermute | solution.py:616
  72.4 3.5 %collective-permute-start.26 = (f32[8,128]{1,0:T(8,128)S(1)}, f32[8,128]{1,0:T(8,128)S(1)}, u32[]{:S(2)}, u32[]{:S(2)}) collective-permute-start(f32[8,128]{1,0:T(8,128)S(1)} %add.78.rest_4_), channel_id=1, source_target_pairs={{0,3},{1,2},{2,1},{3,0},{4,7},{5,6},{6,5},{7,4},{8,11},{9,10},{10,... | collective-permute-start | bytes 12296 | tf_op jit(solution)/shard_map/ppermute | solution.py:616
  79.1 1.6 %collective-permute-start.30 = (bf16[1056,128]{1,0:T(8,128)(2,1)S(1)}, bf16[1056,128]{1,0:T(8,128)(2,1)S(1)}, u32[]{:S(2)}, u32[]{:S(2)}) collective-permute-start(bf16[1056,128]{1,0:T(8,128)(2,1)S(1)} %get-tuple-element.117), channel_id=1, source_target_pairs={{0,1},{1,0},{2,3},{3,2},{4,5},{5,4},{6,7},{7,6},{8,9},{9,8},{10,11... | collective-permute-start | bytes 811016 | tf_op jit(solution)/shard_map/ppermute | solution.py:616
  79.4 9.6 %collective-permute-start.34 = (bf16[1024,128]{1,0:T(8,128)(2,1)S(1)}, bf16[1024,128]{1,0:T(8,128)(2,1)S(1)}, u32[]{:S(2)}, u32[]{:S(2)}) collective-permute-start(bf16[1024,128]{1,0:T(8,128)(2,1)S(1)} %far.11), channel_id=1, source_target_pairs={{1,2},{2,1},{3,4},{4,3},{5,6},{6,5},{9,10},{10,9},{11,12},{12,11},... | collective-permute-start | bytes 786440 | tf_op jit(solution)/shard_map/ppermute | solution.py:623
  80.7 8.3 %collective-permute-start.33 = (f32[8,128]{1,0:T(8,128)S(1)}, f32[8,128]{1,0:T(8,128)S(1)}, u32[]{:S(2)}, u32[]{:S(2)}) collective-permute-start(f32[8,128]{1,0:T(8,128)S(1)} %fusion.2.rest_4_), channel_id=1, source_target_pairs={{0,7},{1,6},{2,5},{3,4},{4,3},{5,2},{6,1},{7,0},{8,15},{9,14},{10,... | collective-permute-start | bytes 12296 | tf_op jit(solution)/shard_map/ppermute | solution.py:616
  82.8 6.2 %collective-permute-start.32 = (f32[8,128]{1,0:T(8,128)S(1)}, f32[8,128]{1,0:T(8,128)S(1)}, u32[]{:S(2)}, u32[]{:S(2)}) collective-permute-start(f32[8,128]{1,0:T(8,128)S(1)} %fusion.2.rest_4_), channel_id=1, source_target_pairs={{0,5},{1,4},{2,7},{3,6},{4,1},{5,0},{6,3},{7,2},{8,13},{9,12},{10,... | collective-permute-start | bytes 12296 | tf_op jit(solution)/shard_map/ppermute | solution.py:616
  84.5 4.5 %collective-permute-start.31 = (f32[8,128]{1,0:T(8,128)S(1)}, f32[8,128]{1,0:T(8,128)S(1)}, u32[]{:S(2)}, u32[]{:S(2)}) collective-permute-start(f32[8,128]{1,0:T(8,128)S(1)} %fusion.2.rest_4_), channel_id=1, source_target_pairs={{0,3},{1,2},{2,1},{3,0},{4,7},{5,6},{6,5},{7,4},{8,11},{9,10},{10,... | collective-permute-start | bytes 12296 | tf_op jit(solution)/shard_map/ppermute | solution.py:616
  92.1 1.6 %collective-permute-start.35 = (bf16[1056,128]{1,0:T(8,128)(2,1)S(1)}, bf16[1056,128]{1,0:T(8,128)(2,1)S(1)}, u32[]{:S(2)}, u32[]{:S(2)}) collective-permute-start(bf16[1056,128]{1,0:T(8,128)(2,1)S(1)} %get-tuple-element.125), channel_id=1, source_target_pairs={{0,1},{1,0},{2,3},{3,2},{4,5},{5,4},{6,7},{7,6},{8,9},{9,8},{10,11... | collective-permute-start | bytes 811016 | tf_op jit(solution)/shard_map/ppermute | solution.py:616
  92.2 9.4 %collective-permute-start.39 = (bf16[1024,128]{1,0:T(8,128)(2,1)S(1)}, bf16[1024,128]{1,0:T(8,128)(2,1)S(1)}, u32[]{:S(2)}, u32[]{:S(2)}) collective-permute-start(bf16[1024,128]{1,0:T(8,128)(2,1)S(1)} %far.12), channel_id=1, source_target_pairs={{1,2},{2,1},{3,4},{4,3},{5,6},{6,5},{9,10},{10,9},{11,12},{12,11},... | collective-permute-start | bytes 786440 | tf_op jit(solution)/shard_map/ppermute | solution.py:623
  93.7 7.9 %collective-permute-start.38 = (f32[8,128]{1,0:T(8,128)S(1)}, f32[8,128]{1,0:T(8,128)S(1)}, u32[]{:S(2)}, u32[]{:S(2)}) collective-permute-start(f32[8,128]{1,0:T(8,128)S(1)} %fusion.1.rest_4_), channel_id=1, source_target_pairs={{0,7},{1,6},{2,5},{3,4},{4,3},{5,2},{6,1},{7,0},{8,15},{9,14},{10,... | collective-permute-start | bytes 12296 | tf_op jit(solution)/shard_map/ppermute | solution.py:616
  95.3 6.3 %collective-permute-start.37 = (f32[8,128]{1,0:T(8,128)S(1)}, f32[8,128]{1,0:T(8,128)S(1)}, u32[]{:S(2)}, u32[]{:S(2)}) collective-permute-start(f32[8,128]{1,0:T(8,128)S(1)} %fusion.1.rest_4_), channel_id=1, source_target_pairs={{0,5},{1,4},{2,7},{3,6},{4,1},{5,0},{6,3},{7,2},{8,13},{9,12},{10,... | collective-permute-start | bytes 12296 | tf_op jit(solution)/shard_map/ppermute | solution.py:616
  97.7 3.9 %collective-permute-start.36 = (f32[8,128]{1,0:T(8,128)S(1)}, f32[8,128]{1,0:T(8,128)S(1)}, u32[]{:S(2)}, u32[]{:S(2)}) collective-permute-start(f32[8,128]{1,0:T(8,128)S(1)} %fusion.1.rest_4_), channel_id=1, source_target_pairs={{0,3},{1,2},{2,1},{3,0},{4,7},{5,6},{6,5},{7,4},{8,11},{9,10},{10,... | collective-permute-start | bytes 12296 | tf_op jit(solution)/shard_map/ppermute | solution.py:616
  104.6 1.6 %collective-permute-start.40 = (bf16[1056,128]{1,0:T(8,128)(2,1)S(1)}, bf16[1056,128]{1,0:T(8,128)(2,1)S(1)}, u32[]{:S(2)}, u32[]{:S(2)}) collective-permute-start(bf16[1056,128]{1,0:T(8,128)(2,1)S(1)} %get-tuple-element.133), channel_id=1, source_target_pairs={{0,1},{1,0},{2,3},{3,2},{4,5},{5,4},{6,7},{7,6},{8,9},{9,8},{10,11... | collective-permute-start | bytes 811016 | tf_op jit(solution)/shard_map/ppermute | solution.py:616
  104.7 12.6 %collective-permute-start.47 = (bf16[4,144,128]{2,1,0:T(8,128)(2,1)S(1)}, bf16[4,144,128]{2,1,0:T(8,128)(2,1)S(1)}, u32[]{:S(2)}, u32[]{:S(2)}) collective-permute-start(bf16[4,144,128]{2,1,0:T(8,128)(2,1)S(1)} %get-tuple-element.120), channel_id=1, source_target_pairs={{0,1},{1,0},{2,3},{3,2},{4,5},{5,4},{6,7},{7,6},{8,9},{9,8},{10,11... | collective-permute-start | bytes 442376 | tf_op jit(solution)/shard_map/ppermute | solution.py:616
  105.2 12.1 %collective-permute-start.46 = (bf16[4,144,128]{2,1,0:T(8,128)(2,1)S(1)}, bf16[4,144,128]{2,1,0:T(8,128)(2,1)S(1)}, u32[]{:S(2)}, u32[]{:S(2)}) collective-permute-start(bf16[4,144,128]{2,1,0:T(8,128)(2,1)S(1)} %get-tuple-element.128), channel_id=1, source_target_pairs={{0,1},{1,0},{2,3},{3,2},{4,5},{5,4},{6,7},{7,6},{8,9},{9,8},{10,11... | collective-permute-start | bytes 442376 | tf_op jit(solution)/shard_map/ppermute | solution.py:616
  106.3 5.7 %collective-permute-start.43 = (f32[8,128]{1,0:T(8,128)S(1)}, f32[8,128]{1,0:T(8,128)S(1)}, u32[]{:S(2)}, u32[]{:S(2)}) collective-permute-start(f32[8,128]{1,0:T(8,128)S(1)} %fusion.rest_4_), channel_id=1, source_target_pairs={{0,7},{1,6},{2,5},{3,4},{4,3},{5,2},{6,1},{7,0},{8,15},{9,14},{10,... | collective-permute-start | bytes 12296 | tf_op jit(solution)/shard_map/ppermute | solution.py:616
  107.7 5.0 %collective-permute-start.42 = (f32[8,128]{1,0:T(8,128)S(1)}, f32[8,128]{1,0:T(8,128)S(1)}, u32[]{:S(2)}, u32[]{:S(2)}) collective-permute-start(f32[8,128]{1,0:T(8,128)S(1)} %fusion.rest_4_), channel_id=1, source_target_pairs={{0,5},{1,4},{2,7},{3,6},{4,1},{5,0},{6,3},{7,2},{8,13},{9,12},{10,... | collective-permute-start | bytes 12296 | tf_op jit(solution)/shard_map/ppermute | solution.py:616
  108.6 6.0 %collective-permute-start.41 = (f32[8,128]{1,0:T(8,128)S(1)}, f32[8,128]{1,0:T(8,128)S(1)}, u32[]{:S(2)}, u32[]{:S(2)}) collective-permute-start(f32[8,128]{1,0:T(8,128)S(1)} %fusion.rest_4_), channel_id=1, source_target_pairs={{0,3},{1,2},{2,1},{3,0},{4,7},{5,6},{6,5},{7,4},{8,11},{9,10},{10,... | collective-permute-start | bytes 12296 | tf_op jit(solution)/shard_map/ppermute | solution.py:616
  112.0 11.9 %collective-permute-start.48 = (bf16[1024,128]{1,0:T(8,128)(2,1)S(1)}, bf16[1024,128]{1,0:T(8,128)(2,1)S(1)}, u32[]{:S(2)}, u32[]{:S(2)}) collective-permute-start(bf16[1024,128]{1,0:T(8,128)(2,1)S(1)} %far.13), channel_id=1, source_target_pairs={{1,2},{2,1},{3,4},{4,3},{5,6},{6,5},{9,10},{10,9},{11,12},{12,11},... | collective-permute-start | bytes 786440 | tf_op jit(solution)/shard_map/ppermute | solution.py:623
  112.7 4.6 %collective-permute-start.45 = (bf16[4,144,128]{2,1,0:T(8,128)(2,1)S(1)}, bf16[4,144,128]{2,1,0:T(8,128)(2,1)S(1)}, u32[]{:S(2)}, u32[]{:S(2)}) collective-permute-start(bf16[4,144,128]{2,1,0:T(8,128)(2,1)S(1)} %get-tuple-element.136), channel_id=1, source_target_pairs={{0,1},{1,0},{2,3},{3,2},{4,5},{5,4},{6,7},{7,6},{8,9},{9,8},{10,11... | collective-permute-start | bytes 442376 | tf_op jit(solution)/shard_map/ppermute | solution.py:616
  117.2 1.4 %collective-permute-start.44 = (bf16[4,144,128]{2,1,0:T(8,128)(2,1)S(1)}, bf16[4,144,128]{2,1,0:T(8,128)(2,1)S(1)}, u32[]{:S(2)}, u32[]{:S(2)}) collective-permute-start(bf16[4,144,128]{2,1,0:T(8,128)(2,1)S(1)} %get-tuple-element.143), channel_id=1, source_target_pairs={{0,1},{1,0},{2,3},{3,2},{4,5},{5,4},{6,7},{7,6},{8,9},{9,8},{10,11... | collective-permute-start | bytes 442376 | tf_op jit(solution)/shard_map/ppermute | solution.py:616
  118.8 8.7 %collective-permute-start.49 = (bf16[608,128]{1,0:T(8,128)(2,1)S(1)}, bf16[608,128]{1,0:T(8,128)(2,1)S(1)}, u32[]{:S(2)}, u32[]{:S(2)}) collective-permute-start(bf16[608,128]{1,0:T(8,128)(2,1)S(1)} %get-tuple-element.153), channel_id=1, source_target_pairs={{0,8},{8,0},{16,24},{24,16},{1,9},{9,1},{17,25},{25,17},{2,10},{10... | collective-permute-start | bytes 466952 | tf_op jit(solution)/shard_map/ppermute | solution.py:616
  120.4 9.1 %collective-permute-start.50 = (bf16[608,128]{1,0:T(8,128)(2,1)S(1)}, bf16[608,128]{1,0:T(8,128)(2,1)S(1)}, u32[]{:S(2)}, u32[]{:S(2)}) collective-permute-start(bf16[608,128]{1,0:T(8,128)(2,1)S(1)} %get-tuple-element.155), channel_id=1, source_target_pairs={{0,16},{8,24},{16,0},{24,8},{1,17},{9,25},{17,1},{25,9},{2,18},{10... | collective-permute-start | bytes 466952 | tf_op jit(solution)/shard_map/ppermute | solution.py:616
  121.9 7.6 %collective-permute-start.51 = (bf16[608,128]{1,0:T(8,128)(2,1)S(1)}, bf16[608,128]{1,0:T(8,128)(2,1)S(1)}, u32[]{:S(2)}, u32[]{:S(2)}) collective-permute-start(bf16[608,128]{1,0:T(8,128)(2,1)S(1)} %get-tuple-element.156), channel_id=1, source_target_pairs={{0,24},{8,16},{16,8},{24,0},{1,25},{9,17},{17,9},{25,1},{2,26},{10... | collective-permute-start | bytes 466952 | tf_op jit(solution)/shard_map/ppermute | solution.py:616
  129.6 4.5 %collective-permute-start.52 = (bf16[144,128]{1,0:T(8,128)(2,1)S(1)}, bf16[144,128]{1,0:T(8,128)(2,1)S(1)}, u32[]{:S(2)}, u32[]{:S(2)}) collective-permute-start(bf16[144,128]{1,0:T(8,128)(2,1)S(1)} %get-tuple-element.158), channel_id=1, source_target_pairs={{0,2},{1,3},{2,0},{3,1},{4,6},{5,7},{6,4},{7,5},{8,10},{9,11},{10,... | collective-permute-start | bytes 110600 | tf_op jit(solution)/shard_map/ppermute | solution.py:616
  131.5 4.9 %collective-permute-start.53 = (bf16[144,128]{1,0:T(8,128)(2,1)S(1)}, bf16[144,128]{1,0:T(8,128)(2,1)S(1)}, u32[]{:S(2)}, u32[]{:S(2)}) collective-permute-start(bf16[144,128]{1,0:T(8,128)(2,1)S(1)} %get-tuple-element.159), channel_id=1, source_target_pairs={{0,4},{1,5},{2,6},{3,7},{4,0},{5,1},{6,2},{7,3},{8,12},{9,13},{10,... | collective-permute-start | bytes 110600 | tf_op jit(solution)/shard_map/ppermute | solution.py:616
  131.8 5.8 %collective-permute-start.54 = (bf16[144,128]{1,0:T(8,128)(2,1)S(1)}, bf16[144,128]{1,0:T(8,128)(2,1)S(1)}, u32[]{:S(2)}, u32[]{:S(2)}) collective-permute-start(bf16[144,128]{1,0:T(8,128)(2,1)S(1)} %get-tuple-element.160), channel_id=1, source_target_pairs={{0,6},{1,7},{2,4},{3,5},{4,2},{5,3},{6,0},{7,1},{8,14},{9,15},{10,... | collective-permute-start | bytes 110600 | tf_op jit(solution)/shard_map/ppermute | solution.py:616

commit v2 on v1

--- a/solution.py
+++ b/solution.py
@@ -645,9 +645,9 @@
     return far
 
 
-def exchange(sums, near, rows_ref):
+def exchange(sums, near, rows_ref=None):
     got = swap(near, "row", 1)
-    far = swap_next(far_rows(rows_ref))
+    far = None if rows_ref is None else swap_next(far_rows(rows_ref))
     parts = got[got.shape[0] - 32 :].astype(f32)
     total = sums + (parts[0:8] + parts[8:16] + parts[16:24])
     return got, far, row_pieces(total), total
@@ -791,7 +791,7 @@
             flops=flops,
             name="backward",
         )
-        g1, g2, grads, total = exchange(sums, near, grad)
+        g1, g2, grads, total = exchange(sums, near, grad if section > 1 else None)
         parts[section] = call(
             weight_kernel,
             part_shapes,
@@ -812,24 +812,28 @@
         name="weight",
     )
 
-    def finish(signal):
-        (feature_grad,) = call(
-            functools.partial(final_grad_kernel, 0, count, last, n),
-            [((1,) + tile_shape, bf16)],
-            (*pieces, *grads, grad, g2, pre, p2, gbs, weights, after(stack, signal)),
-            [outer, blocks],
-            flops=flops,
-            name="final_grad",
-        )
+    def finish_neck(signal):
+        far = swap_next(far_rows(after(grad, signal)))
         last_x, last_pre, _, _, last_pieces, last_count = kept[-1]
         (neck,) = call(
             functools.partial(neck_kernel, last_count, n, sections - 1),
             [((1,) + tile_shape, bf16)],
             (last_x, after(last_pre, signal), *last_pieces, gbs),
+            flops=8 * flops,
+            name="neck",
+        )
+        return neck, far
+
+    def finish_grad(far, signal):
+        (feature_grad,) = call(
+            functools.partial(final_grad_kernel, 0, count, last, n),
+            [((1,) + tile_shape, bf16)],
+            (*pieces, *grads, grad, far, pre, p2, gbs, weights, after(stack, signal)),
+            [outer, blocks],
             flops=flops,
-            name="neck",
-        )
-        return neck, feature_grad
+            name="final_grad",
+        )
+        return feature_grad
 
     m = sections
     if direct:
@@ -843,8 +847,8 @@
             name="chips",
         )
         received = [swap(v, "section", d + 1) for d, v in enumerate(sending)]
-        neck, feature_grad = finish(own)
-        received[0] = after(received[0], (neck, feature_grad))
+        neck, far = finish_neck(own)
+        received[0] = after(received[0], neck)
         mine, one, two, three, total = call(
             section_kernel,
             [((chunk, ch), f32)] + [((chunk, ch), bf16)] * 3 + [(sum_shape, f32)],
@@ -853,6 +857,8 @@
             name="sections",
         )
         chunks = [swap(v, "row", 2 * (k + 1)) for k, v in enumerate((one, two, three))]
+        feature_grad = finish_grad(far, total)
+        mine = after(mine, feature_grad)
         weight_grad, gain_grad, bias_grad = call(
             last_kernel,
             [((1, chunk, ch), f32), ((1, ch), f32), ((1, ch), f32)],
@@ -878,7 +884,8 @@
             chip_sum, "row", scatter_dimension=0, tiled=True, axis_index_groups=lanes
         )
         gain_grad, bias_grad = total[0:1], total[1:2]
-        neck, feature_grad = finish(total)
+        neck, far = finish_neck(total)
+        feature_grad = finish_grad(far, neck)
     return neck, feature_grad, weight_grad, gain_grad, bias_grad
 
 

time: 139 us -> 137 us (0.986)
  transfers between devices with their start and end apart: 55 -> 55, of which waited for: 22 -> 21; matrix products, arithmetic and copies ran while one was open for 0% -> 0% of each run, Pallas kernels for 13% -> 13%
where the time goes in v2:
time: 137 us; the launch traced here: 136 us
  starting transfers between devices  69.9 us (51%)
  Pallas kernels  41.6 us (30%)
  waiting for transfers between devices  23.5 us (17%)
    ppermute x47, starting transfers between devices, swap(): return lax.ppermute(value, axis, [(i, i ^ step) for i in range(count)])  64.1 us
    pallas_call x30, Pallas kernels, call(): pl.pallas_call(body, out_shape=[jax.ShapeDtypeStruct(s, d) for s, d in ou...  41.6 us
    ppermute x47, waiting for transfers between devices, swap(): return lax.ppermute(value, axis, [(i, i ^ step) for i in range(count)])  23.4 us
    ppermute x8, starting transfers between devices, swap_next(): return lax.ppermute(value, 'row', pairs)  5.82 us
  transfers between devices with their start and end apart: 55, of which 21 were waited for; matrix products, arithmetic and copies ran while one was open for 0% of the time, Pallas kernels for 13%

profile of v2, /device:TPU:0, one launch (start us, length us, event | category | flops | bytes accessed | tf_op | source)
XLA Modules:
  0.0 136.2 jit_solution(13025915096857264747)
XLA Ops:
  0.7 2.1 %prep.1 = (bf16[2048,128]{1,0:T(8,128)(2,1)S(1)}, bf16[2048,128]{1,0:T(8,128)(2,1)S(1)}, bf16[608,128]{1,0:T(8,128)(2,1)S(1)}) custom-call(s32[4,4,4,256]{3,2,1,0:T(4,128)} %mask.3, bf16[1,4,4,256,128]{4,3,2,1,0:T(8,128)(2,1)} %features.3, bf16[1,4,4,256,128]{4,3,2,1,0:T(8,128)(2,1)} %rest_15_.1, bf16[1,1152,128]{2,1,0:T(8,128)(2,1)} %own.1, f32[1,128]{1,0:T(1,128)} %gain.3, ...), custom_call_target="tpu_custom_call" | custom-call | tf_op jit(solution)/shard_map/prep/pallas_call | solution.py:602
  3.3 2.6 %collective-permute-start.3 = (bf16[608,128]{1,0:T(8,128)(2,1)S(1)}, bf16[608,128]{1,0:T(8,128)(2,1)S(1)}, u32[]{:S(2)}, u32[]{:S(2)}) collective-permute-start(bf16[608,128]{1,0:T(8,128)(2,1)S(1)} %get-tuple-element.89), channel_id=1, source_target_pairs={{0,16},{8,24},{16,0},{24,8},{1,17},{9,25},{17,1},{25,9},{2,18},{10... | collective-permute-start | bytes 466952 | tf_op jit(solution)/shard_map/ppermute | solution.py:616
  5.9 1.4 %collective-permute-start.4 = (bf16[608,128]{1,0:T(8,128)(2,1)S(1)}, bf16[608,128]{1,0:T(8,128)(2,1)S(1)}, u32[]{:S(2)}, u32[]{:S(2)}) collective-permute-start(bf16[608,128]{1,0:T(8,128)(2,1)S(1)} %get-tuple-element.89), channel_id=1, source_target_pairs={{0,24},{8,16},{16,8},{24,0},{1,25},{9,17},{17,9},{25,1},{2,26},{10... | collective-permute-start | bytes 466952 | tf_op jit(solution)/shard_map/ppermute | solution.py:616
  8.1 5.7 %collective-permute-done.3.r2 = bf16[608,128]{1,0:T(8,128)(2,1)S(1)} collective-permute-done((bf16[608,128]{1,0:T(8,128)(2,1)S(1)}, bf16[608,128]{1,0:T(8,128)(2,1)S(1)}, u32[]{:S(2)}, u32[]{:S(2)}) %collective-permute-start.3) | collective-permute-done | bytes 155680 | tf_op jit(solution)/shard_map/ppermute | solution.py:616
  13.8 1.3 collective-permute-done.2.r1
  15.2 1.8 %collective-permute-done.5.other = bf16[3,608,128]{2,1,0:T(8,128)(2,1)S(1)} collective-permute-done((bf16[3,608,128]{2,1,0:T(8,128)(2,1)S(1)}, bf16[3,608,128]{2,1,0:T(8,128)(2,1)S(1)}, u32[]{:S(2)}, u32[]{:S(2)}) %collective-permute-start.5) | collective-permute-done | bytes 466976 | tf_op jit(solution)/shard_map/ppermute | solution.py:616
  17.2 2.7 %forward.4 = (bf16[4,6,256,128]{3,2,1,0:T(8,128)(2,1)S(1)}, f32[4,4,256,128]{3,2,1,0:T(8,128)S(1)}, bf16[1056,128]{1,0:T(8,128)(2,1)S(1)}, f32[8,128]{1,0:T(8,128)S(1)}) custom-call(s32[4,4,4,256]{3,2,1,0:T(4,128)S(1)} %copy-done.3, bf16[1,4,4,256,128]{4,3,2,1,0:T(8,128)(2,1)S(1)} %copy-done.2, bf16[2048,128]{1,0:T(8,128)(2,1)S(1)} %collective-permute-done.near.rest_16_, ...), custom_call_target="tpu_custom_call" | custom-call | flops 1207959552 | tf_op jit(solution)/shard_map/forward/pallas_call | solution.py:602
  19.9 1.1 collective-permute-start.6
  22.2 3.8 %collective-permute-start.10 = (f32[8,128]{1,0:T(8,128)S(1)}, f32[8,128]{1,0:T(8,128)S(1)}, u32[]{:S(2)}, u32[]{:S(2)}) collective-permute-start(f32[8,128]{1,0:T(8,128)S(1)} %fusion.6.rest_0_.rest_8_), channel_id=1, source_target_pairs={{0,7},{1,6},{2,5},{3,4},{4,3},{5,2},{6,1},{7,0},{8,15},{9,14},{10,... | collective-permute-start | bytes 12296 | tf_op jit(solution)/shard_map/ppermute | solution.py:616
  26.0 1.1 collective-permute-start.9
  27.1 1.5 %collective-permute-start.8 = (f32[8,128]{1,0:T(8,128)S(1)}, f32[8,128]{1,0:T(8,128)S(1)}, u32[]{:S(2)}, u32[]{:S(2)}) collective-permute-start(f32[8,128]{1,0:T(8,128)S(1)} %fusion.6.rest_0_.rest_8_), channel_id=1, source_target_pairs={{0,3},{1,2},{2,1},{3,0},{4,7},{5,6},{6,5},{7,4},{8,11},{9,10},{10,... | collective-permute-start | bytes 12296 | tf_op jit(solution)/shard_map/ppermute | solution.py:616
  28.6 1.4 %collective-permute-done.9.rest_2_.rest_10_ = f32[8,128]{1,0:T(8,128)S(1)} collective-permute-done((f32[8,128]{1,0:T(8,128)S(1)}, f32[8,128]{1,0:T(8,128)S(1)}, u32[]{:S(2)}, u32[]{:S(2)}) %collective-permute-start.9) | collective-permute-done | bytes 4128 | tf_op jit(solution)/shard_map/ppermute | solution.py:616
  30.1 3.1 %forward.5 = (bf16[4,6,256,128]{3,2,1,0:T(8,128)(2,1)S(1)}, f32[4,4,256,128]{3,2,1,0:T(8,128)S(1)}, bf16[1056,128]{1,0:T(8,128)(2,1)S(1)}, f32[8,128]{1,0:T(8,128)S(1)}) custom-call(bf16[4,6,256,128]{3,2,1,0:T(8,128)(2,1)S(1)} %get-tuple-element.92.x_in.rest_14_, f32[4,4,256,128]{3,2,1,0:T(8,128)S(1)} %get-tuple-element.101.rows_ref.pre_in.pre.rest_12_.rest_10_, ...), custom_call_target="tpu_custom_call" | custom-call | flops 1207959552 | tf_op jit(solution)/shard_map/forward/pallas_call | solution.py:602
  33.3 1.4 collective-permute-start.11
  35.8 1.6 %collective-permute-start.15 = (f32[8,128]{1,0:T(8,128)S(1)}, f32[8,128]{1,0:T(8,128)S(1)}, u32[]{:S(2)}, u32[]{:S(2)}) collective-permute-start(f32[8,128]{1,0:T(8,128)S(1)} %fusion.5.rest_0_.rest_8_), channel_id=1, source_target_pairs={{0,7},{1,6},{2,5},{3,4},{4,3},{5,2},{6,1},{7,0},{8,15},{9,14},{10,... | collective-permute-start | bytes 12296 | tf_op jit(solution)/shard_map/ppermute | solution.py:616
  37.5 2.0 %collective-permute-start.14 = (f32[8,128]{1,0:T(8,128)S(1)}, f32[8,128]{1,0:T(8,128)S(1)}, u32[]{:S(2)}, u32[]{:S(2)}) collective-permute-start(f32[8,128]{1,0:T(8,128)S(1)} %fusion.5.rest_0_.rest_8_), channel_id=1, source_target_pairs={{0,5},{1,4},{2,7},{3,6},{4,1},{5,0},{6,3},{7,2},{8,13},{9,12},{10,... | collective-permute-start | bytes 12296 | tf_op jit(solution)/shard_map/ppermute | solution.py:616
  39.5 1.6 %collective-permute-start.13 = (f32[8,128]{1,0:T(8,128)S(1)}, f32[8,128]{1,0:T(8,128)S(1)}, u32[]{:S(2)}, u32[]{:S(2)}) collective-permute-start(f32[8,128]{1,0:T(8,128)S(1)} %fusion.5.rest_0_.rest_8_), channel_id=1, source_target_pairs={{0,3},{1,2},{2,1},{3,0},{4,7},{5,6},{6,5},{7,4},{8,11},{9,10},{10,... | collective-permute-start | bytes 12296 | tf_op jit(solution)/shard_map/ppermute | solution.py:616
  41.1 0.9 slope.4.rest_13_.rest_12_
  42.6 2.9 %forward.6 = (bf16[4,6,256,128]{3,2,1,0:T(8,128)(2,1)S(1)}, f32[4,4,256,128]{3,2,1,0:T(8,128)S(1)}, bf16[1056,128]{1,0:T(8,128)(2,1)S(1)}, f32[8,128]{1,0:T(8,128)S(1)}) custom-call(bf16[4,6,256,128]{3,2,1,0:T(8,128)(2,1)S(1)} %get-tuple-element.97.x_in.x, f32[4,4,256,128]{3,2,1,0:T(8,128)S(1)} %get-tuple-element.107.rows_ref.pre_in.pre.rest_12_.rest_18_, ...), custom_call_target="tpu_custom_call" | custom-call | flops 1207959552 | tf_op jit(solution)/shard_map/forward/pallas_call | solution.py:602
  45.6 1.3 collective-permute-start.16
  46.9 0.9 collective-permute-start.17
  48.1 1.4 collective-permute-start.20
  49.4 2.5 %collective-permute-start.19 = (f32[8,128]{1,0:T(8,128)S(1)}, f32[8,128]{1,0:T(8,128)S(1)}, u32[]{:S(2)}, u32[]{:S(2)}) collective-permute-start(f32[8,128]{1,0:T(8,128)S(1)} %fusion.4.rest_0_.rest_8_), channel_id=1, source_target_pairs={{0,5},{1,4},{2,7},{3,6},{4,1},{5,0},{6,3},{7,2},{8,13},{9,12},{10,... | collective-permute-start | bytes 12296 | tf_op jit(solution)/shard_map/ppermute | solution.py:616
  52.0 1.6 %collective-permute-start.18 = (f32[8,128]{1,0:T(8,128)S(1)}, f32[8,128]{1,0:T(8,128)S(1)}, u32[]{:S(2)}, u32[]{:S(2)}) collective-permute-start(f32[8,128]{1,0:T(8,128)S(1)} %fusion.4.rest_0_.rest_8_), channel_id=1, source_target_pairs={{0,3},{1,2},{2,1},{3,0},{4,7},{5,6},{6,5},{7,4},{8,11},{9,10},{10,... | collective-permute-start | bytes 12296 | tf_op jit(solution)/shard_map/ppermute | solution.py:616
  53.6 0.7 slope.5.rest_13_.rest_21_
  55.0 2.9 %forward.7 = (bf16[4,6,256,128]{3,2,1,0:T(8,128)(2,1)S(1)}, f32[4,4,256,128]{3,2,1,0:T(8,128)S(1)}, bf16[1056,128]{1,0:T(8,128)(2,1)S(1)}, f32[8,128]{1,0:T(8,128)S(1)}) custom-call(bf16[4,6,256,128]{3,2,1,0:T(8,128)(2,1)S(1)} %get-tuple-element.103.x_in.x, f32[4,4,256,128]{3,2,1,0:T(8,128)S(1)} %get-tuple-element.113.rows_ref.pre_in.pre.rest_12_.rest_18_, ...), custom_call_target="tpu_custom_call" | custom-call | flops 1207959552 | tf_op jit(solution)/shard_map/forward/pallas_call | solution.py:602
  57.9 1.4 %collective-permute-start.21 = (bf16[1056,128]{1,0:T(8,128)(2,1)S(1)}, bf16[1056,128]{1,0:T(8,128)(2,1)S(1)}, u32[]{:S(2)}, u32[]{:S(2)}) collective-permute-start(bf16[1056,128]{1,0:T(8,128)(2,1)S(1)} %get-tuple-element.112), channel_id=1, source_target_pairs={{0,1},{1,0},{2,3},{3,2},{4,5},{5,4},{6,7},{7,6},{8,9},{9,8},{10,11... | collective-permute-start | bytes 811016 | tf_op jit(solution)/shard_map/ppermute | solution.py:616
  60.5 1.5 %collective-permute-start.24 = (f32[8,128]{1,0:T(8,128)S(1)}, f32[8,128]{1,0:T(8,128)S(1)}, u32[]{:S(2)}, u32[]{:S(2)}) collective-permute-start(f32[8,128]{1,0:T(8,128)S(1)} %fusion.3.rest_0_), channel_id=1, source_target_pairs={{0,7},{1,6},{2,5},{3,4},{4,3},{5,2},{6,1},{7,0},{8,15},{9,14},{10,... | collective-permute-start | bytes 12296 | tf_op jit(solution)/shard_map/ppermute | solution.py:616
  62.0 2.2 %collective-permute-start.23 = (f32[8,128]{1,0:T(8,128)S(1)}, f32[8,128]{1,0:T(8,128)S(1)}, u32[]{:S(2)}, u32[]{:S(2)}) collective-permute-start(f32[8,128]{1,0:T(8,128)S(1)} %fusion.3.rest_0_), channel_id=1, source_target_pairs={{0,5},{1,4},{2,7},{3,6},{4,1},{5,0},{6,3},{7,2},{8,13},{9,12},{10,... | collective-permute-start | bytes 12296 | tf_op jit(solution)/shard_map/ppermute | solution.py:616
  64.2 1.7 %collective-permute-start.22 = (f32[8,128]{1,0:T(8,128)S(1)}, f32[8,128]{1,0:T(8,128)S(1)}, u32[]{:S(2)}, u32[]{:S(2)}) collective-permute-start(f32[8,128]{1,0:T(8,128)S(1)} %fusion.3.rest_0_), channel_id=1, source_target_pairs={{0,3},{1,2},{2,1},{3,0},{4,7},{5,6},{6,5},{7,4},{8,11},{9,10},{10,... | collective-permute-start | bytes 12296 | tf_op jit(solution)/shard_map/ppermute | solution.py:616
  65.9 0.7 slope.6.rest_13_.rest_21_
  67.3 1.0 turn.1
  68.3 1.4 %collective-permute-start.25 = (f32[8,128]{1,0:T(8,128)S(1)}, f32[8,128]{1,0:T(8,128)S(1)}, u32[]{:S(2)}, u32[]{:S(2)}) collective-permute-start(f32[8,128]{1,0:T(8,128)S(1)} %get-tuple-element.115), channel_id=1, source_target_pairs={{0,1},{1,0},{2,3},{3,2},{4,5},{5,4},{6,7},{7,6},{8,9},{9,8},{10,11... | collective-permute-start | bytes 12296 | tf_op jit(solution)/shard_map/ppermute | solution.py:616
  69.8 0.8 collective-permute-done.25
  70.6 1.3 collective-permute-start.28
  72.4 2.2 %collective-permute-start.26 = (f32[8,128]{1,0:T(8,128)S(1)}, f32[8,128]{1,0:T(8,128)S(1)}, u32[]{:S(2)}, u32[]{:S(2)}) collective-permute-start(f32[8,128]{1,0:T(8,128)S(1)} %add.78.rest_4_), channel_id=1, source_target_pairs={{0,3},{1,2},{2,1},{3,0},{4,7},{5,6},{6,5},{7,4},{8,11},{9,10},{10,... | collective-permute-start | bytes 12296 | tf_op jit(solution)/shard_map/ppermute | solution.py:616
  76.0 3.1 %backward.3 = (bf16[3,3,4,256,256]{4,3,2,1,0:T(8,128)(2,1)S(1)}, bf16[4,4,256,128]{3,2,1,0:T(8,128)(2,1)S(1)}, f32[4,4,256,128]{3,2,1,0:T(8,128)S(1)}, bf16[1056...) custom-call(f32[8,128]{1,0:T(8,128)S(1)} %fusion.3.rest_0_, ...), custom_call_target="tpu_custom_call" | custom-call | flops 1207959552 | tf_op jit(solution)/shard_map/backward/pallas_call | solution.py:602
  80.7 2.1 %collective-permute-start.33 = (f32[8,128]{1,0:T(8,128)S(1)}, f32[8,128]{1,0:T(8,128)S(1)}, u32[]{:S(2)}, u32[]{:S(2)}) collective-permute-start(f32[8,128]{1,0:T(8,128)S(1)} %fusion.2.rest_4_), channel_id=1, source_target_pairs={{0,7},{1,6},{2,5},{3,4},{4,3},{5,2},{6,1},{7,0},{8,15},{9,14},{10,... | collective-permute-start | bytes 12296 | tf_op jit(solution)/shard_map/ppermute | solution.py:616
  82.8 1.7 %collective-permute-start.32 = (f32[8,128]{1,0:T(8,128)S(1)}, f32[8,128]{1,0:T(8,128)S(1)}, u32[]{:S(2)}, u32[]{:S(2)}) collective-permute-start(f32[8,128]{1,0:T(8,128)S(1)} %fusion.2.rest_4_), channel_id=1, source_target_pairs={{0,5},{1,4},{2,7},{3,6},{4,1},{5,0},{6,3},{7,2},{8,13},{9,12},{10,... | collective-permute-start | bytes 12296 | tf_op jit(solution)/shard_map/ppermute | solution.py:616
  84.5 2.6 %collective-permute-start.31 = (f32[8,128]{1,0:T(8,128)S(1)}, f32[8,128]{1,0:T(8,128)S(1)}, u32[]{:S(2)}, u32[]{:S(2)}) collective-permute-start(f32[8,128]{1,0:T(8,128)S(1)} %fusion.2.rest_4_), channel_id=1, source_target_pairs={{0,3},{1,2},{2,1},{3,0},{4,7},{5,6},{6,5},{7,4},{8,11},{9,10},{10,... | collective-permute-start | bytes 12296 | tf_op jit(solution)/shard_map/ppermute | solution.py:616
  87.1 1.9 %weight.6 = (f32[4,144,128]{2,1,0:T(8,128)S(1)}, bf16[4,144,128]{2,1,0:T(8,128)(2,1)S(1)}) custom-call(bf16[4,6,256,128]{3,2,1,0:T(8,128)(2,1)S(1)} %get-tuple-element.109.x, bf16[3,3,4,256,256]{4,3,2,1,0:T(8,128)(2,1)S(1)} %get-tuple-element.121.stack), custom_call_target="tpu_custom_call" | custom-call | flops 1207959552 | tf_op jit(solution)/shard_map/weight/pallas_call | solution.py:602
  89.0 3.0 %backward.4 = (bf16[3,3,4,256,256]{4,3,2,1,0:T(8,128)(2,1)S(1)}, bf16[4,4,256,128]{3,2,1,0:T(8,128)(2,1)S(1)}, f32[4,4,256,128]{3,2,1,0:T(8,128)S(1)}, bf16[1056...) custom-call(f32[8,128]{1,0:T(8,128)S(1)} %fusion.4.rest_0_.rest_8_, ...), custom_call_target="tpu_custom_call" | custom-call | flops 1207959552 | tf_op jit(solution)/shard_map/backward/pallas_call | solution.py:602
  92.1 0.9 collective-permute-start.39
  93.7 1.6 %collective-permute-start.38 = (f32[8,128]{1,0:T(8,128)S(1)}, f32[8,128]{1,0:T(8,128)S(1)}, u32[]{:S(2)}, u32[]{:S(2)}) collective-permute-start(f32[8,128]{1,0:T(8,128)S(1)} %fusion.1.rest_4_), channel_id=1, source_target_pairs={{0,7},{1,6},{2,5},{3,4},{4,3},{5,2},{6,1},{7,0},{8,15},{9,14},{10,... | collective-permute-start | bytes 12296 | tf_op jit(solution)/shard_map/ppermute | solution.py:616
  95.3 2.4 %collective-permute-start.37 = (f32[8,128]{1,0:T(8,128)S(1)}, f32[8,128]{1,0:T(8,128)S(1)}, u32[]{:S(2)}, u32[]{:S(2)}) collective-permute-start(f32[8,128]{1,0:T(8,128)S(1)} %fusion.1.rest_4_), channel_id=1, source_target_pairs={{0,5},{1,4},{2,7},{3,6},{4,1},{5,0},{6,3},{7,2},{8,13},{9,12},{10,... | collective-permute-start | bytes 12296 | tf_op jit(solution)/shard_map/ppermute | solution.py:616
  97.7 2.0 %collective-permute-start.36 = (f32[8,128]{1,0:T(8,128)S(1)}, f32[8,128]{1,0:T(8,128)S(1)}, u32[]{:S(2)}, u32[]{:S(2)}) collective-permute-start(f32[8,128]{1,0:T(8,128)S(1)} %fusion.1.rest_4_), channel_id=1, source_target_pairs={{0,3},{1,2},{2,1},{3,0},{4,7},{5,6},{6,5},{7,4},{8,11},{9,10},{10,... | collective-permute-start | bytes 12296 | tf_op jit(solution)/shard_map/ppermute | solution.py:616
  99.7 1.9 %weight.7 = (f32[4,144,128]{2,1,0:T(8,128)S(1)}, bf16[4,144,128]{2,1,0:T(8,128)(2,1)S(1)}) custom-call(bf16[4,6,256,128]{3,2,1,0:T(8,128)(2,1)S(1)} %get-tuple-element.103.x_in.x, bf16[3,3,4,256,256]{4,3,2,1,0:T(8,128)(2,1)S(1)} %get-tuple-element.129.stack), custom_call_target="tpu_custom_call" | custom-call | flops 1207959552 | tf_op jit(solution)/shard_map/weight/pallas_call | solution.py:602
  101.6 3.0 %backward.5 = (bf16[3,3,4,256,256]{4,3,2,1,0:T(8,128)(2,1)S(1)}, bf16[4,4,256,128]{3,2,1,0:T(8,128)(2,1)S(1)}, f32[4,4,256,128]{3,2,1,0:T(8,128)S(1)}, bf16[1056...) custom-call(f32[8,128]{1,0:T(8,128)S(1)} %fusion.5.rest_0_.rest_8_, ...), custom_call_target="tpu_custom_call" | custom-call | flops 1207959552 | tf_op jit(solution)/shard_map/backward/pallas_call | solution.py:602
  105.3 1.0 collective-permute-done.40.rest_9_
  106.2 1.5 %collective-permute-start.43 = (f32[8,128]{1,0:T(8,128)S(1)}, f32[8,128]{1,0:T(8,128)S(1)}, u32[]{:S(2)}, u32[]{:S(2)}) collective-permute-start(f32[8,128]{1,0:T(8,128)S(1)} %fusion.rest_4_), channel_id=1, source_target_pairs={{0,7},{1,6},{2,5},{3,4},{4,3},{5,2},{6,1},{7,0},{8,15},{9,14},{10,... | collective-permute-start | bytes 12296 | tf_op jit(solution)/shard_map/ppermute | solution.py:616
  107.7 0.9 collective-permute-start.42
  108.6 1.6 %collective-permute-start.41 = (f32[8,128]{1,0:T(8,128)S(1)}, f32[8,128]{1,0:T(8,128)S(1)}, u32[]{:S(2)}, u32[]{:S(2)}) collective-permute-start(f32[8,128]{1,0:T(8,128)S(1)} %fusion.rest_4_), channel_id=1, source_target_pairs={{0,3},{1,2},{2,1},{3,0},{4,7},{5,6},{6,5},{7,4},{8,11},{9,10},{10,... | collective-permute-start | bytes 12296 | tf_op jit(solution)/shard_map/ppermute | solution.py:616
  110.1 1.9 %weight.8 = (f32[4,144,128]{2,1,0:T(8,128)S(1)}, bf16[4,144,128]{2,1,0:T(8,128)(2,1)S(1)}) custom-call(bf16[4,6,256,128]{3,2,1,0:T(8,128)(2,1)S(1)} %get-tuple-element.97.x_in.x, bf16[3,3,4,256,256]{4,3,2,1,0:T(8,128)(2,1)S(1)} %get-tuple-element.137.stack), custom_call_target="tpu_custom_call" | custom-call | flops 1207959552 | tf_op jit(solution)/shard_map/weight/pallas_call | solution.py:602
  112.4 2.6 %weight.9 = (bf16[3,3,4,256,256]{4,3,2,1,0:T(8,128)(2,1)S(1)}, f32[4,144,128]{2,1,0:T(8,128)S(1)}, bf16[4,144,128]{2,1,0:T(8,128)(2,1)S(1)}, f32[8,128]{1,0:T(8,128)S(1)}) custom-call(f32[8,128]{1,0:T(8,128)S(1)} %fusion.6.rest_0_.rest_8_, f32[8,128]{1,0:T(8,128)S(1)} %collective-permute-done.8.rest_1_.rest_9_, ...), custom_call_target="tpu_custom_call" | custom-call | flops 1207959552 | tf_op jit(solution)/shard_map/weight/pallas_call | solution.py:602
  115.3 1.2 collective-permute-done.44.refs_4_
  116.7 1.6 %collective-permute-start.49 = (bf16[608,128]{1,0:T(8,128)(2,1)S(1)}, bf16[608,128]{1,0:T(8,128)(2,1)S(1)}, u32[]{:S(2)}, u32[]{:S(2)}) collective-permute-start(bf16[608,128]{1,0:T(8,128)(2,1)S(1)} %get-tuple-element.155), channel_id=1, source_target_pairs={{0,8},{8,0},{16,24},{24,16},{1,9},{9,1},{17,25},{25,17},{2,10},{10... | collective-permute-start | bytes 466952 | tf_op jit(solution)/shard_map/ppermute | solution.py:616
  118.3 1.5 %collective-permute-start.50 = (bf16[608,128]{1,0:T(8,128)(2,1)S(1)}, bf16[608,128]{1,0:T(8,128)(2,1)S(1)}, u32[]{:S(2)}, u32[]{:S(2)}) collective-permute-start(bf16[608,128]{1,0:T(8,128)(2,1)S(1)} %get-tuple-element.157), channel_id=1, source_target_pairs={{0,16},{8,24},{16,0},{24,8},{1,17},{9,25},{17,1},{25,9},{2,18},{10... | collective-permute-start | bytes 466952 | tf_op jit(solution)/shard_map/ppermute | solution.py:616
  121.0 1.6 %neck.1 = bf16[1,4,4,256,128]{4,3,2,1,0:T(8,128)(2,1)} custom-call(bf16[4,6,256,128]{3,2,1,0:T(8,128)(2,1)S(1)} %get-tuple-element.109.x, f32[4,4,256,128]{3,2,1,0:T(8,128)S(1)} %get-tuple-element.151.pre.rows_ref.rest_18_, f32[8,128]{1,0:T(8,128)S(1)} %fusion.3.rest_0_, f32[8,128]{1,0:T(8,128)S(1)} %collective-permute-done.22.rest_1_, ...), custom_call_target="tpu_custom_call" | custom-call | flops 9663676416 | tf_op jit(solution)/shard_map/neck/pallas_call | solution.py:602
  122.5 1.1 collective-permute-done.49.a
  123.6 3.7 %collective-permute-done.50.b = bf16[608,128]{1,0:T(8,128)(2,1)S(1)} collective-permute-done((bf16[608,128]{1,0:T(8,128)(2,1)S(1)}, bf16[608,128]{1,0:T(8,128)(2,1)S(1)}, u32[]{:S(2)}, u32[]{:S(2)}) %collective-permute-start.50) | collective-permute-done | bytes 155680 | tf_op jit(solution)/shard_map/ppermute | solution.py:616
  127.5 1.0 collective-permute-start.52
  128.5 1.3 collective-permute-start.53
  129.8 2.1 %collective-permute-start.54 = (bf16[144,128]{1,0:T(8,128)(2,1)S(1)}, bf16[144,128]{1,0:T(8,128)(2,1)S(1)}, u32[]{:S(2)}, u32[]{:S(2)}) collective-permute-start(bf16[144,128]{1,0:T(8,128)(2,1)S(1)} %get-tuple-element.165), channel_id=1, source_target_pairs={{0,6},{1,7},{2,4},{3,5},{4,2},{5,3},{6,0},{7,1},{8,14},{9,15},{10,... | collective-permute-start | bytes 110600 | tf_op jit(solution)/shard_map/ppermute | solution.py:616
  131.9 3.6 %final_grad.1 = bf16[1,4,4,256,128]{4,3,2,1,0:T(8,128)(2,1)} custom-call(f32[8,128]{1,0:T(8,128)S(1)} %fusion.6.rest_0_.rest_8_, f32[8,128]{1,0:T(8,128)S(1)} %collective-permute-done.8.rest_1_.rest_9_, f32[8,128]{1,0:T(8,128)S(1)} %collective-permute-done.9.rest_2_.rest_10_, f32[8,128]{1,0:T(8,128)S(1)} %collective-permute-done.10.rest_3_.rest_11_, ...), custom_call_target="tpu_custom_call" | custom-call | flops 1207959552 | tf_op jit(solution)/shard_map/final_grad/pallas_call | solution.py:602
  (104 shorter events, 14.9 us)
Async XLA Ops:
  0.6 16.5 %copy-start.3 = (s32[4,4,4,256]{3,2,1,0:T(4,128)S(1)}, s32[4,4,4,256]{3,2,1,0:T(4,128)}, u32[]{:S(2)}) copy-start(s32[4,4,4,256]{3,2,1,0:T(4,128)} %mask.3) | copy-start | bytes 196612
  0.6 16.4 %copy-start.5 = (f32[1,128]{1,0:T(1,128)S(1)}, f32[1,128]{1,0:T(1,128)}, u32[]{:S(2)}) copy-start(f32[1,128]{1,0:T(1,128)} %bias.3) | copy-start | bytes 1540
  0.7 16.4 %copy-start.4 = (f32[1,128]{1,0:T(1,128)S(1)}, f32[1,128]{1,0:T(1,128)}, u32[]{:S(2)}) copy-start(f32[1,128]{1,0:T(1,128)} %gain.3) | copy-start | bytes 1540
  0.7 16.4 %copy-start.1 = (bf16[1,1152,128]{2,1,0:T(8,128)(2,1)S(1)}, bf16[1,1152,128]{2,1,0:T(8,128)(2,1)}, u32[]{:S(2)}) copy-start(bf16[1,1152,128]{2,1,0:T(8,128)(2,1)} %own.1) | copy-start | bytes 884740
  0.7 16.5 %copy-start.2 = (bf16[1,4,4,256,128]{4,3,2,1,0:T(8,128)(2,1)S(1)}, bf16[1,4,4,256,128]{4,3,2,1,0:T(8,128)(2,1)}, u32[]{:S(2)}) copy-start(bf16[1,4,4,256,128]{4,3,2,1,0:T(8,128)(2,1)} %features.3) | copy-start | bytes 3145732
  2.7 11.1 %collective-permute-start = (bf16[2048,128]{1,0:T(8,128)(2,1)S(1)}, bf16[2048,128]{1,0:T(8,128)(2,1)S(1)}, u32[]{:S(2)}, u32[]{:S(2)}) collective-permute-start(bf16[2048,128]{1,0:T(8,128)(2,1)S(1)} %get-tuple-element.87), channel_id=1, source_target_pairs={{0,1},{1,0},{2,3},{3,2},{4,5},{5,4},{6,7},{7,6},{8,9},{9,8},{10,11... | collective-permute-start | bytes 1572872 | tf_op jit(solution)/shard_map/ppermute | solution.py:616
  3.3 10.5 %collective-permute-start.3 = (bf16[608,128]{1,0:T(8,128)(2,1)S(1)}, bf16[608,128]{1,0:T(8,128)(2,1)S(1)}, u32[]{:S(2)}, u32[]{:S(2)}) collective-permute-start(bf16[608,128]{1,0:T(8,128)(2,1)S(1)} %get-tuple-element.89), channel_id=1, source_target_pairs={{0,16},{8,24},{16,0},{24,8},{1,17},{9,25},{17,1},{25,9},{2,18},{10... | collective-permute-start | bytes 466952 | tf_op jit(solution)/shard_map/ppermute | solution.py:616
  5.9 8.0 %collective-permute-start.4 = (bf16[608,128]{1,0:T(8,128)(2,1)S(1)}, bf16[608,128]{1,0:T(8,128)(2,1)S(1)}, u32[]{:S(2)}, u32[]{:S(2)}) collective-permute-start(bf16[608,128]{1,0:T(8,128)(2,1)S(1)} %get-tuple-element.89), channel_id=1, source_target_pairs={{0,24},{8,16},{16,8},{24,0},{1,25},{9,17},{17,9},{25,1},{2,26},{10... | collective-permute-start | bytes 466952 | tf_op jit(solution)/shard_map/ppermute | solution.py:616
  7.3 7.8 %collective-permute-start.2 = (bf16[608,128]{1,0:T(8,128)(2,1)S(1)}, bf16[608,128]{1,0:T(8,128)(2,1)S(1)}, u32[]{:S(2)}, u32[]{:S(2)}) collective-permute-start(bf16[608,128]{1,0:T(8,128)(2,1)S(1)} %get-tuple-element.89), channel_id=1, source_target_pairs={{0,8},{8,0},{16,24},{24,16},{1,9},{9,1},{17,25},{25,17},{2,10},{10... | collective-permute-start | bytes 466952 | tf_op jit(solution)/shard_map/ppermute | solution.py:616
  7.4 9.8 %collective-permute-start.1 = (bf16[2048,128]{1,0:T(8,128)(2,1)S(1)}, bf16[2048,128]{1,0:T(8,128)(2,1)S(1)}, u32[]{:S(2)}, u32[]{:S(2)}) collective-permute-start(bf16[2048,128]{1,0:T(8,128)(2,1)S(1)} %get-tuple-element.88), channel_id=1, source_target_pairs={{1,2},{2,1},{3,4},{4,3},{5,6},{6,5},{9,10},{10,9},{11,12},{12,11},... | collective-permute-start | bytes 1572872 | tf_op jit(solution)/shard_map/ppermute | solution.py:623
  15.1 1.9 %collective-permute-start.5 = (bf16[3,608,128]{2,1,0:T(8,128)(2,1)S(1)}, bf16[3,608,128]{2,1,0:T(8,128)(2,1)S(1)}, u32[]{:S(2)}, u32[]{:S(2)}) collective-permute-start(bf16[3,608,128]{2,1,0:T(8,128)(2,1)S(1)} %pad_maximum_fusion), channel_id=1, source_target_pairs={{0,1},{1,0},{2,3},{3,2},{4,5},{5,4},{6,7},{7,6},{8,9},{9,8},{10,11... | collective-permute-start | bytes 1400840 | tf_op jit(solution)/shard_map/ppermute | solution.py:616
  19.9 2.3 %collective-permute-start.6 = (bf16[1056,128]{1,0:T(8,128)(2,1)S(1)}, bf16[1056,128]{1,0:T(8,128)(2,1)S(1)}, u32[]{:S(2)}, u32[]{:S(2)}) collective-permute-start(bf16[1056,128]{1,0:T(8,128)(2,1)S(1)} %get-tuple-element.94), channel_id=1, source_target_pairs={{0,1},{1,0},{2,3},{3,2},{4,5},{5,4},{6,7},{7,6},{8,9},{9,8},{10,11... | collective-permute-start | bytes 811016 | tf_op jit(solution)/shard_map/ppermute | solution.py:616
  21.1 7.6 %collective-permute-start.7 = (bf16[1024,128]{1,0:T(8,128)(2,1)S(1)}, bf16[1024,128]{1,0:T(8,128)(2,1)S(1)}, u32[]{:S(2)}, u32[]{:S(2)}) collective-permute-start(bf16[1024,128]{1,0:T(8,128)(2,1)S(1)} %far.7), channel_id=1, source_target_pairs={{1,2},{2,1},{3,4},{4,3},{5,6},{6,5},{9,10},{10,9},{11,12},{12,11},... | collective-permute-start | bytes 786440 | tf_op jit(solution)/shard_map/ppermute | solution.py:623
  22.2 6.4 %collective-permute-start.10 = (f32[8,128]{1,0:T(8,128)S(1)}, f32[8,128]{1,0:T(8,128)S(1)}, u32[]{:S(2)}, u32[]{:S(2)}) collective-permute-start(f32[8,128]{1,0:T(8,128)S(1)} %fusion.6.rest_0_.rest_8_), channel_id=1, source_target_pairs={{0,7},{1,6},{2,5},{3,4},{4,3},{5,2},{6,1},{7,0},{8,15},{9,14},{10,... | collective-permute-start | bytes 12296 | tf_op jit(solution)/shard_map/ppermute | solution.py:616
  26.0 4.0 %collective-permute-start.9 = (f32[8,128]{1,0:T(8,128)S(1)}, f32[8,128]{1,0:T(8,128)S(1)}, u32[]{:S(2)}, u32[]{:S(2)}) collective-permute-start(f32[8,128]{1,0:T(8,128)S(1)} %fusion.6.rest_0_.rest_8_), channel_id=1, source_target_pairs={{0,5},{1,4},{2,7},{3,6},{4,1},{5,0},{6,3},{7,2},{8,13},{9,12},{10,... | collective-permute-start | bytes 12296 | tf_op jit(solution)/shard_map/ppermute | solution.py:616
  27.1 3.0 %collective-permute-start.8 = (f32[8,128]{1,0:T(8,128)S(1)}, f32[8,128]{1,0:T(8,128)S(1)}, u32[]{:S(2)}, u32[]{:S(2)}) collective-permute-start(f32[8,128]{1,0:T(8,128)S(1)} %fusion.6.rest_0_.rest_8_), channel_id=1, source_target_pairs={{0,3},{1,2},{2,1},{3,0},{4,7},{5,6},{6,5},{7,4},{8,11},{9,10},{10,... | collective-permute-start | bytes 12296 | tf_op jit(solution)/shard_map/ppermute | solution.py:616
  33.3 2.5 %collective-permute-start.11 = (bf16[1056,128]{1,0:T(8,128)(2,1)S(1)}, bf16[1056,128]{1,0:T(8,128)(2,1)S(1)}, u32[]{:S(2)}, u32[]{:S(2)}) collective-permute-start(bf16[1056,128]{1,0:T(8,128)(2,1)S(1)} %get-tuple-element.99), channel_id=1, source_target_pairs={{0,1},{1,0},{2,3},{3,2},{4,5},{5,4},{6,7},{7,6},{8,9},{9,8},{10,11... | collective-permute-start | bytes 811016 | tf_op jit(solution)/shard_map/ppermute | solution.py:616
  34.7 7.4 %collective-permute-start.12 = (bf16[1024,128]{1,0:T(8,128)(2,1)S(1)}, bf16[1024,128]{1,0:T(8,128)(2,1)S(1)}, u32[]{:S(2)}, u32[]{:S(2)}) collective-permute-start(bf16[1024,128]{1,0:T(8,128)(2,1)S(1)} %far.8), channel_id=1, source_target_pairs={{1,2},{2,1},{3,4},{4,3},{5,6},{6,5},{9,10},{10,9},{11,12},{12,11},... | collective-permute-start | bytes 786440 | tf_op jit(solution)/shard_map/ppermute | solution.py:623
  35.8 6.3 %collective-permute-start.15 = (f32[8,128]{1,0:T(8,128)S(1)}, f32[8,128]{1,0:T(8,128)S(1)}, u32[]{:S(2)}, u32[]{:S(2)}) collective-permute-start(f32[8,128]{1,0:T(8,128)S(1)} %fusion.5.rest_0_.rest_8_), channel_id=1, source_target_pairs={{0,7},{1,6},{2,5},{3,4},{4,3},{5,2},{6,1},{7,0},{8,15},{9,14},{10,... | collective-permute-start | bytes 12296 | tf_op jit(solution)/shard_map/ppermute | solution.py:616
  37.5 4.6 %collective-permute-start.14 = (f32[8,128]{1,0:T(8,128)S(1)}, f32[8,128]{1,0:T(8,128)S(1)}, u32[]{:S(2)}, u32[]{:S(2)}) collective-permute-start(f32[8,128]{1,0:T(8,128)S(1)} %fusion.5.rest_0_.rest_8_), channel_id=1, source_target_pairs={{0,5},{1,4},{2,7},{3,6},{4,1},{5,0},{6,3},{7,2},{8,13},{9,12},{10,... | collective-permute-start | bytes 12296 | tf_op jit(solution)/shard_map/ppermute | solution.py:616
  39.5 3.1 %collective-permute-start.13 = (f32[8,128]{1,0:T(8,128)S(1)}, f32[8,128]{1,0:T(8,128)S(1)}, u32[]{:S(2)}, u32[]{:S(2)}) collective-permute-start(f32[8,128]{1,0:T(8,128)S(1)} %fusion.5.rest_0_.rest_8_), channel_id=1, source_target_pairs={{0,3},{1,2},{2,1},{3,0},{4,7},{5,6},{6,5},{7,4},{8,11},{9,10},{10,... | collective-permute-start | bytes 12296 | tf_op jit(solution)/shard_map/ppermute | solution.py:616
  45.6 2.5 %collective-permute-start.16 = (bf16[1056,128]{1,0:T(8,128)(2,1)S(1)}, bf16[1056,128]{1,0:T(8,128)(2,1)S(1)}, u32[]{:S(2)}, u32[]{:S(2)}) collective-permute-start(bf16[1056,128]{1,0:T(8,128)(2,1)S(1)} %get-tuple-element.105), channel_id=1, source_target_pairs={{0,1},{1,0},{2,3},{3,2},{4,5},{5,4},{6,7},{7,6},{8,9},{9,8},{10,11... | collective-permute-start | bytes 811016 | tf_op jit(solution)/shard_map/ppermute | solution.py:616
  46.9 7.4 %collective-permute-start.17 = (bf16[1024,128]{1,0:T(8,128)(2,1)S(1)}, bf16[1024,128]{1,0:T(8,128)(2,1)S(1)}, u32[]{:S(2)}, u32[]{:S(2)}) collective-permute-start(bf16[1024,128]{1,0:T(8,128)(2,1)S(1)} %far.9), channel_id=1, source_target_pairs={{1,2},{2,1},{3,4},{4,3},{5,6},{6,5},{9,10},{10,9},{11,12},{12,11},... | collective-permute-start | bytes 786440 | tf_op jit(solution)/shard_map/ppermute | solution.py:623
  48.1 6.3 %collective-permute-start.20 = (f32[8,128]{1,0:T(8,128)S(1)}, f32[8,128]{1,0:T(8,128)S(1)}, u32[]{:S(2)}, u32[]{:S(2)}) collective-permute-start(f32[8,128]{1,0:T(8,128)S(1)} %fusion.4.rest_0_.rest_8_), channel_id=1, source_target_pairs={{0,7},{1,6},{2,5},{3,4},{4,3},{5,2},{6,1},{7,0},{8,15},{9,14},{10,... | collective-permute-start | bytes 12296 | tf_op jit(solution)/shard_map/ppermute | solution.py:616
  49.4 4.9 %collective-permute-start.19 = (f32[8,128]{1,0:T(8,128)S(1)}, f32[8,128]{1,0:T(8,128)S(1)}, u32[]{:S(2)}, u32[]{:S(2)}) collective-permute-start(f32[8,128]{1,0:T(8,128)S(1)} %fusion.4.rest_0_.rest_8_), channel_id=1, source_target_pairs={{0,5},{1,4},{2,7},{3,6},{4,1},{5,0},{6,3},{7,2},{8,13},{9,12},{10,... | collective-permute-start | bytes 12296 | tf_op jit(solution)/shard_map/ppermute | solution.py:616
  52.0 3.0 %collective-permute-start.18 = (f32[8,128]{1,0:T(8,128)S(1)}, f32[8,128]{1,0:T(8,128)S(1)}, u32[]{:S(2)}, u32[]{:S(2)}) collective-permute-start(f32[8,128]{1,0:T(8,128)S(1)} %fusion.4.rest_0_.rest_8_), channel_id=1, source_target_pairs={{0,3},{1,2},{2,1},{3,0},{4,7},{5,6},{6,5},{7,4},{8,11},{9,10},{10,... | collective-permute-start | bytes 12296 | tf_op jit(solution)/shard_map/ppermute | solution.py:616
  57.9 2.5 %collective-permute-start.21 = (bf16[1056,128]{1,0:T(8,128)(2,1)S(1)}, bf16[1056,128]{1,0:T(8,128)(2,1)S(1)}, u32[]{:S(2)}, u32[]{:S(2)}) collective-permute-start(bf16[1056,128]{1,0:T(8,128)(2,1)S(1)} %get-tuple-element.112), channel_id=1, source_target_pairs={{0,1},{1,0},{2,3},{3,2},{4,5},{5,4},{6,7},{7,6},{8,9},{9,8},{10,11... | collective-permute-start | bytes 811016 | tf_op jit(solution)/shard_map/ppermute | solution.py:616
  59.3 16.1 %collective-permute-start.29 = (bf16[1024,128]{1,0:T(8,128)(2,1)S(1)}, bf16[1024,128]{1,0:T(8,128)(2,1)S(1)}, u32[]{:S(2)}, u32[]{:S(2)}) collective-permute-start(bf16[1024,128]{1,0:T(8,128)(2,1)S(1)} %far.10), channel_id=1, source_target_pairs={{1,2},{2,1},{3,4},{4,3},{5,6},{6,5},{9,10},{10,9},{11,12},{12,11},... | collective-permute-start | bytes 786440 | tf_op jit(solution)/shard_map/ppermute | solution.py:623
  60.5 6.8 %copy-start = (bf16[1,4,4,256,128]{4,3,2,1,0:T(8,128)(2,1)S(1)}, bf16[1,4,4,256,128]{4,3,2,1,0:T(8,128)(2,1)}, u32[]{:S(2)}) copy-start(bf16[1,4,4,256,128]{4,3,2,1,0:T(8,128)(2,1)} %rest_15_.1) | copy-start | bytes 3145732
  60.5 6.2 %collective-permute-start.24 = (f32[8,128]{1,0:T(8,128)S(1)}, f32[8,128]{1,0:T(8,128)S(1)}, u32[]{:S(2)}, u32[]{:S(2)}) collective-permute-start(f32[8,128]{1,0:T(8,128)S(1)} %fusion.3.rest_0_), channel_id=1, source_target_pairs={{0,7},{1,6},{2,5},{3,4},{4,3},{5,2},{6,1},{7,0},{8,15},{9,14},{10,... | collective-permute-start | bytes 12296 | tf_op jit(solution)/shard_map/ppermute | solution.py:616
  62.0 4.7 %collective-permute-start.23 = (f32[8,128]{1,0:T(8,128)S(1)}, f32[8,128]{1,0:T(8,128)S(1)}, u32[]{:S(2)}, u32[]{:S(2)}) collective-permute-start(f32[8,128]{1,0:T(8,128)S(1)} %fusion.3.rest_0_), channel_id=1, source_target_pairs={{0,5},{1,4},{2,7},{3,6},{4,1},{5,0},{6,3},{7,2},{8,13},{9,12},{10,... | collective-permute-start | bytes 12296 | tf_op jit(solution)/shard_map/ppermute | solution.py:616
  64.2 3.1 %collective-permute-start.22 = (f32[8,128]{1,0:T(8,128)S(1)}, f32[8,128]{1,0:T(8,128)S(1)}, u32[]{:S(2)}, u32[]{:S(2)}) collective-permute-start(f32[8,128]{1,0:T(8,128)S(1)} %fusion.3.rest_0_), channel_id=1, source_target_pairs={{0,3},{1,2},{2,1},{3,0},{4,7},{5,6},{6,5},{7,4},{8,11},{9,10},{10,... | collective-permute-start | bytes 12296 | tf_op jit(solution)/shard_map/ppermute | solution.py:616
  68.3 2.3 %collective-permute-start.25 = (f32[8,128]{1,0:T(8,128)S(1)}, f32[8,128]{1,0:T(8,128)S(1)}, u32[]{:S(2)}, u32[]{:S(2)}) collective-permute-start(f32[8,128]{1,0:T(8,128)S(1)} %get-tuple-element.115), channel_id=1, source_target_pairs={{0,1},{1,0},{2,3},{3,2},{4,5},{5,4},{6,7},{7,6},{8,9},{9,8},{10,11... | collective-permute-start | bytes 12296 | tf_op jit(solution)/shard_map/ppermute | solution.py:616
  70.6 4.8 %collective-permute-start.28 = (f32[8,128]{1,0:T(8,128)S(1)}, f32[8,128]{1,0:T(8,128)S(1)}, u32[]{:S(2)}, u32[]{:S(2)}) collective-permute-start(f32[8,128]{1,0:T(8,128)S(1)} %add.78.rest_4_), channel_id=1, source_target_pairs={{0,7},{1,6},{2,5},{3,4},{4,3},{5,2},{6,1},{7,0},{8,15},{9,14},{10,... | collective-permute-start | bytes 12296 | tf_op jit(solution)/shard_map/ppermute | solution.py:616
  71.9 3.9 %collective-permute-start.27 = (f32[8,128]{1,0:T(8,128)S(1)}, f32[8,128]{1,0:T(8,128)S(1)}, u32[]{:S(2)}, u32[]{:S(2)}) collective-permute-start(f32[8,128]{1,0:T(8,128)S(1)} %add.78.rest_4_), channel_id=1, source_target_pairs={{0,5},{1,4},{2,7},{3,6},{4,1},{5,0},{6,3},{7,2},{8,13},{9,12},{10,... | collective-permute-start | bytes 12296 | tf_op jit(solution)/shard_map/ppermute | solution.py:616
  72.4 3.5 %collective-permute-start.26 = (f32[8,128]{1,0:T(8,128)S(1)}, f32[8,128]{1,0:T(8,128)S(1)}, u32[]{:S(2)}, u32[]{:S(2)}) collective-permute-start(f32[8,128]{1,0:T(8,128)S(1)} %add.78.rest_4_), channel_id=1, source_target_pairs={{0,3},{1,2},{2,1},{3,0},{4,7},{5,6},{6,5},{7,4},{8,11},{9,10},{10,... | collective-permute-start | bytes 12296 | tf_op jit(solution)/shard_map/ppermute | solution.py:616
  79.1 1.6 %collective-permute-start.30 = (bf16[1056,128]{1,0:T(8,128)(2,1)S(1)}, bf16[1056,128]{1,0:T(8,128)(2,1)S(1)}, u32[]{:S(2)}, u32[]{:S(2)}) collective-permute-start(bf16[1056,128]{1,0:T(8,128)(2,1)S(1)} %get-tuple-element.119), channel_id=1, source_target_pairs={{0,1},{1,0},{2,3},{3,2},{4,5},{5,4},{6,7},{7,6},{8,9},{9,8},{10,11... | collective-permute-start | bytes 811016 | tf_op jit(solution)/shard_map/ppermute | solution.py:616
  79.4 9.6 %collective-permute-start.34 = (bf16[1024,128]{1,0:T(8,128)(2,1)S(1)}, bf16[1024,128]{1,0:T(8,128)(2,1)S(1)}, u32[]{:S(2)}, u32[]{:S(2)}) collective-permute-start(bf16[1024,128]{1,0:T(8,128)(2,1)S(1)} %far.11), channel_id=1, source_target_pairs={{1,2},{2,1},{3,4},{4,3},{5,6},{6,5},{9,10},{10,9},{11,12},{12,11},... | collective-permute-start | bytes 786440 | tf_op jit(solution)/shard_map/ppermute | solution.py:623
  80.7 8.3 %collective-permute-start.33 = (f32[8,128]{1,0:T(8,128)S(1)}, f32[8,128]{1,0:T(8,128)S(1)}, u32[]{:S(2)}, u32[]{:S(2)}) collective-permute-start(f32[8,128]{1,0:T(8,128)S(1)} %fusion.2.rest_4_), channel_id=1, source_target_pairs={{0,7},{1,6},{2,5},{3,4},{4,3},{5,2},{6,1},{7,0},{8,15},{9,14},{10,... | collective-permute-start | bytes 12296 | tf_op jit(solution)/shard_map/ppermute | solution.py:616
  82.8 6.2 %collective-permute-start.32 = (f32[8,128]{1,0:T(8,128)S(1)}, f32[8,128]{1,0:T(8,128)S(1)}, u32[]{:S(2)}, u32[]{:S(2)}) collective-permute-start(f32[8,128]{1,0:T(8,128)S(1)} %fusion.2.rest_4_), channel_id=1, source_target_pairs={{0,5},{1,4},{2,7},{3,6},{4,1},{5,0},{6,3},{7,2},{8,13},{9,12},{10,... | collective-permute-start | bytes 12296 | tf_op jit(solution)/shard_map/ppermute | solution.py:616
  84.5 4.5 %collective-permute-start.31 = (f32[8,128]{1,0:T(8,128)S(1)}, f32[8,128]{1,0:T(8,128)S(1)}, u32[]{:S(2)}, u32[]{:S(2)}) collective-permute-start(f32[8,128]{1,0:T(8,128)S(1)} %fusion.2.rest_4_), channel_id=1, source_target_pairs={{0,3},{1,2},{2,1},{3,0},{4,7},{5,6},{6,5},{7,4},{8,11},{9,10},{10,... | collective-permute-start | bytes 12296 | tf_op jit(solution)/shard_map/ppermute | solution.py:616
  92.0 1.6 %collective-permute-start.35 = (bf16[1056,128]{1,0:T(8,128)(2,1)S(1)}, bf16[1056,128]{1,0:T(8,128)(2,1)S(1)}, u32[]{:S(2)}, u32[]{:S(2)}) collective-permute-start(bf16[1056,128]{1,0:T(8,128)(2,1)S(1)} %get-tuple-element.127), channel_id=1, source_target_pairs={{0,1},{1,0},{2,3},{3,2},{4,5},{5,4},{6,7},{7,6},{8,9},{9,8},{10,11... | collective-permute-start | bytes 811016 | tf_op jit(solution)/shard_map/ppermute | solution.py:616
  92.1 9.4 %collective-permute-start.39 = (bf16[1024,128]{1,0:T(8,128)(2,1)S(1)}, bf16[1024,128]{1,0:T(8,128)(2,1)S(1)}, u32[]{:S(2)}, u32[]{:S(2)}) collective-permute-start(bf16[1024,128]{1,0:T(8,128)(2,1)S(1)} %far.12), channel_id=1, source_target_pairs={{1,2},{2,1},{3,4},{4,3},{5,6},{6,5},{9,10},{10,9},{11,12},{12,11},... | collective-permute-start | bytes 786440 | tf_op jit(solution)/shard_map/ppermute | solution.py:623
  93.7 7.9 %collective-permute-start.38 = (f32[8,128]{1,0:T(8,128)S(1)}, f32[8,128]{1,0:T(8,128)S(1)}, u32[]{:S(2)}, u32[]{:S(2)}) collective-permute-start(f32[8,128]{1,0:T(8,128)S(1)} %fusion.1.rest_4_), channel_id=1, source_target_pairs={{0,7},{1,6},{2,5},{3,4},{4,3},{5,2},{6,1},{7,0},{8,15},{9,14},{10,... | collective-permute-start | bytes 12296 | tf_op jit(solution)/shard_map/ppermute | solution.py:616
  95.3 6.3 %collective-permute-start.37 = (f32[8,128]{1,0:T(8,128)S(1)}, f32[8,128]{1,0:T(8,128)S(1)}, u32[]{:S(2)}, u32[]{:S(2)}) collective-permute-start(f32[8,128]{1,0:T(8,128)S(1)} %fusion.1.rest_4_), channel_id=1, source_target_pairs={{0,5},{1,4},{2,7},{3,6},{4,1},{5,0},{6,3},{7,2},{8,13},{9,12},{10,... | collective-permute-start | bytes 12296 | tf_op jit(solution)/shard_map/ppermute | solution.py:616
  97.7 3.9 %collective-permute-start.36 = (f32[8,128]{1,0:T(8,128)S(1)}, f32[8,128]{1,0:T(8,128)S(1)}, u32[]{:S(2)}, u32[]{:S(2)}) collective-permute-start(f32[8,128]{1,0:T(8,128)S(1)} %fusion.1.rest_4_), channel_id=1, source_target_pairs={{0,3},{1,2},{2,1},{3,0},{4,7},{5,6},{6,5},{7,4},{8,11},{9,10},{10,... | collective-permute-start | bytes 12296 | tf_op jit(solution)/shard_map/ppermute | solution.py:616
  104.6 1.6 %collective-permute-start.40 = (bf16[1056,128]{1,0:T(8,128)(2,1)S(1)}, bf16[1056,128]{1,0:T(8,128)(2,1)S(1)}, u32[]{:S(2)}, u32[]{:S(2)}) collective-permute-start(bf16[1056,128]{1,0:T(8,128)(2,1)S(1)} %get-tuple-element.135), channel_id=1, source_target_pairs={{0,1},{1,0},{2,3},{3,2},{4,5},{5,4},{6,7},{7,6},{8,9},{9,8},{10,11... | collective-permute-start | bytes 811016 | tf_op jit(solution)/shard_map/ppermute | solution.py:616
  104.7 10.6 %collective-permute-start.47 = (bf16[4,144,128]{2,1,0:T(8,128)(2,1)S(1)}, bf16[4,144,128]{2,1,0:T(8,128)(2,1)S(1)}, u32[]{:S(2)}, u32[]{:S(2)}) collective-permute-start(bf16[4,144,128]{2,1,0:T(8,128)(2,1)S(1)} %get-tuple-element.122), channel_id=1, source_target_pairs={{0,1},{1,0},{2,3},{3,2},{4,5},{5,4},{6,7},{7,6},{8,9},{9,8},{10,11... | collective-permute-start | bytes 442376 | tf_op jit(solution)/shard_map/ppermute | solution.py:616
  105.2 10.1 %collective-permute-start.46 = (bf16[4,144,128]{2,1,0:T(8,128)(2,1)S(1)}, bf16[4,144,128]{2,1,0:T(8,128)(2,1)S(1)}, u32[]{:S(2)}, u32[]{:S(2)}) collective-permute-start(bf16[4,144,128]{2,1,0:T(8,128)(2,1)S(1)} %get-tuple-element.130), channel_id=1, source_target_pairs={{0,1},{1,0},{2,3},{3,2},{4,5},{5,4},{6,7},{7,6},{8,9},{9,8},{10,11... | collective-permute-start | bytes 442376 | tf_op jit(solution)/shard_map/ppermute | solution.py:616
  106.2 5.7 %collective-permute-start.43 = (f32[8,128]{1,0:T(8,128)S(1)}, f32[8,128]{1,0:T(8,128)S(1)}, u32[]{:S(2)}, u32[]{:S(2)}) collective-permute-start(f32[8,128]{1,0:T(8,128)S(1)} %fusion.rest_4_), channel_id=1, source_target_pairs={{0,7},{1,6},{2,5},{3,4},{4,3},{5,2},{6,1},{7,0},{8,15},{9,14},{10,... | collective-permute-start | bytes 12296 | tf_op jit(solution)/shard_map/ppermute | solution.py:616
  107.7 4.7 %collective-permute-start.42 = (f32[8,128]{1,0:T(8,128)S(1)}, f32[8,128]{1,0:T(8,128)S(1)}, u32[]{:S(2)}, u32[]{:S(2)}) collective-permute-start(f32[8,128]{1,0:T(8,128)S(1)} %fusion.rest_4_), channel_id=1, source_target_pairs={{0,5},{1,4},{2,7},{3,6},{4,1},{5,0},{6,3},{7,2},{8,13},{9,12},{10,... | collective-permute-start | bytes 12296 | tf_op jit(solution)/shard_map/ppermute | solution.py:616
  108.6 3.9 %collective-permute-start.41 = (f32[8,128]{1,0:T(8,128)S(1)}, f32[8,128]{1,0:T(8,128)S(1)}, u32[]{:S(2)}, u32[]{:S(2)}) collective-permute-start(f32[8,128]{1,0:T(8,128)S(1)} %fusion.rest_4_), channel_id=1, source_target_pairs={{0,3},{1,2},{2,1},{3,0},{4,7},{5,6},{6,5},{7,4},{8,11},{9,10},{10,... | collective-permute-start | bytes 12296 | tf_op jit(solution)/shard_map/ppermute | solution.py:616
  112.0 3.3 %collective-permute-start.45 = (bf16[4,144,128]{2,1,0:T(8,128)(2,1)S(1)}, bf16[4,144,128]{2,1,0:T(8,128)(2,1)S(1)}, u32[]{:S(2)}, u32[]{:S(2)}) collective-permute-start(bf16[4,144,128]{2,1,0:T(8,128)(2,1)S(1)} %get-tuple-element.138), channel_id=1, source_target_pairs={{0,1},{1,0},{2,3},{3,2},{4,5},{5,4},{6,7},{7,6},{8,9},{9,8},{10,11... | collective-permute-start | bytes 442376 | tf_op jit(solution)/shard_map/ppermute | solution.py:616
  115.1 1.4 %collective-permute-start.44 = (bf16[4,144,128]{2,1,0:T(8,128)(2,1)S(1)}, bf16[4,144,128]{2,1,0:T(8,128)(2,1)S(1)}, u32[]{:S(2)}, u32[]{:S(2)}) collective-permute-start(bf16[4,144,128]{2,1,0:T(8,128)(2,1)S(1)} %get-tuple-element.145), channel_id=1, source_target_pairs={{0,1},{1,0},{2,3},{3,2},{4,5},{5,4},{6,7},{7,6},{8,9},{9,8},{10,11... | collective-permute-start | bytes 442376 | tf_op jit(solution)/shard_map/ppermute | solution.py:616
  116.7 6.9 %collective-permute-start.49 = (bf16[608,128]{1,0:T(8,128)(2,1)S(1)}, bf16[608,128]{1,0:T(8,128)(2,1)S(1)}, u32[]{:S(2)}, u32[]{:S(2)}) collective-permute-start(bf16[608,128]{1,0:T(8,128)(2,1)S(1)} %get-tuple-element.155), channel_id=1, source_target_pairs={{0,8},{8,0},{16,24},{24,16},{1,9},{9,1},{17,25},{25,17},{2,10},{10... | collective-permute-start | bytes 466952 | tf_op jit(solution)/shard_map/ppermute | solution.py:616
  118.3 9.1 %collective-permute-start.50 = (bf16[608,128]{1,0:T(8,128)(2,1)S(1)}, bf16[608,128]{1,0:T(8,128)(2,1)S(1)}, u32[]{:S(2)}, u32[]{:S(2)}) collective-permute-start(bf16[608,128]{1,0:T(8,128)(2,1)S(1)} %get-tuple-element.157), channel_id=1, source_target_pairs={{0,16},{8,24},{16,0},{24,8},{1,17},{9,25},{17,1},{25,9},{2,18},{10... | collective-permute-start | bytes 466952 | tf_op jit(solution)/shard_map/ppermute | solution.py:616
  119.8 7.6 %collective-permute-start.51 = (bf16[608,128]{1,0:T(8,128)(2,1)S(1)}, bf16[608,128]{1,0:T(8,128)(2,1)S(1)}, u32[]{:S(2)}, u32[]{:S(2)}) collective-permute-start(bf16[608,128]{1,0:T(8,128)(2,1)S(1)} %get-tuple-element.158), channel_id=1, source_target_pairs={{0,24},{8,16},{16,8},{24,0},{1,25},{9,17},{17,9},{25,1},{2,26},{10... | collective-permute-start | bytes 466952 | tf_op jit(solution)/shard_map/ppermute | solution.py:616
  120.3 11.7 %collective-permute-start.48 = (bf16[1024,128]{1,0:T(8,128)(2,1)S(1)}, bf16[1024,128]{1,0:T(8,128)(2,1)S(1)}, u32[]{:S(2)}, u32[]{:S(2)}) collective-permute-start(bf16[1024,128]{1,0:T(8,128)(2,1)S(1)} %far.13), channel_id=1, source_target_pairs={{1,2},{2,1},{3,4},{4,3},{5,6},{6,5},{9,10},{10,9},{11,12},{12,11},... | collective-permute-start | bytes 786440 | tf_op jit(solution)/shard_map/ppermute | solution.py:623
  127.5 8.1 %collective-permute-start.52 = (bf16[144,128]{1,0:T(8,128)(2,1)S(1)}, bf16[144,128]{1,0:T(8,128)(2,1)S(1)}, u32[]{:S(2)}, u32[]{:S(2)}) collective-permute-start(bf16[144,128]{1,0:T(8,128)(2,1)S(1)} %get-tuple-element.163), channel_id=1, source_target_pairs={{0,2},{1,3},{2,0},{3,1},{4,6},{5,7},{6,4},{7,5},{8,10},{9,11},{10,... | collective-permute-start | bytes 110600 | tf_op jit(solution)/shard_map/ppermute | solution.py:616
  128.5 7.0 %collective-permute-start.53 = (bf16[144,128]{1,0:T(8,128)(2,1)S(1)}, bf16[144,128]{1,0:T(8,128)(2,1)S(1)}, u32[]{:S(2)}, u32[]{:S(2)}) collective-permute-start(bf16[144,128]{1,0:T(8,128)(2,1)S(1)} %get-tuple-element.164), channel_id=1, source_target_pairs={{0,4},{1,5},{2,6},{3,7},{4,0},{5,1},{6,2},{7,3},{8,12},{9,13},{10,... | collective-permute-start | bytes 110600 | tf_op jit(solution)/shard_map/ppermute | solution.py:616
  129.8 5.8 %collective-permute-start.54 = (bf16[144,128]{1,0:T(8,128)(2,1)S(1)}, bf16[144,128]{1,0:T(8,128)(2,1)S(1)}, u32[]{:S(2)}, u32[]{:S(2)}) collective-permute-start(bf16[144,128]{1,0:T(8,128)(2,1)S(1)} %get-tuple-element.165), channel_id=1, source_target_pairs={{0,6},{1,7},{2,4},{3,5},{4,2},{5,3},{6,0},{7,1},{8,14},{9,15},{10,... | collective-permute-start | bytes 110600 | tf_op jit(solution)/shard_map/ppermute | solution.py:616

commit v3 on v2

--- a/solution.py
+++ b/solution.py
@@ -167,7 +167,7 @@
     return jnp.concatenate(parts, axis=0)
 
 
-def prep_kernel(mask, features, cot, weight, gain, bias, near, far, out, held, rows_mask, both, sems):
+def prep_kernel(mask, features, cot, weight, gain, bias, near, far, far_cot, out, held, rows_mask, both, sems):
     place = Place()
     scenes, rows, cols, ch = features.shape[1:]
     half = weight.shape[1] // 2
@@ -200,10 +200,11 @@
         for n, edge in enumerate((near, far)):
             at = 2 * s + n
             edge[here, :] = (held[n, s].astype(f32) * columns[:, at : at + 1]).astype(bf16)
-            edge[there, :] = held[2 + n, s]
-
-
-def gather_kernel(own, gain, bias, r1, r2, r3, other, weights, gbs):
+        near[there, :] = held[2, s]
+        far_cot[here, :] = held[3, s]
+
+
+def gather_kernel(own, gain, bias, r1, r2, r3, o1, o2, o3, weights, gbs):
     place = Place()
     taps, ch = own.shape[1:]
     piece = taps // 6
@@ -215,20 +216,23 @@
     for p in range(6):
         put(place.section, p, own[0, p * piece : (p + 1) * piece])
     gbs[place.section] = jnp.concatenate([gain[...], bias[...], jnp.zeros((6, ch), f32)], axis=0)
-    for d, got in ((1, r1), (2, r2), (3, r3)):
+    for d, got, other in ((1, r1, o1), (2, r2, o2), (3, r3, o3)):
         there = place.section ^ d
         for n in range(3):
             rows = slice(n * piece, (n + 1) * piece)
             put(there, 3 * place.core + n, got[rows])
-            put(there, 3 * (1 - place.core) + n, other[d - 1, rows])
+            put(there, 3 * (1 - place.core) + n, other[rows])
         parts = got[3 * piece :].astype(f32)
         gbs[there] = parts[0:8] + parts[8:16] + parts[16:24]
 
 
-def far_kernel(rows_ref, far):
+def far_kernel(rows_ref, *rest):
+    *more, far = rest
     scenes, rows, cols, ch = rows_ref.shape
     for s in range(scenes):
         far[s * cols : (s + 1) * cols, :] = rows_ref[s, rows - 1].astype(bf16)
+    if more:
+        far[scenes * cols :, :] = more[0][...]
 
 
 def finish_forward(stack, blocks, pre, near, sums, make_rows, columns, third):
@@ -416,7 +420,7 @@
 
 
 def back_outer_row(section, count, last, terms, g2, p2, pieces, gbs, cols):
-    base = p2.shape[0] if last else 0
+    base = p2.shape[0] // 2 if last else 0
     scale, offset = stat_affine(pieces, count, gbs[section])
     inside = Place().inside
 
@@ -639,9 +643,10 @@
     return lax.optimization_barrier((value, signal))[0]
 
 
-def far_rows(rows_ref):
+def far_rows(rows_ref, *more):
     scenes, _, cols, ch = rows_ref.shape
-    (far,) = call(far_kernel, [((scenes * cols, ch), bf16)], (rows_ref,), name="far")
+    size = scenes * cols * (1 + len(more))
+    (far,) = call(far_kernel, [((size, ch), bf16)], (rows_ref, *more), name="far")
     return far
 
 
@@ -676,9 +681,9 @@
     def in_hbm(*values):
         return [pltpu.with_memory_space_constraint(v, pltpu.HBM) for v in values]
 
-    e1, e2, wsend = call(
+    e1, e2, cot_far, wsend = call(
         prep_kernel,
-        [((2 * edge, ch), bf16), ((2 * edge, ch), bf16), ((half + 32, ch), bf16)],
+        [((2 * edge, ch), bf16), ((edge, ch), bf16), ((edge, ch), bf16), ((half + 32, ch), bf16)],
         in_hbm(valid_mask, features, out_cotangent, conv_weight, norm_gain, norm_bias),
         [
             pltpu.VMEM((4, scenes, cols, ch), bf16),
@@ -693,11 +698,11 @@
     e1 = swap(e1, "row", 1)
     e2 = swap_next(e2)
     got[1] = after(got[1], e1)
-    other = swap(jnp.stack(got), "row", 1)
+    others = [swap(v, "row", 1) for v in got]
     weights, gbs = call(
         gather_kernel,
         [((sections, taps, ch), bf16), ((sections, 8, ch), f32)],
-        (conv_weight, norm_gain, norm_bias, *got, other),
+        (conv_weight, norm_gain, norm_bias, *got, *others),
         name="gather",
     )
 
@@ -715,13 +720,17 @@
     )
     for section in range(sections):
         count = None if section == 0 else cells
-        near, far, pieces, total = exchange(sums, near, pre)
+        last = section == sections - 1
+        near, far, pieces, total = exchange(sums, near, None if last else pre)
+        if last:
+            far = swap_next(far_rows(after(pre, total), cot_far))
         if section > 0:
             _, below, below_near, _, below_pieces, below_count = kept[-1]
             slopes += call(
                 functools.partial(slope_kernel, section - 1, below_count, len(pieces)),
                 [(slope_shape, f32)],
                 (after(below, total), below_near, *below_pieces, gbs),
+                flops=8 * flops if last else 0,
                 name="slope",
             )
             pieces[0] = after(pieces[0], slopes[-1])
@@ -751,7 +760,7 @@
         (after(pre, total), near, *pieces, gbs),
         name="slope",
     )
-    grad, g1, g2 = out_cotangent, e1, e2
+    grad, g1, g2 = out_cotangent, e1, far
     parts = [None] * sections
     totals = [None] * sections
     part_shapes = [((tiles // 2, chunk, ch), f32), ((tiles // 2, chunk, ch), bf16)]

time: 137 us -> 135 us (0.985)
  starting transfers between devices: 69.9 us -> 68.4 us
    ppermute x47 -> x49, starting transfers between devices: 64.1 us -> 62.5 us  [swap(): return lax.ppermute(value, axis, [(i, i ^ step) for i in range(count)])]
    ppermute x47 -> x49, waiting for transfers between devices: 23.4 us -> 23.2 us  [swap(): return lax.ppermute(value, axis, [(i, i ^ step) for i in range(count)])]
  transfers between devices with their start and end apart: 55 -> 57, of which waited for: 21 -> 22; matrix products, arithmetic and copies ran while one was open for 0% -> 0% of each run, Pallas kernels for 13% -> 13%
where the time goes in v3:
time: 135 us
  starting transfers between devices  68.4 us (51%)
  Pallas kernels  41.7 us (31%)
  waiting for transfers between devices  23.2 us (17%)
    ppermute x49, starting transfers between devices, swap(): return lax.ppermute(value, axis, [(i, i ^ step) for i in range(count)])  62.5 us
    pallas_call x30, Pallas kernels, call(): pl.pallas_call(body, out_shape=[jax.ShapeDtypeStruct(s, d) for s, d in ou...  41.7 us
    ppermute x49, waiting for transfers between devices, swap(): return lax.ppermute(value, axis, [(i, i ^ step) for i in range(count)])  23.2 us
    ppermute x8, starting transfers between devices, swap_next(): return lax.ppermute(value, 'row', pairs)  5.96 us
  transfers between devices with their start and end apart: 57, of which 22 were waited for; matrix products, arithmetic and copies ran while one was open for 0% of the time, Pallas kernels for 13%

profile of v3, /device:TPU:0, one launch (start us, length us, event | category | flops | bytes accessed | tf_op | source)
XLA Modules:
  0.0 134.6 jit_solution(9462808984145610314)
XLA Ops:
  0.7 2.1 %prep.1 = (bf16[2048,128]{1,0:T(8,128)(2,1)S(1)}, bf16[1024,128]{1,0:T(8,128)(2,1)S(1)}, bf16[1024,128]{1,0:T(8,128)(2,1)S(1)}, bf16[608,128]{1,0:T(8,128)(2,1)S(1)}) custom-call(s32[4,4,4,256]{3,2,1,0:T(4,128)} %mask.3, bf16[1,4,4,256,128]{4,3,2,1,0:T(8,128)(2,1)} %features.3, bf16[1,4,4,256,128]{4,3,2,1,0:T(8,128)(2,1)} %rest_15_.1, ...), custom_call_target="tpu_custom_call" | custom-call | tf_op jit(solution)/shard_map/prep/pallas_call | solution.py:606
  3.3 3.5 %collective-permute-start.4 = (bf16[608,128]{1,0:T(8,128)(2,1)S(1)}, bf16[608,128]{1,0:T(8,128)(2,1)S(1)}, u32[]{:S(2)}, u32[]{:S(2)}) collective-permute-start(bf16[608,128]{1,0:T(8,128)(2,1)S(1)} %get-tuple-element.91), channel_id=1, source_target_pairs={{0,24},{8,16},{16,8},{24,0},{1,25},{9,17},{17,9},{25,1},{2,26},{10... | collective-permute-start | bytes 466952 | tf_op jit(solution)/shard_map/ppermute | solution.py:620
  8.1 3.6 %collective-permute-done.4.r3 = bf16[608,128]{1,0:T(8,128)(2,1)S(1)} collective-permute-done((bf16[608,128]{1,0:T(8,128)(2,1)S(1)}, bf16[608,128]{1,0:T(8,128)(2,1)S(1)}, u32[]{:S(2)}, u32[]{:S(2)}) %collective-permute-start.4) | collective-permute-done | bytes 155680 | tf_op jit(solution)/shard_map/ppermute | solution.py:620
  11.7 3.4 %collective-permute-done.2.r1 = bf16[608,128]{1,0:T(8,128)(2,1)S(1)} collective-permute-done((bf16[608,128]{1,0:T(8,128)(2,1)S(1)}, bf16[608,128]{1,0:T(8,128)(2,1)S(1)}, u32[]{:S(2)}, u32[]{:S(2)}) %collective-permute-start.2) | collective-permute-done | bytes 155680 | tf_op jit(solution)/shard_map/ppermute | solution.py:620
  15.6 0.9 collective-permute-done.5.o1
  16.8 2.7 %forward.4 = (bf16[4,6,256,128]{3,2,1,0:T(8,128)(2,1)S(1)}, f32[4,4,256,128]{3,2,1,0:T(8,128)S(1)}, bf16[1056,128]{1,0:T(8,128)(2,1)S(1)}, f32[8,128]{1,0:T(8,128)S(1)}) custom-call(s32[4,4,4,256]{3,2,1,0:T(4,128)S(1)} %copy-done.3, bf16[1,4,4,256,128]{4,3,2,1,0:T(8,128)(2,1)S(1)} %copy-done.2, bf16[2048,128]{1,0:T(8,128)(2,1)S(1)} %collective-permute-done.near.rest_16_, ...), custom_call_target="tpu_custom_call" | custom-call | flops 1207959552 | tf_op jit(solution)/shard_map/forward/pallas_call | solution.py:606
  21.1 3.5 %collective-permute-start.12 = (f32[8,128]{1,0:T(8,128)S(1)}, f32[8,128]{1,0:T(8,128)S(1)}, u32[]{:S(2)}, u32[]{:S(2)}) collective-permute-start(f32[8,128]{1,0:T(8,128)S(1)} %fusion.6.rest_0_.rest_8_), channel_id=1, source_target_pairs={{0,7},{1,6},{2,5},{3,4},{4,3},{5,2},{6,1},{7,0},{8,15},{9,14},{10,... | collective-permute-start | bytes 12296 | tf_op jit(solution)/shard_map/ppermute | solution.py:620
  24.6 1.2 collective-permute-start.11
  25.9 1.4 %collective-permute-start.10 = (f32[8,128]{1,0:T(8,128)S(1)}, f32[8,128]{1,0:T(8,128)S(1)}, u32[]{:S(2)}, u32[]{:S(2)}) collective-permute-start(f32[8,128]{1,0:T(8,128)S(1)} %fusion.6.rest_0_.rest_8_), channel_id=1, source_target_pairs={{0,3},{1,2},{2,1},{3,0},{4,7},{5,6},{6,5},{7,4},{8,11},{9,10},{10,... | collective-permute-start | bytes 12296 | tf_op jit(solution)/shard_map/ppermute | solution.py:620
  27.3 1.3 collective-permute-done.11.rest_2_.rest_10_
  28.9 3.1 %forward.5 = (bf16[4,6,256,128]{3,2,1,0:T(8,128)(2,1)S(1)}, f32[4,4,256,128]{3,2,1,0:T(8,128)S(1)}, bf16[1056,128]{1,0:T(8,128)(2,1)S(1)}, f32[8,128]{1,0:T(8,128)S(1)}) custom-call(bf16[4,6,256,128]{3,2,1,0:T(8,128)(2,1)S(1)} %get-tuple-element.94.x_in.rest_14_, f32[4,4,256,128]{3,2,1,0:T(8,128)S(1)} %get-tuple-element.103.rows_ref.pre_in.pre.rest_12_.rest_10_, ...), custom_call_target="tpu_custom_call" | custom-call | flops 1207959552 | tf_op jit(solution)/shard_map/forward/pallas_call | solution.py:606
  32.0 1.1 collective-permute-start.13
  34.3 1.9 %collective-permute-start.17 = (f32[8,128]{1,0:T(8,128)S(1)}, f32[8,128]{1,0:T(8,128)S(1)}, u32[]{:S(2)}, u32[]{:S(2)}) collective-permute-start(f32[8,128]{1,0:T(8,128)S(1)} %fusion.5.rest_0_.rest_8_), channel_id=1, source_target_pairs={{0,7},{1,6},{2,5},{3,4},{4,3},{5,2},{6,1},{7,0},{8,15},{9,14},{10,... | collective-permute-start | bytes 12296 | tf_op jit(solution)/shard_map/ppermute | solution.py:620
  36.2 1.8 %collective-permute-start.16 = (f32[8,128]{1,0:T(8,128)S(1)}, f32[8,128]{1,0:T(8,128)S(1)}, u32[]{:S(2)}, u32[]{:S(2)}) collective-permute-start(f32[8,128]{1,0:T(8,128)S(1)} %fusion.5.rest_0_.rest_8_), channel_id=1, source_target_pairs={{0,5},{1,4},{2,7},{3,6},{4,1},{5,0},{6,3},{7,2},{8,13},{9,12},{10,... | collective-permute-start | bytes 12296 | tf_op jit(solution)/shard_map/ppermute | solution.py:620
  38.0 1.8 %collective-permute-start.15 = (f32[8,128]{1,0:T(8,128)S(1)}, f32[8,128]{1,0:T(8,128)S(1)}, u32[]{:S(2)}, u32[]{:S(2)}) collective-permute-start(f32[8,128]{1,0:T(8,128)S(1)} %fusion.5.rest_0_.rest_8_), channel_id=1, source_target_pairs={{0,3},{1,2},{2,1},{3,0},{4,7},{5,6},{6,5},{7,4},{8,11},{9,10},{10,... | collective-permute-start | bytes 12296 | tf_op jit(solution)/shard_map/ppermute | solution.py:620
  39.8 0.9 slope.4.rest_13_.rest_12_
  41.2 2.9 %forward.6 = (bf16[4,6,256,128]{3,2,1,0:T(8,128)(2,1)S(1)}, f32[4,4,256,128]{3,2,1,0:T(8,128)S(1)}, bf16[1056,128]{1,0:T(8,128)(2,1)S(1)}, f32[8,128]{1,0:T(8,128)S(1)}) custom-call(bf16[4,6,256,128]{3,2,1,0:T(8,128)(2,1)S(1)} %get-tuple-element.99.x_in.x, f32[4,4,256,128]{3,2,1,0:T(8,128)S(1)} %get-tuple-element.109.rows_ref.pre_in.pre.rest_12_.rest_18_, ...), custom_call_target="tpu_custom_call" | custom-call | flops 1207959552 | tf_op jit(solution)/shard_map/forward/pallas_call | solution.py:606
  44.1 1.3 collective-permute-start.18
  45.4 0.9 collective-permute-start.19
  46.6 1.3 %collective-permute-start.22 = (f32[8,128]{1,0:T(8,128)S(1)}, f32[8,128]{1,0:T(8,128)S(1)}, u32[]{:S(2)}, u32[]{:S(2)}) collective-permute-start(f32[8,128]{1,0:T(8,128)S(1)} %fusion.4.rest_0_.rest_8_), channel_id=1, source_target_pairs={{0,7},{1,6},{2,5},{3,4},{4,3},{5,2},{6,1},{7,0},{8,15},{9,14},{10,... | collective-permute-start | bytes 12296 | tf_op jit(solution)/shard_map/ppermute | solution.py:620
  47.9 2.5 %collective-permute-start.21 = (f32[8,128]{1,0:T(8,128)S(1)}, f32[8,128]{1,0:T(8,128)S(1)}, u32[]{:S(2)}, u32[]{:S(2)}) collective-permute-start(f32[8,128]{1,0:T(8,128)S(1)} %fusion.4.rest_0_.rest_8_), channel_id=1, source_target_pairs={{0,5},{1,4},{2,7},{3,6},{4,1},{5,0},{6,3},{7,2},{8,13},{9,12},{10,... | collective-permute-start | bytes 12296 | tf_op jit(solution)/shard_map/ppermute | solution.py:620
  50.5 1.8 %collective-permute-start.20 = (f32[8,128]{1,0:T(8,128)S(1)}, f32[8,128]{1,0:T(8,128)S(1)}, u32[]{:S(2)}, u32[]{:S(2)}) collective-permute-start(f32[8,128]{1,0:T(8,128)S(1)} %fusion.4.rest_0_.rest_8_), channel_id=1, source_target_pairs={{0,3},{1,2},{2,1},{3,0},{4,7},{5,6},{6,5},{7,4},{8,11},{9,10},{10,... | collective-permute-start | bytes 12296 | tf_op jit(solution)/shard_map/ppermute | solution.py:620
  53.6 2.9 %forward.7 = (bf16[4,6,256,128]{3,2,1,0:T(8,128)(2,1)S(1)}, f32[4,4,256,128]{3,2,1,0:T(8,128)S(1)}, bf16[1056,128]{1,0:T(8,128)(2,1)S(1)}, f32[8,128]{1,0:T(8,128)S(1)}) custom-call(bf16[4,6,256,128]{3,2,1,0:T(8,128)(2,1)S(1)} %get-tuple-element.105.x_in.x, f32[4,4,256,128]{3,2,1,0:T(8,128)S(1)} %get-tuple-element.115.rows_ref.pre_in.pre.rest_12_.rest_18_, ...), custom_call_target="tpu_custom_call" | custom-call | flops 1207959552 | tf_op jit(solution)/shard_map/forward/pallas_call | solution.py:606
  56.5 1.2 collective-permute-start.23
  57.8 1.2 collective-permute-done.23.near.rest_19_
  59.0 1.4 %collective-permute-start.26 = (f32[8,128]{1,0:T(8,128)S(1)}, f32[8,128]{1,0:T(8,128)S(1)}, u32[]{:S(2)}, u32[]{:S(2)}) collective-permute-start(f32[8,128]{1,0:T(8,128)S(1)} %fusion.3.rest_0_), channel_id=1, source_target_pairs={{0,7},{1,6},{2,5},{3,4},{4,3},{5,2},{6,1},{7,0},{8,15},{9,14},{10,... | collective-permute-start | bytes 12296 | tf_op jit(solution)/shard_map/ppermute | solution.py:620
  61.1 2.0 %collective-permute-start.24 = (f32[8,128]{1,0:T(8,128)S(1)}, f32[8,128]{1,0:T(8,128)S(1)}, u32[]{:S(2)}, u32[]{:S(2)}) collective-permute-start(f32[8,128]{1,0:T(8,128)S(1)} %fusion.3.rest_0_), channel_id=1, source_target_pairs={{0,3},{1,2},{2,1},{3,0},{4,7},{5,6},{6,5},{7,4},{8,11},{9,10},{10,... | collective-permute-start | bytes 12296 | tf_op jit(solution)/shard_map/ppermute | solution.py:620
  63.1 0.8 collective-permute-start.31
  64.0 0.8 slope.6.rest_13_.rest_21_
  64.8 1.0 turn.1
  65.8 1.5 %collective-permute-start.27 = (f32[8,128]{1,0:T(8,128)S(1)}, f32[8,128]{1,0:T(8,128)S(1)}, u32[]{:S(2)}, u32[]{:S(2)}) collective-permute-start(f32[8,128]{1,0:T(8,128)S(1)} %get-tuple-element.117), channel_id=1, source_target_pairs={{0,1},{1,0},{2,3},{3,2},{4,5},{5,4},{6,7},{7,6},{8,9},{9,8},{10,11... | collective-permute-start | bytes 12296 | tf_op jit(solution)/shard_map/ppermute | solution.py:620
  67.2 0.8 collective-permute-done.27
  68.1 2.2 %collective-permute-start.30 = (f32[8,128]{1,0:T(8,128)S(1)}, f32[8,128]{1,0:T(8,128)S(1)}, u32[]{:S(2)}, u32[]{:S(2)}) collective-permute-start(f32[8,128]{1,0:T(8,128)S(1)} %add.78.rest_4_), channel_id=1, source_target_pairs={{0,7},{1,6},{2,5},{3,4},{4,3},{5,2},{6,1},{7,0},{8,15},{9,14},{10,... | collective-permute-start | bytes 12296 | tf_op jit(solution)/shard_map/ppermute | solution.py:620
  70.3 0.9 collective-permute-start.29
  71.2 0.9 collective-permute-start.28
  72.1 0.7 slope.7.rest_21_
  73.0 1.2 collective-permute-done.29.rest_6_
  74.3 3.1 %backward.3 = (bf16[3,3,4,256,256]{4,3,2,1,0:T(8,128)(2,1)S(1)}, bf16[4,4,256,128]{3,2,1,0:T(8,128)(2,1)S(1)}, f32[4,4,256,128]{3,2,1,0:T(8,128)S(1)}, bf16[1056...) custom-call(f32[8,128]{1,0:T(8,128)S(1)} %fusion.3.rest_0_, ...), custom_call_target="tpu_custom_call" | custom-call | flops 1207959552 | tf_op jit(solution)/shard_map/backward/pallas_call | solution.py:606
  79.0 1.4 %collective-permute-start.35 = (f32[8,128]{1,0:T(8,128)S(1)}, f32[8,128]{1,0:T(8,128)S(1)}, u32[]{:S(2)}, u32[]{:S(2)}) collective-permute-start(f32[8,128]{1,0:T(8,128)S(1)} %fusion.2.rest_4_), channel_id=1, source_target_pairs={{0,7},{1,6},{2,5},{3,4},{4,3},{5,2},{6,1},{7,0},{8,15},{9,14},{10,... | collective-permute-start | bytes 12296 | tf_op jit(solution)/shard_map/ppermute | solution.py:620
  80.4 2.4 %collective-permute-start.34 = (f32[8,128]{1,0:T(8,128)S(1)}, f32[8,128]{1,0:T(8,128)S(1)}, u32[]{:S(2)}, u32[]{:S(2)}) collective-permute-start(f32[8,128]{1,0:T(8,128)S(1)} %fusion.2.rest_4_), channel_id=1, source_target_pairs={{0,5},{1,4},{2,7},{3,6},{4,1},{5,0},{6,3},{7,2},{8,13},{9,12},{10,... | collective-permute-start | bytes 12296 | tf_op jit(solution)/shard_map/ppermute | solution.py:620
  82.8 1.8 %collective-permute-start.33 = (f32[8,128]{1,0:T(8,128)S(1)}, f32[8,128]{1,0:T(8,128)S(1)}, u32[]{:S(2)}, u32[]{:S(2)}) collective-permute-start(f32[8,128]{1,0:T(8,128)S(1)} %fusion.2.rest_4_), channel_id=1, source_target_pairs={{0,3},{1,2},{2,1},{3,0},{4,7},{5,6},{6,5},{7,4},{8,11},{9,10},{10,... | collective-permute-start | bytes 12296 | tf_op jit(solution)/shard_map/ppermute | solution.py:620
  84.6 1.9 %weight.6 = (f32[4,144,128]{2,1,0:T(8,128)S(1)}, bf16[4,144,128]{2,1,0:T(8,128)(2,1)S(1)}) custom-call(bf16[4,6,256,128]{3,2,1,0:T(8,128)(2,1)S(1)} %get-tuple-element.111.x, bf16[3,3,4,256,256]{4,3,2,1,0:T(8,128)(2,1)S(1)} %get-tuple-element.125.stack), custom_call_target="tpu_custom_call" | custom-call | flops 1207959552 | tf_op jit(solution)/shard_map/weight/pallas_call | solution.py:606
  86.5 3.0 %backward.4 = (bf16[3,3,4,256,256]{4,3,2,1,0:T(8,128)(2,1)S(1)}, bf16[4,4,256,128]{3,2,1,0:T(8,128)(2,1)S(1)}, f32[4,4,256,128]{3,2,1,0:T(8,128)S(1)}, bf16[1056...) custom-call(f32[8,128]{1,0:T(8,128)S(1)} %fusion.4.rest_0_.rest_8_, ...), custom_call_target="tpu_custom_call" | custom-call | flops 1207959552 | tf_op jit(solution)/shard_map/backward/pallas_call | solution.py:606
  90.2 0.9 collective-permute-start.41
  91.4 2.0 %collective-permute-start.40 = (f32[8,128]{1,0:T(8,128)S(1)}, f32[8,128]{1,0:T(8,128)S(1)}, u32[]{:S(2)}, u32[]{:S(2)}) collective-permute-start(f32[8,128]{1,0:T(8,128)S(1)} %fusion.1.rest_4_), channel_id=1, source_target_pairs={{0,7},{1,6},{2,5},{3,4},{4,3},{5,2},{6,1},{7,0},{8,15},{9,14},{10,... | collective-permute-start | bytes 12296 | tf_op jit(solution)/shard_map/ppermute | solution.py:620
  93.4 1.9 %collective-permute-start.39 = (f32[8,128]{1,0:T(8,128)S(1)}, f32[8,128]{1,0:T(8,128)S(1)}, u32[]{:S(2)}, u32[]{:S(2)}) collective-permute-start(f32[8,128]{1,0:T(8,128)S(1)} %fusion.1.rest_4_), channel_id=1, source_target_pairs={{0,5},{1,4},{2,7},{3,6},{4,1},{5,0},{6,3},{7,2},{8,13},{9,12},{10,... | collective-permute-start | bytes 12296 | tf_op jit(solution)/shard_map/ppermute | solution.py:620
  95.3 1.9 %collective-permute-start.38 = (f32[8,128]{1,0:T(8,128)S(1)}, f32[8,128]{1,0:T(8,128)S(1)}, u32[]{:S(2)}, u32[]{:S(2)}) collective-permute-start(f32[8,128]{1,0:T(8,128)S(1)} %fusion.1.rest_4_), channel_id=1, source_target_pairs={{0,3},{1,2},{2,1},{3,0},{4,7},{5,6},{6,5},{7,4},{8,11},{9,10},{10,... | collective-permute-start | bytes 12296 | tf_op jit(solution)/shard_map/ppermute | solution.py:620
  97.2 1.9 %weight.7 = (f32[4,144,128]{2,1,0:T(8,128)S(1)}, bf16[4,144,128]{2,1,0:T(8,128)(2,1)S(1)}) custom-call(bf16[4,6,256,128]{3,2,1,0:T(8,128)(2,1)S(1)} %get-tuple-element.105.x_in.x, bf16[3,3,4,256,256]{4,3,2,1,0:T(8,128)(2,1)S(1)} %get-tuple-element.133.stack), custom_call_target="tpu_custom_call" | custom-call | flops 1207959552 | tf_op jit(solution)/shard_map/weight/pallas_call | solution.py:606
  99.1 3.0 %backward.5 = (bf16[3,3,4,256,256]{4,3,2,1,0:T(8,128)(2,1)S(1)}, bf16[4,4,256,128]{3,2,1,0:T(8,128)(2,1)S(1)}, f32[4,4,256,128]{3,2,1,0:T(8,128)S(1)}, bf16[1056...) custom-call(f32[8,128]{1,0:T(8,128)S(1)} %fusion.5.rest_0_.rest_8_, ...), custom_call_target="tpu_custom_call" | custom-call | flops 1207959552 | tf_op jit(solution)/shard_map/backward/pallas_call | solution.py:606
  103.9 2.1 %collective-permute-start.45 = (f32[8,128]{1,0:T(8,128)S(1)}, f32[8,128]{1,0:T(8,128)S(1)}, u32[]{:S(2)}, u32[]{:S(2)}) collective-permute-start(f32[8,128]{1,0:T(8,128)S(1)} %fusion.rest_4_), channel_id=1, source_target_pairs={{0,7},{1,6},{2,5},{3,4},{4,3},{5,2},{6,1},{7,0},{8,15},{9,14},{10,... | collective-permute-start | bytes 12296 | tf_op jit(solution)/shard_map/ppermute | solution.py:620
  106.1 1.9 %collective-permute-start.43 = (f32[8,128]{1,0:T(8,128)S(1)}, f32[8,128]{1,0:T(8,128)S(1)}, u32[]{:S(2)}, u32[]{:S(2)}) collective-permute-start(f32[8,128]{1,0:T(8,128)S(1)} %fusion.rest_4_), channel_id=1, source_target_pairs={{0,3},{1,2},{2,1},{3,0},{4,7},{5,6},{6,5},{7,4},{8,11},{9,10},{10,... | collective-permute-start | bytes 12296 | tf_op jit(solution)/shard_map/ppermute | solution.py:620
  108.0 1.9 %weight.8 = (f32[4,144,128]{2,1,0:T(8,128)S(1)}, bf16[4,144,128]{2,1,0:T(8,128)(2,1)S(1)}) custom-call(bf16[4,6,256,128]{3,2,1,0:T(8,128)(2,1)S(1)} %get-tuple-element.99.x_in.x, bf16[3,3,4,256,256]{4,3,2,1,0:T(8,128)(2,1)S(1)} %get-tuple-element.141.stack), custom_call_target="tpu_custom_call" | custom-call | flops 1207959552 | tf_op jit(solution)/shard_map/weight/pallas_call | solution.py:606
  110.2 2.6 %weight.9 = (bf16[3,3,4,256,256]{4,3,2,1,0:T(8,128)(2,1)S(1)}, f32[4,144,128]{2,1,0:T(8,128)S(1)}, bf16[4,144,128]{2,1,0:T(8,128)(2,1)S(1)}, f32[8,128]{1,0:T(8,128)S(1)}) custom-call(f32[8,128]{1,0:T(8,128)S(1)} %fusion.6.rest_0_.rest_8_, f32[8,128]{1,0:T(8,128)S(1)} %collective-permute-done.10.rest_1_.rest_9_, ...), custom_call_target="tpu_custom_call" | custom-call | flops 1207959552 | tf_op jit(solution)/shard_map/weight/pallas_call | solution.py:606
  113.2 1.0 collective-permute-done.46.refs_4_
  114.4 1.6 %collective-permute-start.51 = (bf16[608,128]{1,0:T(8,128)(2,1)S(1)}, bf16[608,128]{1,0:T(8,128)(2,1)S(1)}, u32[]{:S(2)}, u32[]{:S(2)}) collective-permute-start(bf16[608,128]{1,0:T(8,128)(2,1)S(1)} %get-tuple-element.159), channel_id=1, source_target_pairs={{0,8},{8,0},{16,24},{24,16},{1,9},{9,1},{17,25},{25,17},{2,10},{10... | collective-permute-start | bytes 466952 | tf_op jit(solution)/shard_map/ppermute | solution.py:620
  116.0 1.2 collective-permute-start.52
  117.2 0.8 collective-permute-start.53
  118.7 1.5 %neck.1 = bf16[1,4,4,256,128]{4,3,2,1,0:T(8,128)(2,1)} custom-call(bf16[4,6,256,128]{3,2,1,0:T(8,128)(2,1)S(1)} %get-tuple-element.111.x, f32[4,4,256,128]{3,2,1,0:T(8,128)S(1)} %get-tuple-element.155.pre.rows_ref.rest_18_, f32[8,128]{1,0:T(8,128)S(1)} %fusion.3.rest_0_, f32[8,128]{1,0:T(8,128)S(1)} %collective-permute-done.24.rest_1_, ...), custom_call_target="tpu_custom_call" | custom-call | flops 9663676416 | tf_op jit(solution)/shard_map/neck/pallas_call | solution.py:606
  120.2 1.1 collective-permute-done.51.a
  121.3 4.0 %collective-permute-done.52.b = bf16[608,128]{1,0:T(8,128)(2,1)S(1)} collective-permute-done((bf16[608,128]{1,0:T(8,128)(2,1)S(1)}, bf16[608,128]{1,0:T(8,128)(2,1)S(1)}, u32[]{:S(2)}, u32[]{:S(2)}) %collective-permute-start.52) | collective-permute-done | bytes 155680 | tf_op jit(solution)/shard_map/ppermute | solution.py:620
  125.4 1.0 collective-permute-start.54
  126.4 1.7 %collective-permute-start.55 = (bf16[144,128]{1,0:T(8,128)(2,1)S(1)}, bf16[144,128]{1,0:T(8,128)(2,1)S(1)}, u32[]{:S(2)}, u32[]{:S(2)}) collective-permute-start(bf16[144,128]{1,0:T(8,128)(2,1)S(1)} %get-tuple-element.168), channel_id=1, source_target_pairs={{0,4},{1,5},{2,6},{3,7},{4,0},{5,1},{6,2},{7,3},{8,12},{9,13},{10,... | collective-permute-start | bytes 110600 | tf_op jit(solution)/shard_map/ppermute | solution.py:620
  128.1 1.7 %collective-permute-start.56 = (bf16[144,128]{1,0:T(8,128)(2,1)S(1)}, bf16[144,128]{1,0:T(8,128)(2,1)S(1)}, u32[]{:S(2)}, u32[]{:S(2)}) collective-permute-start(bf16[144,128]{1,0:T(8,128)(2,1)S(1)} %get-tuple-element.169), channel_id=1, source_target_pairs={{0,6},{1,7},{2,4},{3,5},{4,2},{5,3},{6,0},{7,1},{8,14},{9,15},{10,... | collective-permute-start | bytes 110600 | tf_op jit(solution)/shard_map/ppermute | solution.py:620
  129.9 3.6 %final_grad.1 = bf16[1,4,4,256,128]{4,3,2,1,0:T(8,128)(2,1)} custom-call(f32[8,128]{1,0:T(8,128)S(1)} %fusion.6.rest_0_.rest_8_, f32[8,128]{1,0:T(8,128)S(1)} %collective-permute-done.10.rest_1_.rest_9_, f32[8,128]{1,0:T(8,128)S(1)} %collective-permute-done.11.rest_2_.rest_10_, f32[8,128]{1,0:T(8,128)S(1)} %collective-permute-done.12.rest_3_.rest_11_, ...), custom_call_target="tpu_custom_call" | custom-call | flops 1207959552 | tf_op jit(solution)/shard_map/final_grad/pallas_call | solution.py:606
  (107 shorter events, 15.8 us)
Async XLA Ops:
  0.6 16.2 %copy-start.3 = (s32[4,4,4,256]{3,2,1,0:T(4,128)S(1)}, s32[4,4,4,256]{3,2,1,0:T(4,128)}, u32[]{:S(2)}) copy-start(s32[4,4,4,256]{3,2,1,0:T(4,128)} %mask.3) | copy-start | bytes 196612
  0.6 16.0 %copy-start.5 = (f32[1,128]{1,0:T(1,128)S(1)}, f32[1,128]{1,0:T(1,128)}, u32[]{:S(2)}) copy-start(f32[1,128]{1,0:T(1,128)} %bias.3) | copy-start | bytes 1540
  0.7 16.0 %copy-start.4 = (f32[1,128]{1,0:T(1,128)S(1)}, f32[1,128]{1,0:T(1,128)}, u32[]{:S(2)}) copy-start(f32[1,128]{1,0:T(1,128)} %gain.3) | copy-start | bytes 1540
  0.7 16.0 %copy-start.1 = (bf16[1,1152,128]{2,1,0:T(8,128)(2,1)S(1)}, bf16[1,1152,128]{2,1,0:T(8,128)(2,1)}, u32[]{:S(2)}) copy-start(bf16[1,1152,128]{2,1,0:T(8,128)(2,1)} %own.1) | copy-start | bytes 884740
  0.7 16.1 %copy-start.2 = (bf16[1,4,4,256,128]{4,3,2,1,0:T(8,128)(2,1)S(1)}, bf16[1,4,4,256,128]{4,3,2,1,0:T(8,128)(2,1)}, u32[]{:S(2)}) copy-start(bf16[1,4,4,256,128]{4,3,2,1,0:T(8,128)(2,1)} %features.3) | copy-start | bytes 3145732
  2.7 12.3 %collective-permute-start = (bf16[2048,128]{1,0:T(8,128)(2,1)S(1)}, bf16[2048,128]{1,0:T(8,128)(2,1)S(1)}, u32[]{:S(2)}, u32[]{:S(2)}) collective-permute-start(bf16[2048,128]{1,0:T(8,128)(2,1)S(1)} %get-tuple-element.89), channel_id=1, source_target_pairs={{0,1},{1,0},{2,3},{3,2},{4,5},{5,4},{6,7},{7,6},{8,9},{9,8},{10,11... | collective-permute-start | bytes 1572872 | tf_op jit(solution)/shard_map/ppermute | solution.py:620
  3.3 8.4 %collective-permute-start.4 = (bf16[608,128]{1,0:T(8,128)(2,1)S(1)}, bf16[608,128]{1,0:T(8,128)(2,1)S(1)}, u32[]{:S(2)}, u32[]{:S(2)}) collective-permute-start(bf16[608,128]{1,0:T(8,128)(2,1)S(1)} %get-tuple-element.91), channel_id=1, source_target_pairs={{0,24},{8,16},{16,8},{24,0},{1,25},{9,17},{17,9},{25,1},{2,26},{10... | collective-permute-start | bytes 466952 | tf_op jit(solution)/shard_map/ppermute | solution.py:620
  6.8 8.3 %collective-permute-start.2 = (bf16[608,128]{1,0:T(8,128)(2,1)S(1)}, bf16[608,128]{1,0:T(8,128)(2,1)S(1)}, u32[]{:S(2)}, u32[]{:S(2)}) collective-permute-start(bf16[608,128]{1,0:T(8,128)(2,1)S(1)} %get-tuple-element.91), channel_id=1, source_target_pairs={{0,8},{8,0},{16,24},{24,16},{1,9},{9,1},{17,25},{25,17},{2,10},{10... | collective-permute-start | bytes 466952 | tf_op jit(solution)/shard_map/ppermute | solution.py:620
  7.3 7.7 %collective-permute-start.3 = (bf16[608,128]{1,0:T(8,128)(2,1)S(1)}, bf16[608,128]{1,0:T(8,128)(2,1)S(1)}, u32[]{:S(2)}, u32[]{:S(2)}) collective-permute-start(bf16[608,128]{1,0:T(8,128)(2,1)S(1)} %get-tuple-element.91), channel_id=1, source_target_pairs={{0,16},{8,24},{16,0},{24,8},{1,17},{9,25},{17,1},{25,9},{2,18},{10... | collective-permute-start | bytes 466952 | tf_op jit(solution)/shard_map/ppermute | solution.py:620
  7.4 9.4 %collective-permute-start.1 = (bf16[1024,128]{1,0:T(8,128)(2,1)S(1)}, bf16[1024,128]{1,0:T(8,128)(2,1)S(1)}, u32[]{:S(2)}, u32[]{:S(2)}) collective-permute-start(bf16[1024,128]{1,0:T(8,128)(2,1)S(1)} %get-tuple-element.90), channel_id=1, source_target_pairs={{1,2},{2,1},{3,4},{4,3},{5,6},{6,5},{9,10},{10,9},{11,12},{12,11},... | collective-permute-start | bytes 786440 | tf_op jit(solution)/shard_map/ppermute | solution.py:627
  11.7 3.9 %collective-permute-start.7 = (bf16[608,128]{1,0:T(8,128)(2,1)S(1)}, bf16[608,128]{1,0:T(8,128)(2,1)S(1)}, u32[]{:S(2)}, u32[]{:S(2)}) collective-permute-start(bf16[608,128]{1,0:T(8,128)(2,1)S(1)} %collective-permute-done.4.r3), channel_id=1, source_target_pairs={{0,1},{1,0},{2,3},{3,2},{4,5},{5,4},{6,7},{7,6},{8,9},{9,8},{10,11... | collective-permute-start | bytes 466952 | tf_op jit(solution)/shard_map/ppermute | solution.py:620
  15.0 1.4 %collective-permute-start.5 = (bf16[608,128]{1,0:T(8,128)(2,1)S(1)}, bf16[608,128]{1,0:T(8,128)(2,1)S(1)}, u32[]{:S(2)}, u32[]{:S(2)}) collective-permute-start(bf16[608,128]{1,0:T(8,128)(2,1)S(1)} %collective-permute-done.2.r1), channel_id=1, source_target_pairs={{0,1},{1,0},{2,3},{3,2},{4,5},{5,4},{6,7},{7,6},{8,9},{9,8},{10,11... | collective-permute-start | bytes 466952 | tf_op jit(solution)/shard_map/ppermute | solution.py:620
  15.1 1.6 %collective-permute-start.6 = (bf16[608,128]{1,0:T(8,128)(2,1)S(1)}, bf16[608,128]{1,0:T(8,128)(2,1)S(1)}, u32[]{:S(2)}, u32[]{:S(2)}) collective-permute-start(bf16[608,128]{1,0:T(8,128)(2,1)S(1)} %collective-permute-done.3.r2), channel_id=1, source_target_pairs={{0,1},{1,0},{2,3},{3,2},{4,5},{5,4},{6,7},{7,6},{8,9},{9,8},{10,11... | collective-permute-start | bytes 466952 | tf_op jit(solution)/shard_map/ppermute | solution.py:620
  19.5 1.6 %collective-permute-start.8 = (bf16[1056,128]{1,0:T(8,128)(2,1)S(1)}, bf16[1056,128]{1,0:T(8,128)(2,1)S(1)}, u32[]{:S(2)}, u32[]{:S(2)}) collective-permute-start(bf16[1056,128]{1,0:T(8,128)(2,1)S(1)} %get-tuple-element.96), channel_id=1, source_target_pairs={{0,1},{1,0},{2,3},{3,2},{4,5},{5,4},{6,7},{7,6},{8,9},{9,8},{10,11... | collective-permute-start | bytes 811016 | tf_op jit(solution)/shard_map/ppermute | solution.py:620
  19.9 7.4 %collective-permute-start.9 = (bf16[1024,128]{1,0:T(8,128)(2,1)S(1)}, bf16[1024,128]{1,0:T(8,128)(2,1)S(1)}, u32[]{:S(2)}, u32[]{:S(2)}) collective-permute-start(bf16[1024,128]{1,0:T(8,128)(2,1)S(1)} %far.7), channel_id=1, source_target_pairs={{1,2},{2,1},{3,4},{4,3},{5,6},{6,5},{9,10},{10,9},{11,12},{12,11},... | collective-permute-start | bytes 786440 | tf_op jit(solution)/shard_map/ppermute | solution.py:627
  21.1 6.2 %collective-permute-start.12 = (f32[8,128]{1,0:T(8,128)S(1)}, f32[8,128]{1,0:T(8,128)S(1)}, u32[]{:S(2)}, u32[]{:S(2)}) collective-permute-start(f32[8,128]{1,0:T(8,128)S(1)} %fusion.6.rest_0_.rest_8_), channel_id=1, source_target_pairs={{0,7},{1,6},{2,5},{3,4},{4,3},{5,2},{6,1},{7,0},{8,15},{9,14},{10,... | collective-permute-start | bytes 12296 | tf_op jit(solution)/shard_map/ppermute | solution.py:620
  24.6 4.0 %collective-permute-start.11 = (f32[8,128]{1,0:T(8,128)S(1)}, f32[8,128]{1,0:T(8,128)S(1)}, u32[]{:S(2)}, u32[]{:S(2)}) collective-permute-start(f32[8,128]{1,0:T(8,128)S(1)} %fusion.6.rest_0_.rest_8_), channel_id=1, source_target_pairs={{0,5},{1,4},{2,7},{3,6},{4,1},{5,0},{6,3},{7,2},{8,13},{9,12},{10,... | collective-permute-start | bytes 12296 | tf_op jit(solution)/shard_map/ppermute | solution.py:620
  25.9 3.0 %collective-permute-start.10 = (f32[8,128]{1,0:T(8,128)S(1)}, f32[8,128]{1,0:T(8,128)S(1)}, u32[]{:S(2)}, u32[]{:S(2)}) collective-permute-start(f32[8,128]{1,0:T(8,128)S(1)} %fusion.6.rest_0_.rest_8_), channel_id=1, source_target_pairs={{0,3},{1,2},{2,1},{3,0},{4,7},{5,6},{6,5},{7,4},{8,11},{9,10},{10,... | collective-permute-start | bytes 12296 | tf_op jit(solution)/shard_map/ppermute | solution.py:620
  32.0 2.2 %collective-permute-start.13 = (bf16[1056,128]{1,0:T(8,128)(2,1)S(1)}, bf16[1056,128]{1,0:T(8,128)(2,1)S(1)}, u32[]{:S(2)}, u32[]{:S(2)}) collective-permute-start(bf16[1056,128]{1,0:T(8,128)(2,1)S(1)} %get-tuple-element.101), channel_id=1, source_target_pairs={{0,1},{1,0},{2,3},{3,2},{4,5},{5,4},{6,7},{7,6},{8,9},{9,8},{10,11... | collective-permute-start | bytes 811016 | tf_op jit(solution)/shard_map/ppermute | solution.py:620
  33.2 7.6 %collective-permute-start.14 = (bf16[1024,128]{1,0:T(8,128)(2,1)S(1)}, bf16[1024,128]{1,0:T(8,128)(2,1)S(1)}, u32[]{:S(2)}, u32[]{:S(2)}) collective-permute-start(bf16[1024,128]{1,0:T(8,128)(2,1)S(1)} %far.8), channel_id=1, source_target_pairs={{1,2},{2,1},{3,4},{4,3},{5,6},{6,5},{9,10},{10,9},{11,12},{12,11},... | collective-permute-start | bytes 786440 | tf_op jit(solution)/shard_map/ppermute | solution.py:627
  34.3 6.4 %collective-permute-start.17 = (f32[8,128]{1,0:T(8,128)S(1)}, f32[8,128]{1,0:T(8,128)S(1)}, u32[]{:S(2)}, u32[]{:S(2)}) collective-permute-start(f32[8,128]{1,0:T(8,128)S(1)} %fusion.5.rest_0_.rest_8_), channel_id=1, source_target_pairs={{0,7},{1,6},{2,5},{3,4},{4,3},{5,2},{6,1},{7,0},{8,15},{9,14},{10,... | collective-permute-start | bytes 12296 | tf_op jit(solution)/shard_map/ppermute | solution.py:620
  36.2 4.5 %collective-permute-start.16 = (f32[8,128]{1,0:T(8,128)S(1)}, f32[8,128]{1,0:T(8,128)S(1)}, u32[]{:S(2)}, u32[]{:S(2)}) collective-permute-start(f32[8,128]{1,0:T(8,128)S(1)} %fusion.5.rest_0_.rest_8_), channel_id=1, source_target_pairs={{0,5},{1,4},{2,7},{3,6},{4,1},{5,0},{6,3},{7,2},{8,13},{9,12},{10,... | collective-permute-start | bytes 12296 | tf_op jit(solution)/shard_map/ppermute | solution.py:620
  38.0 3.2 %collective-permute-start.15 = (f32[8,128]{1,0:T(8,128)S(1)}, f32[8,128]{1,0:T(8,128)S(1)}, u32[]{:S(2)}, u32[]{:S(2)}) collective-permute-start(f32[8,128]{1,0:T(8,128)S(1)} %fusion.5.rest_0_.rest_8_), channel_id=1, source_target_pairs={{0,3},{1,2},{2,1},{3,0},{4,7},{5,6},{6,5},{7,4},{8,11},{9,10},{10,... | collective-permute-start | bytes 12296 | tf_op jit(solution)/shard_map/ppermute | solution.py:620
  44.1 2.5 %collective-permute-start.18 = (bf16[1056,128]{1,0:T(8,128)(2,1)S(1)}, bf16[1056,128]{1,0:T(8,128)(2,1)S(1)}, u32[]{:S(2)}, u32[]{:S(2)}) collective-permute-start(bf16[1056,128]{1,0:T(8,128)(2,1)S(1)} %get-tuple-element.107), channel_id=1, source_target_pairs={{0,1},{1,0},{2,3},{3,2},{4,5},{5,4},{6,7},{7,6},{8,9},{9,8},{10,11... | collective-permute-start | bytes 811016 | tf_op jit(solution)/shard_map/ppermute | solution.py:620
  45.4 7.6 %collective-permute-start.19 = (bf16[1024,128]{1,0:T(8,128)(2,1)S(1)}, bf16[1024,128]{1,0:T(8,128)(2,1)S(1)}, u32[]{:S(2)}, u32[]{:S(2)}) collective-permute-start(bf16[1024,128]{1,0:T(8,128)(2,1)S(1)} %far.9), channel_id=1, source_target_pairs={{1,2},{2,1},{3,4},{4,3},{5,6},{6,5},{9,10},{10,9},{11,12},{12,11},... | collective-permute-start | bytes 786440 | tf_op jit(solution)/shard_map/ppermute | solution.py:627
  46.6 6.5 %collective-permute-start.22 = (f32[8,128]{1,0:T(8,128)S(1)}, f32[8,128]{1,0:T(8,128)S(1)}, u32[]{:S(2)}, u32[]{:S(2)}) collective-permute-start(f32[8,128]{1,0:T(8,128)S(1)} %fusion.4.rest_0_.rest_8_), channel_id=1, source_target_pairs={{0,7},{1,6},{2,5},{3,4},{4,3},{5,2},{6,1},{7,0},{8,15},{9,14},{10,... | collective-permute-start | bytes 12296 | tf_op jit(solution)/shard_map/ppermute | solution.py:620
  47.9 5.1 %collective-permute-start.21 = (f32[8,128]{1,0:T(8,128)S(1)}, f32[8,128]{1,0:T(8,128)S(1)}, u32[]{:S(2)}, u32[]{:S(2)}) collective-permute-start(f32[8,128]{1,0:T(8,128)S(1)} %fusion.4.rest_0_.rest_8_), channel_id=1, source_target_pairs={{0,5},{1,4},{2,7},{3,6},{4,1},{5,0},{6,3},{7,2},{8,13},{9,12},{10,... | collective-permute-start | bytes 12296 | tf_op jit(solution)/shard_map/ppermute | solution.py:620
  50.5 3.2 %collective-permute-start.20 = (f32[8,128]{1,0:T(8,128)S(1)}, f32[8,128]{1,0:T(8,128)S(1)}, u32[]{:S(2)}, u32[]{:S(2)}) collective-permute-start(f32[8,128]{1,0:T(8,128)S(1)} %fusion.4.rest_0_.rest_8_), channel_id=1, source_target_pairs={{0,3},{1,2},{2,1},{3,0},{4,7},{5,6},{6,5},{7,4},{8,11},{9,10},{10,... | collective-permute-start | bytes 12296 | tf_op jit(solution)/shard_map/ppermute | solution.py:620
  56.5 2.4 %collective-permute-start.23 = (bf16[1056,128]{1,0:T(8,128)(2,1)S(1)}, bf16[1056,128]{1,0:T(8,128)(2,1)S(1)}, u32[]{:S(2)}, u32[]{:S(2)}) collective-permute-start(bf16[1056,128]{1,0:T(8,128)(2,1)S(1)} %get-tuple-element.114), channel_id=1, source_target_pairs={{0,1},{1,0},{2,3},{3,2},{4,5},{5,4},{6,7},{7,6},{8,9},{9,8},{10,11... | collective-permute-start | bytes 811016 | tf_op jit(solution)/shard_map/ppermute | solution.py:620
  59.0 5.7 %collective-permute-start.26 = (f32[8,128]{1,0:T(8,128)S(1)}, f32[8,128]{1,0:T(8,128)S(1)}, u32[]{:S(2)}, u32[]{:S(2)}) collective-permute-start(f32[8,128]{1,0:T(8,128)S(1)} %fusion.3.rest_0_), channel_id=1, source_target_pairs={{0,7},{1,6},{2,5},{3,4},{4,3},{5,2},{6,1},{7,0},{8,15},{9,14},{10,... | collective-permute-start | bytes 12296 | tf_op jit(solution)/shard_map/ppermute | solution.py:620
  60.4 4.3 %collective-permute-start.25 = (f32[8,128]{1,0:T(8,128)S(1)}, f32[8,128]{1,0:T(8,128)S(1)}, u32[]{:S(2)}, u32[]{:S(2)}) collective-permute-start(f32[8,128]{1,0:T(8,128)S(1)} %fusion.3.rest_0_), channel_id=1, source_target_pairs={{0,5},{1,4},{2,7},{3,6},{4,1},{5,0},{6,3},{7,2},{8,13},{9,12},{10,... | collective-permute-start | bytes 12296 | tf_op jit(solution)/shard_map/ppermute | solution.py:620
  61.1 3.6 %collective-permute-start.24 = (f32[8,128]{1,0:T(8,128)S(1)}, f32[8,128]{1,0:T(8,128)S(1)}, u32[]{:S(2)}, u32[]{:S(2)}) collective-permute-start(f32[8,128]{1,0:T(8,128)S(1)} %fusion.3.rest_0_), channel_id=1, source_target_pairs={{0,3},{1,2},{2,1},{3,0},{4,7},{5,6},{6,5},{7,4},{8,11},{9,10},{10,... | collective-permute-start | bytes 12296 | tf_op jit(solution)/shard_map/ppermute | solution.py:620
  63.1 1.6 %copy-start = (bf16[1,4,4,256,128]{4,3,2,1,0:T(8,128)(2,1)S(1)}, bf16[1,4,4,256,128]{4,3,2,1,0:T(8,128)(2,1)}, u32[]{:S(2)}) copy-start(bf16[1,4,4,256,128]{4,3,2,1,0:T(8,128)(2,1)} %rest_15_.1) | copy-start | bytes 3145732
  63.1 11.2 %collective-permute-start.31 = (bf16[2048,128]{1,0:T(8,128)(2,1)S(1)}, bf16[2048,128]{1,0:T(8,128)(2,1)S(1)}, u32[]{:S(2)}, u32[]{:S(2)}) collective-permute-start(bf16[2048,128]{1,0:T(8,128)(2,1)S(1)} %far.10), channel_id=1, source_target_pairs={{1,2},{2,1},{3,4},{4,3},{5,6},{6,5},{9,10},{10,9},{11,12},{12,11},... | collective-permute-start | bytes 1572872 | tf_op jit(solution)/shard_map/ppermute | solution.py:627
  65.8 2.3 %collective-permute-start.27 = (f32[8,128]{1,0:T(8,128)S(1)}, f32[8,128]{1,0:T(8,128)S(1)}, u32[]{:S(2)}, u32[]{:S(2)}) collective-permute-start(f32[8,128]{1,0:T(8,128)S(1)} %get-tuple-element.117), channel_id=1, source_target_pairs={{0,1},{1,0},{2,3},{3,2},{4,5},{5,4},{6,7},{7,6},{8,9},{9,8},{10,11... | collective-permute-start | bytes 12296 | tf_op jit(solution)/shard_map/ppermute | solution.py:620
  68.1 4.9 %collective-permute-start.30 = (f32[8,128]{1,0:T(8,128)S(1)}, f32[8,128]{1,0:T(8,128)S(1)}, u32[]{:S(2)}, u32[]{:S(2)}) collective-permute-start(f32[8,128]{1,0:T(8,128)S(1)} %add.78.rest_4_), channel_id=1, source_target_pairs={{0,7},{1,6},{2,5},{3,4},{4,3},{5,2},{6,1},{7,0},{8,15},{9,14},{10,... | collective-permute-start | bytes 12296 | tf_op jit(solution)/shard_map/ppermute | solution.py:620
  70.3 3.9 %collective-permute-start.29 = (f32[8,128]{1,0:T(8,128)S(1)}, f32[8,128]{1,0:T(8,128)S(1)}, u32[]{:S(2)}, u32[]{:S(2)}) collective-permute-start(f32[8,128]{1,0:T(8,128)S(1)} %add.78.rest_4_), channel_id=1, source_target_pairs={{0,5},{1,4},{2,7},{3,6},{4,1},{5,0},{6,3},{7,2},{8,13},{9,12},{10,... | collective-permute-start | bytes 12296 | tf_op jit(solution)/shard_map/ppermute | solution.py:620
  71.2 3.1 %collective-permute-start.28 = (f32[8,128]{1,0:T(8,128)S(1)}, f32[8,128]{1,0:T(8,128)S(1)}, u32[]{:S(2)}, u32[]{:S(2)}) collective-permute-start(f32[8,128]{1,0:T(8,128)S(1)} %add.78.rest_4_), channel_id=1, source_target_pairs={{0,3},{1,2},{2,1},{3,0},{4,7},{5,6},{6,5},{7,4},{8,11},{9,10},{10,... | collective-permute-start | bytes 12296 | tf_op jit(solution)/shard_map/ppermute | solution.py:620
  77.4 1.6 %collective-permute-start.32 = (bf16[1056,128]{1,0:T(8,128)(2,1)S(1)}, bf16[1056,128]{1,0:T(8,128)(2,1)S(1)}, u32[]{:S(2)}, u32[]{:S(2)}) collective-permute-start(bf16[1056,128]{1,0:T(8,128)(2,1)S(1)} %get-tuple-element.123), channel_id=1, source_target_pairs={{0,1},{1,0},{2,3},{3,2},{4,5},{5,4},{6,7},{7,6},{8,9},{9,8},{10,11... | collective-permute-start | bytes 811016 | tf_op jit(solution)/shard_map/ppermute | solution.py:620
  77.8 8.6 %collective-permute-start.36 = (bf16[1024,128]{1,0:T(8,128)(2,1)S(1)}, bf16[1024,128]{1,0:T(8,128)(2,1)S(1)}, u32[]{:S(2)}, u32[]{:S(2)}) collective-permute-start(bf16[1024,128]{1,0:T(8,128)(2,1)S(1)} %far.11), channel_id=1, source_target_pairs={{1,2},{2,1},{3,4},{4,3},{5,6},{6,5},{9,10},{10,9},{11,12},{12,11},... | collective-permute-start | bytes 786440 | tf_op jit(solution)/shard_map/ppermute | solution.py:627
  79.0 7.5 %collective-permute-start.35 = (f32[8,128]{1,0:T(8,128)S(1)}, f32[8,128]{1,0:T(8,128)S(1)}, u32[]{:S(2)}, u32[]{:S(2)}) collective-permute-start(f32[8,128]{1,0:T(8,128)S(1)} %fusion.2.rest_4_), channel_id=1, source_target_pairs={{0,7},{1,6},{2,5},{3,4},{4,3},{5,2},{6,1},{7,0},{8,15},{9,14},{10,... | collective-permute-start | bytes 12296 | tf_op jit(solution)/shard_map/ppermute | solution.py:620
  80.4 6.1 %collective-permute-start.34 = (f32[8,128]{1,0:T(8,128)S(1)}, f32[8,128]{1,0:T(8,128)S(1)}, u32[]{:S(2)}, u32[]{:S(2)}) collective-permute-start(f32[8,128]{1,0:T(8,128)S(1)} %fusion.2.rest_4_), channel_id=1, source_target_pairs={{0,5},{1,4},{2,7},{3,6},{4,1},{5,0},{6,3},{7,2},{8,13},{9,12},{10,... | collective-permute-start | bytes 12296 | tf_op jit(solution)/shard_map/ppermute | solution.py:620
  82.8 3.7 %collective-permute-start.33 = (f32[8,128]{1,0:T(8,128)S(1)}, f32[8,128]{1,0:T(8,128)S(1)}, u32[]{:S(2)}, u32[]{:S(2)}) collective-permute-start(f32[8,128]{1,0:T(8,128)S(1)} %fusion.2.rest_4_), channel_id=1, source_target_pairs={{0,3},{1,2},{2,1},{3,0},{4,7},{5,6},{6,5},{7,4},{8,11},{9,10},{10,... | collective-permute-start | bytes 12296 | tf_op jit(solution)/shard_map/ppermute | solution.py:620
  89.5 1.9 %collective-permute-start.37 = (bf16[1056,128]{1,0:T(8,128)(2,1)S(1)}, bf16[1056,128]{1,0:T(8,128)(2,1)S(1)}, u32[]{:S(2)}, u32[]{:S(2)}) collective-permute-start(bf16[1056,128]{1,0:T(8,128)(2,1)S(1)} %get-tuple-element.131), channel_id=1, source_target_pairs={{0,1},{1,0},{2,3},{3,2},{4,5},{5,4},{6,7},{7,6},{8,9},{9,8},{10,11... | collective-permute-start | bytes 811016 | tf_op jit(solution)/shard_map/ppermute | solution.py:620
  90.2 8.8 %collective-permute-start.41 = (bf16[1024,128]{1,0:T(8,128)(2,1)S(1)}, bf16[1024,128]{1,0:T(8,128)(2,1)S(1)}, u32[]{:S(2)}, u32[]{:S(2)}) collective-permute-start(bf16[1024,128]{1,0:T(8,128)(2,1)S(1)} %far.12), channel_id=1, source_target_pairs={{1,2},{2,1},{3,4},{4,3},{5,6},{6,5},{9,10},{10,9},{11,12},{12,11},... | collective-permute-start | bytes 786440 | tf_op jit(solution)/shard_map/ppermute | solution.py:627
  91.4 7.7 %collective-permute-start.40 = (f32[8,128]{1,0:T(8,128)S(1)}, f32[8,128]{1,0:T(8,128)S(1)}, u32[]{:S(2)}, u32[]{:S(2)}) collective-permute-start(f32[8,128]{1,0:T(8,128)S(1)} %fusion.1.rest_4_), channel_id=1, source_target_pairs={{0,7},{1,6},{2,5},{3,4},{4,3},{5,2},{6,1},{7,0},{8,15},{9,14},{10,... | collective-permute-start | bytes 12296 | tf_op jit(solution)/shard_map/ppermute | solution.py:620
  93.4 5.7 %collective-permute-start.39 = (f32[8,128]{1,0:T(8,128)S(1)}, f32[8,128]{1,0:T(8,128)S(1)}, u32[]{:S(2)}, u32[]{:S(2)}) collective-permute-start(f32[8,128]{1,0:T(8,128)S(1)} %fusion.1.rest_4_), channel_id=1, source_target_pairs={{0,5},{1,4},{2,7},{3,6},{4,1},{5,0},{6,3},{7,2},{8,13},{9,12},{10,... | collective-permute-start | bytes 12296 | tf_op jit(solution)/shard_map/ppermute | solution.py:620
  95.3 3.8 %collective-permute-start.38 = (f32[8,128]{1,0:T(8,128)S(1)}, f32[8,128]{1,0:T(8,128)S(1)}, u32[]{:S(2)}, u32[]{:S(2)}) collective-permute-start(f32[8,128]{1,0:T(8,128)S(1)} %fusion.1.rest_4_), channel_id=1, source_target_pairs={{0,3},{1,2},{2,1},{3,0},{4,7},{5,6},{6,5},{7,4},{8,11},{9,10},{10,... | collective-permute-start | bytes 12296 | tf_op jit(solution)/shard_map/ppermute | solution.py:620
  102.2 1.8 %collective-permute-start.42 = (bf16[1056,128]{1,0:T(8,128)(2,1)S(1)}, bf16[1056,128]{1,0:T(8,128)(2,1)S(1)}, u32[]{:S(2)}, u32[]{:S(2)}) collective-permute-start(bf16[1056,128]{1,0:T(8,128)(2,1)S(1)} %get-tuple-element.139), channel_id=1, source_target_pairs={{0,1},{1,0},{2,3},{3,2},{4,5},{5,4},{6,7},{7,6},{8,9},{9,8},{10,11... | collective-permute-start | bytes 811016 | tf_op jit(solution)/shard_map/ppermute | solution.py:620
  102.8 10.5 %collective-permute-start.49 = (bf16[4,144,128]{2,1,0:T(8,128)(2,1)S(1)}, bf16[4,144,128]{2,1,0:T(8,128)(2,1)S(1)}, u32[]{:S(2)}, u32[]{:S(2)}) collective-permute-start(bf16[4,144,128]{2,1,0:T(8,128)(2,1)S(1)} %get-tuple-element.126), channel_id=1, source_target_pairs={{0,1},{1,0},{2,3},{3,2},{4,5},{5,4},{6,7},{7,6},{8,9},{9,8},{10,11... | collective-permute-start | bytes 442376 | tf_op jit(solution)/shard_map/ppermute | solution.py:620
  102.8 10.4 %collective-permute-start.48 = (bf16[4,144,128]{2,1,0:T(8,128)(2,1)S(1)}, bf16[4,144,128]{2,1,0:T(8,128)(2,1)S(1)}, u32[]{:S(2)}, u32[]{:S(2)}) collective-permute-start(bf16[4,144,128]{2,1,0:T(8,128)(2,1)S(1)} %get-tuple-element.134), channel_id=1, source_target_pairs={{0,1},{1,0},{2,3},{3,2},{4,5},{5,4},{6,7},{7,6},{8,9},{9,8},{10,11... | collective-permute-start | bytes 442376 | tf_op jit(solution)/shard_map/ppermute | solution.py:620
  103.9 6.0 %collective-permute-start.45 = (f32[8,128]{1,0:T(8,128)S(1)}, f32[8,128]{1,0:T(8,128)S(1)}, u32[]{:S(2)}, u32[]{:S(2)}) collective-permute-start(f32[8,128]{1,0:T(8,128)S(1)} %fusion.rest_4_), channel_id=1, source_target_pairs={{0,7},{1,6},{2,5},{3,4},{4,3},{5,2},{6,1},{7,0},{8,15},{9,14},{10,... | collective-permute-start | bytes 12296 | tf_op jit(solution)/shard_map/ppermute | solution.py:620
  106.0 4.1 %collective-permute-start.44 = (f32[8,128]{1,0:T(8,128)S(1)}, f32[8,128]{1,0:T(8,128)S(1)}, u32[]{:S(2)}, u32[]{:S(2)}) collective-permute-start(f32[8,128]{1,0:T(8,128)S(1)} %fusion.rest_4_), channel_id=1, source_target_pairs={{0,5},{1,4},{2,7},{3,6},{4,1},{5,0},{6,3},{7,2},{8,13},{9,12},{10,... | collective-permute-start | bytes 12296 | tf_op jit(solution)/shard_map/ppermute | solution.py:620
  106.1 4.1 %collective-permute-start.43 = (f32[8,128]{1,0:T(8,128)S(1)}, f32[8,128]{1,0:T(8,128)S(1)}, u32[]{:S(2)}, u32[]{:S(2)}) collective-permute-start(f32[8,128]{1,0:T(8,128)S(1)} %fusion.rest_4_), channel_id=1, source_target_pairs={{0,3},{1,2},{2,1},{3,0},{4,7},{5,6},{6,5},{7,4},{8,11},{9,10},{10,... | collective-permute-start | bytes 12296 | tf_op jit(solution)/shard_map/ppermute | solution.py:620
  109.9 3.3 %collective-permute-start.47 = (bf16[4,144,128]{2,1,0:T(8,128)(2,1)S(1)}, bf16[4,144,128]{2,1,0:T(8,128)(2,1)S(1)}, u32[]{:S(2)}, u32[]{:S(2)}) collective-permute-start(bf16[4,144,128]{2,1,0:T(8,128)(2,1)S(1)} %get-tuple-element.142), channel_id=1, source_target_pairs={{0,1},{1,0},{2,3},{3,2},{4,5},{5,4},{6,7},{7,6},{8,9},{9,8},{10,11... | collective-permute-start | bytes 442376 | tf_op jit(solution)/shard_map/ppermute | solution.py:620
  112.8 1.4 %collective-permute-start.46 = (bf16[4,144,128]{2,1,0:T(8,128)(2,1)S(1)}, bf16[4,144,128]{2,1,0:T(8,128)(2,1)S(1)}, u32[]{:S(2)}, u32[]{:S(2)}) collective-permute-start(bf16[4,144,128]{2,1,0:T(8,128)(2,1)S(1)} %get-tuple-element.149), channel_id=1, source_target_pairs={{0,1},{1,0},{2,3},{3,2},{4,5},{5,4},{6,7},{7,6},{8,9},{9,8},{10,11... | collective-permute-start | bytes 442376 | tf_op jit(solution)/shard_map/ppermute | solution.py:620
  114.4 6.9 %collective-permute-start.51 = (bf16[608,128]{1,0:T(8,128)(2,1)S(1)}, bf16[608,128]{1,0:T(8,128)(2,1)S(1)}, u32[]{:S(2)}, u32[]{:S(2)}) collective-permute-start(bf16[608,128]{1,0:T(8,128)(2,1)S(1)} %get-tuple-element.159), channel_id=1, source_target_pairs={{0,8},{8,0},{16,24},{24,16},{1,9},{9,1},{17,25},{25,17},{2,10},{10... | collective-permute-start | bytes 466952 | tf_op jit(solution)/shard_map/ppermute | solution.py:620
  116.0 9.3 %collective-permute-start.52 = (bf16[608,128]{1,0:T(8,128)(2,1)S(1)}, bf16[608,128]{1,0:T(8,128)(2,1)S(1)}, u32[]{:S(2)}, u32[]{:S(2)}) collective-permute-start(bf16[608,128]{1,0:T(8,128)(2,1)S(1)} %get-tuple-element.161), channel_id=1, source_target_pairs={{0,16},{8,24},{16,0},{24,8},{1,17},{9,25},{17,1},{25,9},{2,18},{10... | collective-permute-start | bytes 466952 | tf_op jit(solution)/shard_map/ppermute | solution.py:620
  117.2 8.1 %collective-permute-start.53 = (bf16[608,128]{1,0:T(8,128)(2,1)S(1)}, bf16[608,128]{1,0:T(8,128)(2,1)S(1)}, u32[]{:S(2)}, u32[]{:S(2)}) collective-permute-start(bf16[608,128]{1,0:T(8,128)(2,1)S(1)} %get-tuple-element.162), channel_id=1, source_target_pairs={{0,24},{8,16},{16,8},{24,0},{1,25},{9,17},{17,9},{25,1},{2,26},{10... | collective-permute-start | bytes 466952 | tf_op jit(solution)/shard_map/ppermute | solution.py:620
  118.0 11.9 %collective-permute-start.50 = (bf16[1024,128]{1,0:T(8,128)(2,1)S(1)}, bf16[1024,128]{1,0:T(8,128)(2,1)S(1)}, u32[]{:S(2)}, u32[]{:S(2)}) collective-permute-start(bf16[1024,128]{1,0:T(8,128)(2,1)S(1)} %far.13), channel_id=1, source_target_pairs={{1,2},{2,1},{3,4},{4,3},{5,6},{6,5},{9,10},{10,9},{11,12},{12,11},... | collective-permute-start | bytes 786440 | tf_op jit(solution)/shard_map/ppermute | solution.py:627
  125.4 8.1 %collective-permute-start.54 = (bf16[144,128]{1,0:T(8,128)(2,1)S(1)}, bf16[144,128]{1,0:T(8,128)(2,1)S(1)}, u32[]{:S(2)}, u32[]{:S(2)}) collective-permute-start(bf16[144,128]{1,0:T(8,128)(2,1)S(1)} %get-tuple-element.167), channel_id=1, source_target_pairs={{0,2},{1,3},{2,0},{3,1},{4,6},{5,7},{6,4},{7,5},{8,10},{9,11},{10,... | collective-permute-start | bytes 110600 | tf_op jit(solution)/shard_map/ppermute | solution.py:620
  126.4 7.1 %collective-permute-start.55 = (bf16[144,128]{1,0:T(8,128)(2,1)S(1)}, bf16[144,128]{1,0:T(8,128)(2,1)S(1)}, u32[]{:S(2)}, u32[]{:S(2)}) collective-permute-start(bf16[144,128]{1,0:T(8,128)(2,1)S(1)} %get-tuple-element.168), channel_id=1, source_target_pairs={{0,4},{1,5},{2,6},{3,7},{4,0},{5,1},{6,2},{7,3},{8,12},{9,13},{10,... | collective-permute-start | bytes 110600 | tf_op jit(solution)/shard_map/ppermute | solution.py:620
  128.1 5.8 %collective-permute-start.56 = (bf16[144,128]{1,0:T(8,128)(2,1)S(1)}, bf16[144,128]{1,0:T(8,128)(2,1)S(1)}, u32[]{:S(2)}, u32[]{:S(2)}) collective-permute-start(bf16[144,128]{1,0:T(8,128)(2,1)S(1)} %get-tuple-element.169), channel_id=1, source_target_pairs={{0,6},{1,7},{2,4},{3,5},{4,2},{5,3},{6,0},{7,1},{8,14},{9,15},{10,... | collective-permute-start | bytes 110600 | tf_op jit(solution)/shard_map/ppermute | solution.py:620

commit v4 on v3

--- a/solution.py
+++ b/solution.py
@@ -697,7 +697,6 @@
     got = [swap(wsend, "section", d) for d in (1, 2, 3)]
     e1 = swap(e1, "row", 1)
     e2 = swap_next(e2)
-    got[1] = after(got[1], e1)
     others = [swap(v, "row", 1) for v in got]
     weights, gbs = call(
         gather_kernel,

time: 135 us -> 135 us (level)
  transfers between devices with their start and end apart: 57 -> 57, of which waited for: 22 -> 23; matrix products, arithmetic and copies ran while one was open for 0% -> 0% of each run, Pallas kernels for 13% -> 13%
where the time goes in v4:
time: 135 us; the launch traced here: 134 us
  starting transfers between devices  68.2 us (51%)
  Pallas kernels  41.7 us (31%)
  waiting for transfers between devices  23.4 us (17%)
    ppermute x49, starting transfers between devices, swap(): return lax.ppermute(value, axis, [(i, i ^ step) for i in range(count)])  62.2 us
    pallas_call x30, Pallas kernels, call(): pl.pallas_call(body, out_shape=[jax.ShapeDtypeStruct(s, d) for s, d in ou...  41.7 us
    ppermute x49, waiting for transfers between devices, swap(): return lax.ppermute(value, axis, [(i, i ^ step) for i in range(count)])  23.3 us
    ppermute x8, starting transfers between devices, swap_next(): return lax.ppermute(value, 'row', pairs)  5.96 us
  transfers between devices with their start and end apart: 57, of which 23 were waited for; matrix products, arithmetic and copies ran while one was open for 0% of the time, Pallas kernels for 13%

profile of v4, /device:TPU:0, one launch (start us, length us, event | category | flops | bytes accessed | tf_op | source)
XLA Modules:
  0.0 134.5 jit_solution(1665765822448276310)
XLA Ops:
  0.7 2.1 %prep.1 = (bf16[2048,128]{1,0:T(8,128)(2,1)S(1)}, bf16[1024,128]{1,0:T(8,128)(2,1)S(1)}, bf16[1024,128]{1,0:T(8,128)(2,1)S(1)}, bf16[608,128]{1,0:T(8,128)(2,1)S(1)}) custom-call(s32[4,4,4,256]{3,2,1,0:T(4,128)} %mask.3, bf16[1,4,4,256,128]{4,3,2,1,0:T(8,128)(2,1)} %features.3, bf16[1,4,4,256,128]{4,3,2,1,0:T(8,128)(2,1)} %rest_15_.1, ...), custom_call_target="tpu_custom_call" | custom-call | tf_op jit(solution)/shard_map/prep/pallas_call | solution.py:606
  3.3 3.5 %collective-permute-start.4 = (bf16[608,128]{1,0:T(8,128)(2,1)S(1)}, bf16[608,128]{1,0:T(8,128)(2,1)S(1)}, u32[]{:S(2)}, u32[]{:S(2)}) collective-permute-start(bf16[608,128]{1,0:T(8,128)(2,1)S(1)} %get-tuple-element.90), channel_id=1, source_target_pairs={{0,24},{8,16},{16,8},{24,0},{1,25},{9,17},{17,9},{25,1},{2,26},{10... | collective-permute-start | bytes 466952 | tf_op jit(solution)/shard_map/ppermute | solution.py:620
  8.1 3.6 %collective-permute-done.4.r3 = bf16[608,128]{1,0:T(8,128)(2,1)S(1)} collective-permute-done((bf16[608,128]{1,0:T(8,128)(2,1)S(1)}, bf16[608,128]{1,0:T(8,128)(2,1)S(1)}, u32[]{:S(2)}, u32[]{:S(2)}) %collective-permute-start.4) | collective-permute-done | bytes 155680 | tf_op jit(solution)/shard_map/ppermute | solution.py:620
  11.7 3.1 %collective-permute-done.3.r2 = bf16[608,128]{1,0:T(8,128)(2,1)S(1)} collective-permute-done((bf16[608,128]{1,0:T(8,128)(2,1)S(1)}, bf16[608,128]{1,0:T(8,128)(2,1)S(1)}, u32[]{:S(2)}, u32[]{:S(2)}) %collective-permute-start.3) | collective-permute-done | bytes 155680 | tf_op jit(solution)/shard_map/ppermute | solution.py:620
  15.3 0.9 collective-permute-done.6.o2
  16.6 2.7 %forward.4 = (bf16[4,6,256,128]{3,2,1,0:T(8,128)(2,1)S(1)}, f32[4,4,256,128]{3,2,1,0:T(8,128)S(1)}, bf16[1056,128]{1,0:T(8,128)(2,1)S(1)}, f32[8,128]{1,0:T(8,128)S(1)}) custom-call(s32[4,4,4,256]{3,2,1,0:T(4,128)S(1)} %copy-done.3, bf16[1,4,4,256,128]{4,3,2,1,0:T(8,128)(2,1)S(1)} %copy-done.2, bf16[2048,128]{1,0:T(8,128)(2,1)S(1)} %collective-permute-done.near.rest_16_, ...), custom_call_target="tpu_custom_call" | custom-call | flops 1207959552 | tf_op jit(solution)/shard_map/forward/pallas_call | solution.py:606
  20.9 3.6 %collective-permute-start.12 = (f32[8,128]{1,0:T(8,128)S(1)}, f32[8,128]{1,0:T(8,128)S(1)}, u32[]{:S(2)}, u32[]{:S(2)}) collective-permute-start(f32[8,128]{1,0:T(8,128)S(1)} %fusion.6.rest_0_.rest_8_), channel_id=1, source_target_pairs={{0,7},{1,6},{2,5},{3,4},{4,3},{5,2},{6,1},{7,0},{8,15},{9,14},{10,... | collective-permute-start | bytes 12296 | tf_op jit(solution)/shard_map/ppermute | solution.py:620
  24.5 1.2 collective-permute-start.11
  25.8 1.4 %collective-permute-start.10 = (f32[8,128]{1,0:T(8,128)S(1)}, f32[8,128]{1,0:T(8,128)S(1)}, u32[]{:S(2)}, u32[]{:S(2)}) collective-permute-start(f32[8,128]{1,0:T(8,128)S(1)} %fusion.6.rest_0_.rest_8_), channel_id=1, source_target_pairs={{0,3},{1,2},{2,1},{3,0},{4,7},{5,6},{6,5},{7,4},{8,11},{9,10},{10,... | collective-permute-start | bytes 12296 | tf_op jit(solution)/shard_map/ppermute | solution.py:620
  27.2 1.4 %collective-permute-done.11.rest_2_.rest_10_ = f32[8,128]{1,0:T(8,128)S(1)} collective-permute-done((f32[8,128]{1,0:T(8,128)S(1)}, f32[8,128]{1,0:T(8,128)S(1)}, u32[]{:S(2)}, u32[]{:S(2)}) %collective-permute-start.11) | collective-permute-done | bytes 4128 | tf_op jit(solution)/shard_map/ppermute | solution.py:620
  28.8 3.1 %forward.5 = (bf16[4,6,256,128]{3,2,1,0:T(8,128)(2,1)S(1)}, f32[4,4,256,128]{3,2,1,0:T(8,128)S(1)}, bf16[1056,128]{1,0:T(8,128)(2,1)S(1)}, f32[8,128]{1,0:T(8,128)S(1)}) custom-call(bf16[4,6,256,128]{3,2,1,0:T(8,128)(2,1)S(1)} %get-tuple-element.92.x_in.rest_14_, f32[4,4,256,128]{3,2,1,0:T(8,128)S(1)} %get-tuple-element.101.rows_ref.pre_in.pre.rest_12_.rest_10_, ...), custom_call_target="tpu_custom_call" | custom-call | flops 1207959552 | tf_op jit(solution)/shard_map/forward/pallas_call | solution.py:606
  32.0 1.1 collective-permute-start.13
  34.2 1.9 %collective-permute-start.17 = (f32[8,128]{1,0:T(8,128)S(1)}, f32[8,128]{1,0:T(8,128)S(1)}, u32[]{:S(2)}, u32[]{:S(2)}) collective-permute-start(f32[8,128]{1,0:T(8,128)S(1)} %fusion.5.rest_0_.rest_8_), channel_id=1, source_target_pairs={{0,7},{1,6},{2,5},{3,4},{4,3},{5,2},{6,1},{7,0},{8,15},{9,14},{10,... | collective-permute-start | bytes 12296 | tf_op jit(solution)/shard_map/ppermute | solution.py:620
  36.1 1.8 %collective-permute-start.16 = (f32[8,128]{1,0:T(8,128)S(1)}, f32[8,128]{1,0:T(8,128)S(1)}, u32[]{:S(2)}, u32[]{:S(2)}) collective-permute-start(f32[8,128]{1,0:T(8,128)S(1)} %fusion.5.rest_0_.rest_8_), channel_id=1, source_target_pairs={{0,5},{1,4},{2,7},{3,6},{4,1},{5,0},{6,3},{7,2},{8,13},{9,12},{10,... | collective-permute-start | bytes 12296 | tf_op jit(solution)/shard_map/ppermute | solution.py:620
  37.9 1.8 %collective-permute-start.15 = (f32[8,128]{1,0:T(8,128)S(1)}, f32[8,128]{1,0:T(8,128)S(1)}, u32[]{:S(2)}, u32[]{:S(2)}) collective-permute-start(f32[8,128]{1,0:T(8,128)S(1)} %fusion.5.rest_0_.rest_8_), channel_id=1, source_target_pairs={{0,3},{1,2},{2,1},{3,0},{4,7},{5,6},{6,5},{7,4},{8,11},{9,10},{10,... | collective-permute-start | bytes 12296 | tf_op jit(solution)/shard_map/ppermute | solution.py:620
  39.7 0.9 slope.4.rest_13_.rest_12_
  41.1 2.9 %forward.6 = (bf16[4,6,256,128]{3,2,1,0:T(8,128)(2,1)S(1)}, f32[4,4,256,128]{3,2,1,0:T(8,128)S(1)}, bf16[1056,128]{1,0:T(8,128)(2,1)S(1)}, f32[8,128]{1,0:T(8,128)S(1)}) custom-call(bf16[4,6,256,128]{3,2,1,0:T(8,128)(2,1)S(1)} %get-tuple-element.97.x_in.x, f32[4,4,256,128]{3,2,1,0:T(8,128)S(1)} %get-tuple-element.107.rows_ref.pre_in.pre.rest_12_.rest_18_, ...), custom_call_target="tpu_custom_call" | custom-call | flops 1207959552 | tf_op jit(solution)/shard_map/forward/pallas_call | solution.py:606
  44.0 1.3 collective-permute-start.18
  45.3 0.9 collective-permute-start.19
  46.5 1.4 %collective-permute-start.22 = (f32[8,128]{1,0:T(8,128)S(1)}, f32[8,128]{1,0:T(8,128)S(1)}, u32[]{:S(2)}, u32[]{:S(2)}) collective-permute-start(f32[8,128]{1,0:T(8,128)S(1)} %fusion.4.rest_0_.rest_8_), channel_id=1, source_target_pairs={{0,7},{1,6},{2,5},{3,4},{4,3},{5,2},{6,1},{7,0},{8,15},{9,14},{10,... | collective-permute-start | bytes 12296 | tf_op jit(solution)/shard_map/ppermute | solution.py:620
  47.9 2.5 %collective-permute-start.21 = (f32[8,128]{1,0:T(8,128)S(1)}, f32[8,128]{1,0:T(8,128)S(1)}, u32[]{:S(2)}, u32[]{:S(2)}) collective-permute-start(f32[8,128]{1,0:T(8,128)S(1)} %fusion.4.rest_0_.rest_8_), channel_id=1, source_target_pairs={{0,5},{1,4},{2,7},{3,6},{4,1},{5,0},{6,3},{7,2},{8,13},{9,12},{10,... | collective-permute-start | bytes 12296 | tf_op jit(solution)/shard_map/ppermute | solution.py:620
  50.4 1.8 %collective-permute-start.20 = (f32[8,128]{1,0:T(8,128)S(1)}, f32[8,128]{1,0:T(8,128)S(1)}, u32[]{:S(2)}, u32[]{:S(2)}) collective-permute-start(f32[8,128]{1,0:T(8,128)S(1)} %fusion.4.rest_0_.rest_8_), channel_id=1, source_target_pairs={{0,3},{1,2},{2,1},{3,0},{4,7},{5,6},{6,5},{7,4},{8,11},{9,10},{10,... | collective-permute-start | bytes 12296 | tf_op jit(solution)/shard_map/ppermute | solution.py:620
  53.5 2.9 %forward.7 = (bf16[4,6,256,128]{3,2,1,0:T(8,128)(2,1)S(1)}, f32[4,4,256,128]{3,2,1,0:T(8,128)S(1)}, bf16[1056,128]{1,0:T(8,128)(2,1)S(1)}, f32[8,128]{1,0:T(8,128)S(1)}) custom-call(bf16[4,6,256,128]{3,2,1,0:T(8,128)(2,1)S(1)} %get-tuple-element.103.x_in.x, f32[4,4,256,128]{3,2,1,0:T(8,128)S(1)} %get-tuple-element.113.rows_ref.pre_in.pre.rest_12_.rest_18_, ...), custom_call_target="tpu_custom_call" | custom-call | flops 1207959552 | tf_op jit(solution)/shard_map/forward/pallas_call | solution.py:606
  56.4 1.3 collective-permute-start.23
  57.7 1.2 collective-permute-done.23.near.rest_19_
  58.9 1.4 %collective-permute-start.26 = (f32[8,128]{1,0:T(8,128)S(1)}, f32[8,128]{1,0:T(8,128)S(1)}, u32[]{:S(2)}, u32[]{:S(2)}) collective-permute-start(f32[8,128]{1,0:T(8,128)S(1)} %fusion.3.rest_0_), channel_id=1, source_target_pairs={{0,7},{1,6},{2,5},{3,4},{4,3},{5,2},{6,1},{7,0},{8,15},{9,14},{10,... | collective-permute-start | bytes 12296 | tf_op jit(solution)/shard_map/ppermute | solution.py:620
  61.0 2.0 %collective-permute-start.24 = (f32[8,128]{1,0:T(8,128)S(1)}, f32[8,128]{1,0:T(8,128)S(1)}, u32[]{:S(2)}, u32[]{:S(2)}) collective-permute-start(f32[8,128]{1,0:T(8,128)S(1)} %fusion.3.rest_0_), channel_id=1, source_target_pairs={{0,3},{1,2},{2,1},{3,0},{4,7},{5,6},{6,5},{7,4},{8,11},{9,10},{10,... | collective-permute-start | bytes 12296 | tf_op jit(solution)/shard_map/ppermute | solution.py:620
  63.0 0.8 collective-permute-start.31
  63.9 0.8 slope.6.rest_13_.rest_21_
  64.7 1.0 turn.1
  65.7 1.5 %collective-permute-start.27 = (f32[8,128]{1,0:T(8,128)S(1)}, f32[8,128]{1,0:T(8,128)S(1)}, u32[]{:S(2)}, u32[]{:S(2)}) collective-permute-start(f32[8,128]{1,0:T(8,128)S(1)} %get-tuple-element.115), channel_id=1, source_target_pairs={{0,1},{1,0},{2,3},{3,2},{4,5},{5,4},{6,7},{7,6},{8,9},{9,8},{10,11... | collective-permute-start | bytes 12296 | tf_op jit(solution)/shard_map/ppermute | solution.py:620
  67.1 0.8 collective-permute-done.27
  68.0 2.2 %collective-permute-start.30 = (f32[8,128]{1,0:T(8,128)S(1)}, f32[8,128]{1,0:T(8,128)S(1)}, u32[]{:S(2)}, u32[]{:S(2)}) collective-permute-start(f32[8,128]{1,0:T(8,128)S(1)} %add.78.rest_4_), channel_id=1, source_target_pairs={{0,7},{1,6},{2,5},{3,4},{4,3},{5,2},{6,1},{7,0},{8,15},{9,14},{10,... | collective-permute-start | bytes 12296 | tf_op jit(solution)/shard_map/ppermute | solution.py:620
  70.2 0.9 collective-permute-start.29
  71.1 0.9 collective-permute-start.28
  72.0 0.7 slope.7.rest_21_
  72.9 1.2 collective-permute-done.29.rest_6_
  74.2 3.1 %backward.3 = (bf16[3,3,4,256,256]{4,3,2,1,0:T(8,128)(2,1)S(1)}, bf16[4,4,256,128]{3,2,1,0:T(8,128)(2,1)S(1)}, f32[4,4,256,128]{3,2,1,0:T(8,128)S(1)}, bf16[1056...) custom-call(f32[8,128]{1,0:T(8,128)S(1)} %fusion.3.rest_0_, ...), custom_call_target="tpu_custom_call" | custom-call | flops 1207959552 | tf_op jit(solution)/shard_map/backward/pallas_call | solution.py:606
  78.9 1.4 %collective-permute-start.35 = (f32[8,128]{1,0:T(8,128)S(1)}, f32[8,128]{1,0:T(8,128)S(1)}, u32[]{:S(2)}, u32[]{:S(2)}) collective-permute-start(f32[8,128]{1,0:T(8,128)S(1)} %fusion.2.rest_4_), channel_id=1, source_target_pairs={{0,7},{1,6},{2,5},{3,4},{4,3},{5,2},{6,1},{7,0},{8,15},{9,14},{10,... | collective-permute-start | bytes 12296 | tf_op jit(solution)/shard_map/ppermute | solution.py:620
  80.3 2.4 %collective-permute-start.34 = (f32[8,128]{1,0:T(8,128)S(1)}, f32[8,128]{1,0:T(8,128)S(1)}, u32[]{:S(2)}, u32[]{:S(2)}) collective-permute-start(f32[8,128]{1,0:T(8,128)S(1)} %fusion.2.rest_4_), channel_id=1, source_target_pairs={{0,5},{1,4},{2,7},{3,6},{4,1},{5,0},{6,3},{7,2},{8,13},{9,12},{10,... | collective-permute-start | bytes 12296 | tf_op jit(solution)/shard_map/ppermute | solution.py:620
  82.7 1.8 %collective-permute-start.33 = (f32[8,128]{1,0:T(8,128)S(1)}, f32[8,128]{1,0:T(8,128)S(1)}, u32[]{:S(2)}, u32[]{:S(2)}) collective-permute-start(f32[8,128]{1,0:T(8,128)S(1)} %fusion.2.rest_4_), channel_id=1, source_target_pairs={{0,3},{1,2},{2,1},{3,0},{4,7},{5,6},{6,5},{7,4},{8,11},{9,10},{10,... | collective-permute-start | bytes 12296 | tf_op jit(solution)/shard_map/ppermute | solution.py:620
  84.5 1.9 %weight.6 = (f32[4,144,128]{2,1,0:T(8,128)S(1)}, bf16[4,144,128]{2,1,0:T(8,128)(2,1)S(1)}) custom-call(bf16[4,6,256,128]{3,2,1,0:T(8,128)(2,1)S(1)} %get-tuple-element.109.x, bf16[3,3,4,256,256]{4,3,2,1,0:T(8,128)(2,1)S(1)} %get-tuple-element.123.stack), custom_call_target="tpu_custom_call" | custom-call | flops 1207959552 | tf_op jit(solution)/shard_map/weight/pallas_call | solution.py:606
  86.4 3.0 %backward.4 = (bf16[3,3,4,256,256]{4,3,2,1,0:T(8,128)(2,1)S(1)}, bf16[4,4,256,128]{3,2,1,0:T(8,128)(2,1)S(1)}, f32[4,4,256,128]{3,2,1,0:T(8,128)S(1)}, bf16[1056...) custom-call(f32[8,128]{1,0:T(8,128)S(1)} %fusion.4.rest_0_.rest_8_, ...), custom_call_target="tpu_custom_call" | custom-call | flops 1207959552 | tf_op jit(solution)/shard_map/backward/pallas_call | solution.py:606
  90.2 0.9 collective-permute-start.41
  91.3 2.0 %collective-permute-start.40 = (f32[8,128]{1,0:T(8,128)S(1)}, f32[8,128]{1,0:T(8,128)S(1)}, u32[]{:S(2)}, u32[]{:S(2)}) collective-permute-start(f32[8,128]{1,0:T(8,128)S(1)} %fusion.1.rest_4_), channel_id=1, source_target_pairs={{0,7},{1,6},{2,5},{3,4},{4,3},{5,2},{6,1},{7,0},{8,15},{9,14},{10,... | collective-permute-start | bytes 12296 | tf_op jit(solution)/shard_map/ppermute | solution.py:620
  93.3 1.9 %collective-permute-start.39 = (f32[8,128]{1,0:T(8,128)S(1)}, f32[8,128]{1,0:T(8,128)S(1)}, u32[]{:S(2)}, u32[]{:S(2)}) collective-permute-start(f32[8,128]{1,0:T(8,128)S(1)} %fusion.1.rest_4_), channel_id=1, source_target_pairs={{0,5},{1,4},{2,7},{3,6},{4,1},{5,0},{6,3},{7,2},{8,13},{9,12},{10,... | collective-permute-start | bytes 12296 | tf_op jit(solution)/shard_map/ppermute | solution.py:620
  95.2 1.9 %collective-permute-start.38 = (f32[8,128]{1,0:T(8,128)S(1)}, f32[8,128]{1,0:T(8,128)S(1)}, u32[]{:S(2)}, u32[]{:S(2)}) collective-permute-start(f32[8,128]{1,0:T(8,128)S(1)} %fusion.1.rest_4_), channel_id=1, source_target_pairs={{0,3},{1,2},{2,1},{3,0},{4,7},{5,6},{6,5},{7,4},{8,11},{9,10},{10,... | collective-permute-start | bytes 12296 | tf_op jit(solution)/shard_map/ppermute | solution.py:620
  97.1 1.9 %weight.7 = (f32[4,144,128]{2,1,0:T(8,128)S(1)}, bf16[4,144,128]{2,1,0:T(8,128)(2,1)S(1)}) custom-call(bf16[4,6,256,128]{3,2,1,0:T(8,128)(2,1)S(1)} %get-tuple-element.103.x_in.x, bf16[3,3,4,256,256]{4,3,2,1,0:T(8,128)(2,1)S(1)} %get-tuple-element.131.stack), custom_call_target="tpu_custom_call" | custom-call | flops 1207959552 | tf_op jit(solution)/shard_map/weight/pallas_call | solution.py:606
  99.0 3.0 %backward.5 = (bf16[3,3,4,256,256]{4,3,2,1,0:T(8,128)(2,1)S(1)}, bf16[4,4,256,128]{3,2,1,0:T(8,128)(2,1)S(1)}, f32[4,4,256,128]{3,2,1,0:T(8,128)S(1)}, bf16[1056...) custom-call(f32[8,128]{1,0:T(8,128)S(1)} %fusion.5.rest_0_.rest_8_, ...), custom_call_target="tpu_custom_call" | custom-call | flops 1207959552 | tf_op jit(solution)/shard_map/backward/pallas_call | solution.py:606
  103.9 2.1 %collective-permute-start.45 = (f32[8,128]{1,0:T(8,128)S(1)}, f32[8,128]{1,0:T(8,128)S(1)}, u32[]{:S(2)}, u32[]{:S(2)}) collective-permute-start(f32[8,128]{1,0:T(8,128)S(1)} %fusion.rest_4_), channel_id=1, source_target_pairs={{0,7},{1,6},{2,5},{3,4},{4,3},{5,2},{6,1},{7,0},{8,15},{9,14},{10,... | collective-permute-start | bytes 12296 | tf_op jit(solution)/shard_map/ppermute | solution.py:620
  106.0 1.9 %collective-permute-start.43 = (f32[8,128]{1,0:T(8,128)S(1)}, f32[8,128]{1,0:T(8,128)S(1)}, u32[]{:S(2)}, u32[]{:S(2)}) collective-permute-start(f32[8,128]{1,0:T(8,128)S(1)} %fusion.rest_4_), channel_id=1, source_target_pairs={{0,3},{1,2},{2,1},{3,0},{4,7},{5,6},{6,5},{7,4},{8,11},{9,10},{10,... | collective-permute-start | bytes 12296 | tf_op jit(solution)/shard_map/ppermute | solution.py:620
  107.9 1.9 %weight.8 = (f32[4,144,128]{2,1,0:T(8,128)S(1)}, bf16[4,144,128]{2,1,0:T(8,128)(2,1)S(1)}) custom-call(bf16[4,6,256,128]{3,2,1,0:T(8,128)(2,1)S(1)} %get-tuple-element.97.x_in.x, bf16[3,3,4,256,256]{4,3,2,1,0:T(8,128)(2,1)S(1)} %get-tuple-element.139.stack), custom_call_target="tpu_custom_call" | custom-call | flops 1207959552 | tf_op jit(solution)/shard_map/weight/pallas_call | solution.py:606
  110.1 2.6 %weight.9 = (bf16[3,3,4,256,256]{4,3,2,1,0:T(8,128)(2,1)S(1)}, f32[4,144,128]{2,1,0:T(8,128)S(1)}, bf16[4,144,128]{2,1,0:T(8,128)(2,1)S(1)}, f32[8,128]{1,0:T(8,128)S(1)}) custom-call(f32[8,128]{1,0:T(8,128)S(1)} %fusion.6.rest_0_.rest_8_, f32[8,128]{1,0:T(8,128)S(1)} %collective-permute-done.10.rest_1_.rest_9_, ...), custom_call_target="tpu_custom_call" | custom-call | flops 1207959552 | tf_op jit(solution)/shard_map/weight/pallas_call | solution.py:606
  113.1 1.0 collective-permute-done.46.refs_4_
  114.3 1.6 %collective-permute-start.51 = (bf16[608,128]{1,0:T(8,128)(2,1)S(1)}, bf16[608,128]{1,0:T(8,128)(2,1)S(1)}, u32[]{:S(2)}, u32[]{:S(2)}) collective-permute-start(bf16[608,128]{1,0:T(8,128)(2,1)S(1)} %get-tuple-element.157), channel_id=1, source_target_pairs={{0,8},{8,0},{16,24},{24,16},{1,9},{9,1},{17,25},{25,17},{2,10},{10... | collective-permute-start | bytes 466952 | tf_op jit(solution)/shard_map/ppermute | solution.py:620
  115.9 0.8 collective-permute-start.52
  116.7 1.2 collective-permute-start.53
  118.6 1.5 %neck.1 = bf16[1,4,4,256,128]{4,3,2,1,0:T(8,128)(2,1)} custom-call(bf16[4,6,256,128]{3,2,1,0:T(8,128)(2,1)S(1)} %get-tuple-element.109.x, f32[4,4,256,128]{3,2,1,0:T(8,128)S(1)} %get-tuple-element.153.pre.rows_ref.rest_18_, f32[8,128]{1,0:T(8,128)S(1)} %fusion.3.rest_0_, f32[8,128]{1,0:T(8,128)S(1)} %collective-permute-done.24.rest_1_, ...), custom_call_target="tpu_custom_call" | custom-call | flops 9663676416 | tf_op jit(solution)/shard_map/neck/pallas_call | solution.py:606
  120.1 1.1 collective-permute-done.51.a
  121.2 4.0 %collective-permute-done.52.b = bf16[608,128]{1,0:T(8,128)(2,1)S(1)} collective-permute-done((bf16[608,128]{1,0:T(8,128)(2,1)S(1)}, bf16[608,128]{1,0:T(8,128)(2,1)S(1)}, u32[]{:S(2)}, u32[]{:S(2)}) %collective-permute-start.52) | collective-permute-done | bytes 155680 | tf_op jit(solution)/shard_map/ppermute | solution.py:620
  125.3 1.0 collective-permute-start.54
  126.3 1.7 %collective-permute-start.55 = (bf16[144,128]{1,0:T(8,128)(2,1)S(1)}, bf16[144,128]{1,0:T(8,128)(2,1)S(1)}, u32[]{:S(2)}, u32[]{:S(2)}) collective-permute-start(bf16[144,128]{1,0:T(8,128)(2,1)S(1)} %get-tuple-element.166), channel_id=1, source_target_pairs={{0,4},{1,5},{2,6},{3,7},{4,0},{5,1},{6,2},{7,3},{8,12},{9,13},{10,... | collective-permute-start | bytes 110600 | tf_op jit(solution)/shard_map/ppermute | solution.py:620
  128.1 1.7 %collective-permute-start.56 = (bf16[144,128]{1,0:T(8,128)(2,1)S(1)}, bf16[144,128]{1,0:T(8,128)(2,1)S(1)}, u32[]{:S(2)}, u32[]{:S(2)}) collective-permute-start(bf16[144,128]{1,0:T(8,128)(2,1)S(1)} %get-tuple-element.167), channel_id=1, source_target_pairs={{0,6},{1,7},{2,4},{3,5},{4,2},{5,3},{6,0},{7,1},{8,14},{9,15},{10,... | collective-permute-start | bytes 110600 | tf_op jit(solution)/shard_map/ppermute | solution.py:620
  129.8 3.6 %final_grad.1 = bf16[1,4,4,256,128]{4,3,2,1,0:T(8,128)(2,1)} custom-call(f32[8,128]{1,0:T(8,128)S(1)} %fusion.6.rest_0_.rest_8_, f32[8,128]{1,0:T(8,128)S(1)} %collective-permute-done.10.rest_1_.rest_9_, f32[8,128]{1,0:T(8,128)S(1)} %collective-permute-done.11.rest_2_.rest_10_, f32[8,128]{1,0:T(8,128)S(1)} %collective-permute-done.12.rest_3_.rest_11_, ...), custom_call_target="tpu_custom_call" | custom-call | flops 1207959552 | tf_op jit(solution)/shard_map/final_grad/pallas_call | solution.py:606
  (107 shorter events, 15.9 us)
Async XLA Ops:
  0.6 16.0 %copy-start.3 = (s32[4,4,4,256]{3,2,1,0:T(4,128)S(1)}, s32[4,4,4,256]{3,2,1,0:T(4,128)}, u32[]{:S(2)}) copy-start(s32[4,4,4,256]{3,2,1,0:T(4,128)} %mask.3) | copy-start | bytes 196612
  0.6 15.8 %copy-start.5 = (f32[1,128]{1,0:T(1,128)S(1)}, f32[1,128]{1,0:T(1,128)}, u32[]{:S(2)}) copy-start(f32[1,128]{1,0:T(1,128)} %bias.3) | copy-start | bytes 1540
  0.7 15.8 %copy-start.4 = (f32[1,128]{1,0:T(1,128)S(1)}, f32[1,128]{1,0:T(1,128)}, u32[]{:S(2)}) copy-start(f32[1,128]{1,0:T(1,128)} %gain.3) | copy-start | bytes 1540
  0.7 15.8 %copy-start.1 = (bf16[1,1152,128]{2,1,0:T(8,128)(2,1)S(1)}, bf16[1,1152,128]{2,1,0:T(8,128)(2,1)}, u32[]{:S(2)}) copy-start(bf16[1,1152,128]{2,1,0:T(8,128)(2,1)} %own.1) | copy-start | bytes 884740
  0.7 15.9 %copy-start.2 = (bf16[1,4,4,256,128]{4,3,2,1,0:T(8,128)(2,1)S(1)}, bf16[1,4,4,256,128]{4,3,2,1,0:T(8,128)(2,1)}, u32[]{:S(2)}) copy-start(bf16[1,4,4,256,128]{4,3,2,1,0:T(8,128)(2,1)} %features.3) | copy-start | bytes 3145732
  2.7 13.8 %collective-permute-start = (bf16[2048,128]{1,0:T(8,128)(2,1)S(1)}, bf16[2048,128]{1,0:T(8,128)(2,1)S(1)}, u32[]{:S(2)}, u32[]{:S(2)}) collective-permute-start(bf16[2048,128]{1,0:T(8,128)(2,1)S(1)} %get-tuple-element.88), channel_id=1, source_target_pairs={{0,1},{1,0},{2,3},{3,2},{4,5},{5,4},{6,7},{7,6},{8,9},{9,8},{10,11... | collective-permute-start | bytes 1572872 | tf_op jit(solution)/shard_map/ppermute | solution.py:620
  3.3 8.4 %collective-permute-start.4 = (bf16[608,128]{1,0:T(8,128)(2,1)S(1)}, bf16[608,128]{1,0:T(8,128)(2,1)S(1)}, u32[]{:S(2)}, u32[]{:S(2)}) collective-permute-start(bf16[608,128]{1,0:T(8,128)(2,1)S(1)} %get-tuple-element.90), channel_id=1, source_target_pairs={{0,24},{8,16},{16,8},{24,0},{1,25},{9,17},{17,9},{25,1},{2,26},{10... | collective-permute-start | bytes 466952 | tf_op jit(solution)/shard_map/ppermute | solution.py:620
  6.8 8.0 %collective-permute-start.3 = (bf16[608,128]{1,0:T(8,128)(2,1)S(1)}, bf16[608,128]{1,0:T(8,128)(2,1)S(1)}, u32[]{:S(2)}, u32[]{:S(2)}) collective-permute-start(bf16[608,128]{1,0:T(8,128)(2,1)S(1)} %get-tuple-element.90), channel_id=1, source_target_pairs={{0,16},{8,24},{16,0},{24,8},{1,17},{9,25},{17,1},{25,9},{2,18},{10... | collective-permute-start | bytes 466952 | tf_op jit(solution)/shard_map/ppermute | solution.py:620
  7.3 7.8 %collective-permute-start.2 = (bf16[608,128]{1,0:T(8,128)(2,1)S(1)}, bf16[608,128]{1,0:T(8,128)(2,1)S(1)}, u32[]{:S(2)}, u32[]{:S(2)}) collective-permute-start(bf16[608,128]{1,0:T(8,128)(2,1)S(1)} %get-tuple-element.90), channel_id=1, source_target_pairs={{0,8},{8,0},{16,24},{24,16},{1,9},{9,1},{17,25},{25,17},{2,10},{10... | collective-permute-start | bytes 466952 | tf_op jit(solution)/shard_map/ppermute | solution.py:620
  7.4 9.1 %collective-permute-start.1 = (bf16[1024,128]{1,0:T(8,128)(2,1)S(1)}, bf16[1024,128]{1,0:T(8,128)(2,1)S(1)}, u32[]{:S(2)}, u32[]{:S(2)}) collective-permute-start(bf16[1024,128]{1,0:T(8,128)(2,1)S(1)} %get-tuple-element.89), channel_id=1, source_target_pairs={{1,2},{2,1},{3,4},{4,3},{5,6},{6,5},{9,10},{10,9},{11,12},{12,11},... | collective-permute-start | bytes 786440 | tf_op jit(solution)/shard_map/ppermute | solution.py:627
  11.7 3.6 %collective-permute-start.7 = (bf16[608,128]{1,0:T(8,128)(2,1)S(1)}, bf16[608,128]{1,0:T(8,128)(2,1)S(1)}, u32[]{:S(2)}, u32[]{:S(2)}) collective-permute-start(bf16[608,128]{1,0:T(8,128)(2,1)S(1)} %collective-permute-done.4.r3), channel_id=1, source_target_pairs={{0,1},{1,0},{2,3},{3,2},{4,5},{5,4},{6,7},{7,6},{8,9},{9,8},{10,11... | collective-permute-start | bytes 466952 | tf_op jit(solution)/shard_map/ppermute | solution.py:620
  14.7 1.4 %collective-permute-start.6 = (bf16[608,128]{1,0:T(8,128)(2,1)S(1)}, bf16[608,128]{1,0:T(8,128)(2,1)S(1)}, u32[]{:S(2)}, u32[]{:S(2)}) collective-permute-start(bf16[608,128]{1,0:T(8,128)(2,1)S(1)} %collective-permute-done.3.r2), channel_id=1, source_target_pairs={{0,1},{1,0},{2,3},{3,2},{4,5},{5,4},{6,7},{7,6},{8,9},{9,8},{10,11... | collective-permute-start | bytes 466952 | tf_op jit(solution)/shard_map/ppermute | solution.py:620
  15.0 1.4 %collective-permute-start.5 = (bf16[608,128]{1,0:T(8,128)(2,1)S(1)}, bf16[608,128]{1,0:T(8,128)(2,1)S(1)}, u32[]{:S(2)}, u32[]{:S(2)}) collective-permute-start(bf16[608,128]{1,0:T(8,128)(2,1)S(1)} %collective-permute-done.2.r1), channel_id=1, source_target_pairs={{0,1},{1,0},{2,3},{3,2},{4,5},{5,4},{6,7},{7,6},{8,9},{9,8},{10,11... | collective-permute-start | bytes 466952 | tf_op jit(solution)/shard_map/ppermute | solution.py:620
  19.3 1.6 %collective-permute-start.8 = (bf16[1056,128]{1,0:T(8,128)(2,1)S(1)}, bf16[1056,128]{1,0:T(8,128)(2,1)S(1)}, u32[]{:S(2)}, u32[]{:S(2)}) collective-permute-start(bf16[1056,128]{1,0:T(8,128)(2,1)S(1)} %get-tuple-element.94), channel_id=1, source_target_pairs={{0,1},{1,0},{2,3},{3,2},{4,5},{5,4},{6,7},{7,6},{8,9},{9,8},{10,11... | collective-permute-start | bytes 811016 | tf_op jit(solution)/shard_map/ppermute | solution.py:620
  19.6 7.6 %collective-permute-start.9 = (bf16[1024,128]{1,0:T(8,128)(2,1)S(1)}, bf16[1024,128]{1,0:T(8,128)(2,1)S(1)}, u32[]{:S(2)}, u32[]{:S(2)}) collective-permute-start(bf16[1024,128]{1,0:T(8,128)(2,1)S(1)} %far.7), channel_id=1, source_target_pairs={{1,2},{2,1},{3,4},{4,3},{5,6},{6,5},{9,10},{10,9},{11,12},{12,11},... | collective-permute-start | bytes 786440 | tf_op jit(solution)/shard_map/ppermute | solution.py:627
  20.9 6.3 %collective-permute-start.12 = (f32[8,128]{1,0:T(8,128)S(1)}, f32[8,128]{1,0:T(8,128)S(1)}, u32[]{:S(2)}, u32[]{:S(2)}) collective-permute-start(f32[8,128]{1,0:T(8,128)S(1)} %fusion.6.rest_0_.rest_8_), channel_id=1, source_target_pairs={{0,7},{1,6},{2,5},{3,4},{4,3},{5,2},{6,1},{7,0},{8,15},{9,14},{10,... | collective-permute-start | bytes 12296 | tf_op jit(solution)/shard_map/ppermute | solution.py:620
  24.5 4.0 %collective-permute-start.11 = (f32[8,128]{1,0:T(8,128)S(1)}, f32[8,128]{1,0:T(8,128)S(1)}, u32[]{:S(2)}, u32[]{:S(2)}) collective-permute-start(f32[8,128]{1,0:T(8,128)S(1)} %fusion.6.rest_0_.rest_8_), channel_id=1, source_target_pairs={{0,5},{1,4},{2,7},{3,6},{4,1},{5,0},{6,3},{7,2},{8,13},{9,12},{10,... | collective-permute-start | bytes 12296 | tf_op jit(solution)/shard_map/ppermute | solution.py:620
  25.8 3.0 %collective-permute-start.10 = (f32[8,128]{1,0:T(8,128)S(1)}, f32[8,128]{1,0:T(8,128)S(1)}, u32[]{:S(2)}, u32[]{:S(2)}) collective-permute-start(f32[8,128]{1,0:T(8,128)S(1)} %fusion.6.rest_0_.rest_8_), channel_id=1, source_target_pairs={{0,3},{1,2},{2,1},{3,0},{4,7},{5,6},{6,5},{7,4},{8,11},{9,10},{10,... | collective-permute-start | bytes 12296 | tf_op jit(solution)/shard_map/ppermute | solution.py:620
  32.0 2.3 %collective-permute-start.13 = (bf16[1056,128]{1,0:T(8,128)(2,1)S(1)}, bf16[1056,128]{1,0:T(8,128)(2,1)S(1)}, u32[]{:S(2)}, u32[]{:S(2)}) collective-permute-start(bf16[1056,128]{1,0:T(8,128)(2,1)S(1)} %get-tuple-element.99), channel_id=1, source_target_pairs={{0,1},{1,0},{2,3},{3,2},{4,5},{5,4},{6,7},{7,6},{8,9},{9,8},{10,11... | collective-permute-start | bytes 811016 | tf_op jit(solution)/shard_map/ppermute | solution.py:620
  33.1 7.6 %collective-permute-start.14 = (bf16[1024,128]{1,0:T(8,128)(2,1)S(1)}, bf16[1024,128]{1,0:T(8,128)(2,1)S(1)}, u32[]{:S(2)}, u32[]{:S(2)}) collective-permute-start(bf16[1024,128]{1,0:T(8,128)(2,1)S(1)} %far.8), channel_id=1, source_target_pairs={{1,2},{2,1},{3,4},{4,3},{5,6},{6,5},{9,10},{10,9},{11,12},{12,11},... | collective-permute-start | bytes 786440 | tf_op jit(solution)/shard_map/ppermute | solution.py:627
  34.2 6.4 %collective-permute-start.17 = (f32[8,128]{1,0:T(8,128)S(1)}, f32[8,128]{1,0:T(8,128)S(1)}, u32[]{:S(2)}, u32[]{:S(2)}) collective-permute-start(f32[8,128]{1,0:T(8,128)S(1)} %fusion.5.rest_0_.rest_8_), channel_id=1, source_target_pairs={{0,7},{1,6},{2,5},{3,4},{4,3},{5,2},{6,1},{7,0},{8,15},{9,14},{10,... | collective-permute-start | bytes 12296 | tf_op jit(solution)/shard_map/ppermute | solution.py:620
  36.1 4.5 %collective-permute-start.16 = (f32[8,128]{1,0:T(8,128)S(1)}, f32[8,128]{1,0:T(8,128)S(1)}, u32[]{:S(2)}, u32[]{:S(2)}) collective-permute-start(f32[8,128]{1,0:T(8,128)S(1)} %fusion.5.rest_0_.rest_8_), channel_id=1, source_target_pairs={{0,5},{1,4},{2,7},{3,6},{4,1},{5,0},{6,3},{7,2},{8,13},{9,12},{10,... | collective-permute-start | bytes 12296 | tf_op jit(solution)/shard_map/ppermute | solution.py:620
  37.9 3.2 %collective-permute-start.15 = (f32[8,128]{1,0:T(8,128)S(1)}, f32[8,128]{1,0:T(8,128)S(1)}, u32[]{:S(2)}, u32[]{:S(2)}) collective-permute-start(f32[8,128]{1,0:T(8,128)S(1)} %fusion.5.rest_0_.rest_8_), channel_id=1, source_target_pairs={{0,3},{1,2},{2,1},{3,0},{4,7},{5,6},{6,5},{7,4},{8,11},{9,10},{10,... | collective-permute-start | bytes 12296 | tf_op jit(solution)/shard_map/ppermute | solution.py:620
  44.0 2.5 %collective-permute-start.18 = (bf16[1056,128]{1,0:T(8,128)(2,1)S(1)}, bf16[1056,128]{1,0:T(8,128)(2,1)S(1)}, u32[]{:S(2)}, u32[]{:S(2)}) collective-permute-start(bf16[1056,128]{1,0:T(8,128)(2,1)S(1)} %get-tuple-element.105), channel_id=1, source_target_pairs={{0,1},{1,0},{2,3},{3,2},{4,5},{5,4},{6,7},{7,6},{8,9},{9,8},{10,11... | collective-permute-start | bytes 811016 | tf_op jit(solution)/shard_map/ppermute | solution.py:620
  45.3 7.6 %collective-permute-start.19 = (bf16[1024,128]{1,0:T(8,128)(2,1)S(1)}, bf16[1024,128]{1,0:T(8,128)(2,1)S(1)}, u32[]{:S(2)}, u32[]{:S(2)}) collective-permute-start(bf16[1024,128]{1,0:T(8,128)(2,1)S(1)} %far.9), channel_id=1, source_target_pairs={{1,2},{2,1},{3,4},{4,3},{5,6},{6,5},{9,10},{10,9},{11,12},{12,11},... | collective-permute-start | bytes 786440 | tf_op jit(solution)/shard_map/ppermute | solution.py:627
  46.5 6.5 %collective-permute-start.22 = (f32[8,128]{1,0:T(8,128)S(1)}, f32[8,128]{1,0:T(8,128)S(1)}, u32[]{:S(2)}, u32[]{:S(2)}) collective-permute-start(f32[8,128]{1,0:T(8,128)S(1)} %fusion.4.rest_0_.rest_8_), channel_id=1, source_target_pairs={{0,7},{1,6},{2,5},{3,4},{4,3},{5,2},{6,1},{7,0},{8,15},{9,14},{10,... | collective-permute-start | bytes 12296 | tf_op jit(solution)/shard_map/ppermute | solution.py:620
  47.9 5.1 %collective-permute-start.21 = (f32[8,128]{1,0:T(8,128)S(1)}, f32[8,128]{1,0:T(8,128)S(1)}, u32[]{:S(2)}, u32[]{:S(2)}) collective-permute-start(f32[8,128]{1,0:T(8,128)S(1)} %fusion.4.rest_0_.rest_8_), channel_id=1, source_target_pairs={{0,5},{1,4},{2,7},{3,6},{4,1},{5,0},{6,3},{7,2},{8,13},{9,12},{10,... | collective-permute-start | bytes 12296 | tf_op jit(solution)/shard_map/ppermute | solution.py:620
  50.4 3.1 %collective-permute-start.20 = (f32[8,128]{1,0:T(8,128)S(1)}, f32[8,128]{1,0:T(8,128)S(1)}, u32[]{:S(2)}, u32[]{:S(2)}) collective-permute-start(f32[8,128]{1,0:T(8,128)S(1)} %fusion.4.rest_0_.rest_8_), channel_id=1, source_target_pairs={{0,3},{1,2},{2,1},{3,0},{4,7},{5,6},{6,5},{7,4},{8,11},{9,10},{10,... | collective-permute-start | bytes 12296 | tf_op jit(solution)/shard_map/ppermute | solution.py:620
  56.4 2.4 %collective-permute-start.23 = (bf16[1056,128]{1,0:T(8,128)(2,1)S(1)}, bf16[1056,128]{1,0:T(8,128)(2,1)S(1)}, u32[]{:S(2)}, u32[]{:S(2)}) collective-permute-start(bf16[1056,128]{1,0:T(8,128)(2,1)S(1)} %get-tuple-element.112), channel_id=1, source_target_pairs={{0,1},{1,0},{2,3},{3,2},{4,5},{5,4},{6,7},{7,6},{8,9},{9,8},{10,11... | collective-permute-start | bytes 811016 | tf_op jit(solution)/shard_map/ppermute | solution.py:620
  58.9 5.7 %collective-permute-start.26 = (f32[8,128]{1,0:T(8,128)S(1)}, f32[8,128]{1,0:T(8,128)S(1)}, u32[]{:S(2)}, u32[]{:S(2)}) collective-permute-start(f32[8,128]{1,0:T(8,128)S(1)} %fusion.3.rest_0_), channel_id=1, source_target_pairs={{0,7},{1,6},{2,5},{3,4},{4,3},{5,2},{6,1},{7,0},{8,15},{9,14},{10,... | collective-permute-start | bytes 12296 | tf_op jit(solution)/shard_map/ppermute | solution.py:620
  60.3 4.3 %collective-permute-start.25 = (f32[8,128]{1,0:T(8,128)S(1)}, f32[8,128]{1,0:T(8,128)S(1)}, u32[]{:S(2)}, u32[]{:S(2)}) collective-permute-start(f32[8,128]{1,0:T(8,128)S(1)} %fusion.3.rest_0_), channel_id=1, source_target_pairs={{0,5},{1,4},{2,7},{3,6},{4,1},{5,0},{6,3},{7,2},{8,13},{9,12},{10,... | collective-permute-start | bytes 12296 | tf_op jit(solution)/shard_map/ppermute | solution.py:620
  61.0 3.7 %collective-permute-start.24 = (f32[8,128]{1,0:T(8,128)S(1)}, f32[8,128]{1,0:T(8,128)S(1)}, u32[]{:S(2)}, u32[]{:S(2)}) collective-permute-start(f32[8,128]{1,0:T(8,128)S(1)} %fusion.3.rest_0_), channel_id=1, source_target_pairs={{0,3},{1,2},{2,1},{3,0},{4,7},{5,6},{6,5},{7,4},{8,11},{9,10},{10,... | collective-permute-start | bytes 12296 | tf_op jit(solution)/shard_map/ppermute | solution.py:620
  63.0 1.6 %copy-start = (bf16[1,4,4,256,128]{4,3,2,1,0:T(8,128)(2,1)S(1)}, bf16[1,4,4,256,128]{4,3,2,1,0:T(8,128)(2,1)}, u32[]{:S(2)}) copy-start(bf16[1,4,4,256,128]{4,3,2,1,0:T(8,128)(2,1)} %rest_15_.1) | copy-start | bytes 3145732
  63.0 11.2 %collective-permute-start.31 = (bf16[2048,128]{1,0:T(8,128)(2,1)S(1)}, bf16[2048,128]{1,0:T(8,128)(2,1)S(1)}, u32[]{:S(2)}, u32[]{:S(2)}) collective-permute-start(bf16[2048,128]{1,0:T(8,128)(2,1)S(1)} %far.10), channel_id=1, source_target_pairs={{1,2},{2,1},{3,4},{4,3},{5,6},{6,5},{9,10},{10,9},{11,12},{12,11},... | collective-permute-start | bytes 1572872 | tf_op jit(solution)/shard_map/ppermute | solution.py:627
  65.7 2.3 %collective-permute-start.27 = (f32[8,128]{1,0:T(8,128)S(1)}, f32[8,128]{1,0:T(8,128)S(1)}, u32[]{:S(2)}, u32[]{:S(2)}) collective-permute-start(f32[8,128]{1,0:T(8,128)S(1)} %get-tuple-element.115), channel_id=1, source_target_pairs={{0,1},{1,0},{2,3},{3,2},{4,5},{5,4},{6,7},{7,6},{8,9},{9,8},{10,11... | collective-permute-start | bytes 12296 | tf_op jit(solution)/shard_map/ppermute | solution.py:620
  68.0 4.9 %collective-permute-start.30 = (f32[8,128]{1,0:T(8,128)S(1)}, f32[8,128]{1,0:T(8,128)S(1)}, u32[]{:S(2)}, u32[]{:S(2)}) collective-permute-start(f32[8,128]{1,0:T(8,128)S(1)} %add.78.rest_4_), channel_id=1, source_target_pairs={{0,7},{1,6},{2,5},{3,4},{4,3},{5,2},{6,1},{7,0},{8,15},{9,14},{10,... | collective-permute-start | bytes 12296 | tf_op jit(solution)/shard_map/ppermute | solution.py:620
  70.2 3.9 %collective-permute-start.29 = (f32[8,128]{1,0:T(8,128)S(1)}, f32[8,128]{1,0:T(8,128)S(1)}, u32[]{:S(2)}, u32[]{:S(2)}) collective-permute-start(f32[8,128]{1,0:T(8,128)S(1)} %add.78.rest_4_), channel_id=1, source_target_pairs={{0,5},{1,4},{2,7},{3,6},{4,1},{5,0},{6,3},{7,2},{8,13},{9,12},{10,... | collective-permute-start | bytes 12296 | tf_op jit(solution)/shard_map/ppermute | solution.py:620
  71.1 3.1 %collective-permute-start.28 = (f32[8,128]{1,0:T(8,128)S(1)}, f32[8,128]{1,0:T(8,128)S(1)}, u32[]{:S(2)}, u32[]{:S(2)}) collective-permute-start(f32[8,128]{1,0:T(8,128)S(1)} %add.78.rest_4_), channel_id=1, source_target_pairs={{0,3},{1,2},{2,1},{3,0},{4,7},{5,6},{6,5},{7,4},{8,11},{9,10},{10,... | collective-permute-start | bytes 12296 | tf_op jit(solution)/shard_map/ppermute | solution.py:620
  77.3 1.6 %collective-permute-start.32 = (bf16[1056,128]{1,0:T(8,128)(2,1)S(1)}, bf16[1056,128]{1,0:T(8,128)(2,1)S(1)}, u32[]{:S(2)}, u32[]{:S(2)}) collective-permute-start(bf16[1056,128]{1,0:T(8,128)(2,1)S(1)} %get-tuple-element.121), channel_id=1, source_target_pairs={{0,1},{1,0},{2,3},{3,2},{4,5},{5,4},{6,7},{7,6},{8,9},{9,8},{10,11... | collective-permute-start | bytes 811016 | tf_op jit(solution)/shard_map/ppermute | solution.py:620
  77.8 8.6 %collective-permute-start.36 = (bf16[1024,128]{1,0:T(8,128)(2,1)S(1)}, bf16[1024,128]{1,0:T(8,128)(2,1)S(1)}, u32[]{:S(2)}, u32[]{:S(2)}) collective-permute-start(bf16[1024,128]{1,0:T(8,128)(2,1)S(1)} %far.11), channel_id=1, source_target_pairs={{1,2},{2,1},{3,4},{4,3},{5,6},{6,5},{9,10},{10,9},{11,12},{12,11},... | collective-permute-start | bytes 786440 | tf_op jit(solution)/shard_map/ppermute | solution.py:627
  78.9 7.5 %collective-permute-start.35 = (f32[8,128]{1,0:T(8,128)S(1)}, f32[8,128]{1,0:T(8,128)S(1)}, u32[]{:S(2)}, u32[]{:S(2)}) collective-permute-start(f32[8,128]{1,0:T(8,128)S(1)} %fusion.2.rest_4_), channel_id=1, source_target_pairs={{0,7},{1,6},{2,5},{3,4},{4,3},{5,2},{6,1},{7,0},{8,15},{9,14},{10,... | collective-permute-start | bytes 12296 | tf_op jit(solution)/shard_map/ppermute | solution.py:620
  80.3 6.1 %collective-permute-start.34 = (f32[8,128]{1,0:T(8,128)S(1)}, f32[8,128]{1,0:T(8,128)S(1)}, u32[]{:S(2)}, u32[]{:S(2)}) collective-permute-start(f32[8,128]{1,0:T(8,128)S(1)} %fusion.2.rest_4_), channel_id=1, source_target_pairs={{0,5},{1,4},{2,7},{3,6},{4,1},{5,0},{6,3},{7,2},{8,13},{9,12},{10,... | collective-permute-start | bytes 12296 | tf_op jit(solution)/shard_map/ppermute | solution.py:620
  82.7 3.7 %collective-permute-start.33 = (f32[8,128]{1,0:T(8,128)S(1)}, f32[8,128]{1,0:T(8,128)S(1)}, u32[]{:S(2)}, u32[]{:S(2)}) collective-permute-start(f32[8,128]{1,0:T(8,128)S(1)} %fusion.2.rest_4_), channel_id=1, source_target_pairs={{0,3},{1,2},{2,1},{3,0},{4,7},{5,6},{6,5},{7,4},{8,11},{9,10},{10,... | collective-permute-start | bytes 12296 | tf_op jit(solution)/shard_map/ppermute | solution.py:620
  89.5 1.9 %collective-permute-start.37 = (bf16[1056,128]{1,0:T(8,128)(2,1)S(1)}, bf16[1056,128]{1,0:T(8,128)(2,1)S(1)}, u32[]{:S(2)}, u32[]{:S(2)}) collective-permute-start(bf16[1056,128]{1,0:T(8,128)(2,1)S(1)} %get-tuple-element.129), channel_id=1, source_target_pairs={{0,1},{1,0},{2,3},{3,2},{4,5},{5,4},{6,7},{7,6},{8,9},{9,8},{10,11... | collective-permute-start | bytes 811016 | tf_op jit(solution)/shard_map/ppermute | solution.py:620
  90.2 8.8 %collective-permute-start.41 = (bf16[1024,128]{1,0:T(8,128)(2,1)S(1)}, bf16[1024,128]{1,0:T(8,128)(2,1)S(1)}, u32[]{:S(2)}, u32[]{:S(2)}) collective-permute-start(bf16[1024,128]{1,0:T(8,128)(2,1)S(1)} %far.12), channel_id=1, source_target_pairs={{1,2},{2,1},{3,4},{4,3},{5,6},{6,5},{9,10},{10,9},{11,12},{12,11},... | collective-permute-start | bytes 786440 | tf_op jit(solution)/shard_map/ppermute | solution.py:627
  91.3 7.7 %collective-permute-start.40 = (f32[8,128]{1,0:T(8,128)S(1)}, f32[8,128]{1,0:T(8,128)S(1)}, u32[]{:S(2)}, u32[]{:S(2)}) collective-permute-start(f32[8,128]{1,0:T(8,128)S(1)} %fusion.1.rest_4_), channel_id=1, source_target_pairs={{0,7},{1,6},{2,5},{3,4},{4,3},{5,2},{6,1},{7,0},{8,15},{9,14},{10,... | collective-permute-start | bytes 12296 | tf_op jit(solution)/shard_map/ppermute | solution.py:620
  93.3 5.7 %collective-permute-start.39 = (f32[8,128]{1,0:T(8,128)S(1)}, f32[8,128]{1,0:T(8,128)S(1)}, u32[]{:S(2)}, u32[]{:S(2)}) collective-permute-start(f32[8,128]{1,0:T(8,128)S(1)} %fusion.1.rest_4_), channel_id=1, source_target_pairs={{0,5},{1,4},{2,7},{3,6},{4,1},{5,0},{6,3},{7,2},{8,13},{9,12},{10,... | collective-permute-start | bytes 12296 | tf_op jit(solution)/shard_map/ppermute | solution.py:620
  95.2 3.8 %collective-permute-start.38 = (f32[8,128]{1,0:T(8,128)S(1)}, f32[8,128]{1,0:T(8,128)S(1)}, u32[]{:S(2)}, u32[]{:S(2)}) collective-permute-start(f32[8,128]{1,0:T(8,128)S(1)} %fusion.1.rest_4_), channel_id=1, source_target_pairs={{0,3},{1,2},{2,1},{3,0},{4,7},{5,6},{6,5},{7,4},{8,11},{9,10},{10,... | collective-permute-start | bytes 12296 | tf_op jit(solution)/shard_map/ppermute | solution.py:620
  102.1 1.8 %collective-permute-start.42 = (bf16[1056,128]{1,0:T(8,128)(2,1)S(1)}, bf16[1056,128]{1,0:T(8,128)(2,1)S(1)}, u32[]{:S(2)}, u32[]{:S(2)}) collective-permute-start(bf16[1056,128]{1,0:T(8,128)(2,1)S(1)} %get-tuple-element.137), channel_id=1, source_target_pairs={{0,1},{1,0},{2,3},{3,2},{4,5},{5,4},{6,7},{7,6},{8,9},{9,8},{10,11... | collective-permute-start | bytes 811016 | tf_op jit(solution)/shard_map/ppermute | solution.py:620
  102.7 10.5 %collective-permute-start.49 = (bf16[4,144,128]{2,1,0:T(8,128)(2,1)S(1)}, bf16[4,144,128]{2,1,0:T(8,128)(2,1)S(1)}, u32[]{:S(2)}, u32[]{:S(2)}) collective-permute-start(bf16[4,144,128]{2,1,0:T(8,128)(2,1)S(1)} %get-tuple-element.124), channel_id=1, source_target_pairs={{0,1},{1,0},{2,3},{3,2},{4,5},{5,4},{6,7},{7,6},{8,9},{9,8},{10,11... | collective-permute-start | bytes 442376 | tf_op jit(solution)/shard_map/ppermute | solution.py:620
  102.7 10.4 %collective-permute-start.48 = (bf16[4,144,128]{2,1,0:T(8,128)(2,1)S(1)}, bf16[4,144,128]{2,1,0:T(8,128)(2,1)S(1)}, u32[]{:S(2)}, u32[]{:S(2)}) collective-permute-start(bf16[4,144,128]{2,1,0:T(8,128)(2,1)S(1)} %get-tuple-element.132), channel_id=1, source_target_pairs={{0,1},{1,0},{2,3},{3,2},{4,5},{5,4},{6,7},{7,6},{8,9},{9,8},{10,11... | collective-permute-start | bytes 442376 | tf_op jit(solution)/shard_map/ppermute | solution.py:620
  103.9 6.0 %collective-permute-start.45 = (f32[8,128]{1,0:T(8,128)S(1)}, f32[8,128]{1,0:T(8,128)S(1)}, u32[]{:S(2)}, u32[]{:S(2)}) collective-permute-start(f32[8,128]{1,0:T(8,128)S(1)} %fusion.rest_4_), channel_id=1, source_target_pairs={{0,7},{1,6},{2,5},{3,4},{4,3},{5,2},{6,1},{7,0},{8,15},{9,14},{10,... | collective-permute-start | bytes 12296 | tf_op jit(solution)/shard_map/ppermute | solution.py:620
  106.0 4.1 %collective-permute-start.44 = (f32[8,128]{1,0:T(8,128)S(1)}, f32[8,128]{1,0:T(8,128)S(1)}, u32[]{:S(2)}, u32[]{:S(2)}) collective-permute-start(f32[8,128]{1,0:T(8,128)S(1)} %fusion.rest_4_), channel_id=1, source_target_pairs={{0,5},{1,4},{2,7},{3,6},{4,1},{5,0},{6,3},{7,2},{8,13},{9,12},{10,... | collective-permute-start | bytes 12296 | tf_op jit(solution)/shard_map/ppermute | solution.py:620
  106.0 4.1 %collective-permute-start.43 = (f32[8,128]{1,0:T(8,128)S(1)}, f32[8,128]{1,0:T(8,128)S(1)}, u32[]{:S(2)}, u32[]{:S(2)}) collective-permute-start(f32[8,128]{1,0:T(8,128)S(1)} %fusion.rest_4_), channel_id=1, source_target_pairs={{0,3},{1,2},{2,1},{3,0},{4,7},{5,6},{6,5},{7,4},{8,11},{9,10},{10,... | collective-permute-start | bytes 12296 | tf_op jit(solution)/shard_map/ppermute | solution.py:620
  109.8 3.3 %collective-permute-start.47 = (bf16[4,144,128]{2,1,0:T(8,128)(2,1)S(1)}, bf16[4,144,128]{2,1,0:T(8,128)(2,1)S(1)}, u32[]{:S(2)}, u32[]{:S(2)}) collective-permute-start(bf16[4,144,128]{2,1,0:T(8,128)(2,1)S(1)} %get-tuple-element.140), channel_id=1, source_target_pairs={{0,1},{1,0},{2,3},{3,2},{4,5},{5,4},{6,7},{7,6},{8,9},{9,8},{10,11... | collective-permute-start | bytes 442376 | tf_op jit(solution)/shard_map/ppermute | solution.py:620
  112.7 1.4 %collective-permute-start.46 = (bf16[4,144,128]{2,1,0:T(8,128)(2,1)S(1)}, bf16[4,144,128]{2,1,0:T(8,128)(2,1)S(1)}, u32[]{:S(2)}, u32[]{:S(2)}) collective-permute-start(bf16[4,144,128]{2,1,0:T(8,128)(2,1)S(1)} %get-tuple-element.147), channel_id=1, source_target_pairs={{0,1},{1,0},{2,3},{3,2},{4,5},{5,4},{6,7},{7,6},{8,9},{9,8},{10,11... | collective-permute-start | bytes 442376 | tf_op jit(solution)/shard_map/ppermute | solution.py:620
  114.3 6.9 %collective-permute-start.51 = (bf16[608,128]{1,0:T(8,128)(2,1)S(1)}, bf16[608,128]{1,0:T(8,128)(2,1)S(1)}, u32[]{:S(2)}, u32[]{:S(2)}) collective-permute-start(bf16[608,128]{1,0:T(8,128)(2,1)S(1)} %get-tuple-element.157), channel_id=1, source_target_pairs={{0,8},{8,0},{16,24},{24,16},{1,9},{9,1},{17,25},{25,17},{2,10},{10... | collective-permute-start | bytes 466952 | tf_op jit(solution)/shard_map/ppermute | solution.py:620
  115.9 9.3 %collective-permute-start.52 = (bf16[608,128]{1,0:T(8,128)(2,1)S(1)}, bf16[608,128]{1,0:T(8,128)(2,1)S(1)}, u32[]{:S(2)}, u32[]{:S(2)}) collective-permute-start(bf16[608,128]{1,0:T(8,128)(2,1)S(1)} %get-tuple-element.159), channel_id=1, source_target_pairs={{0,16},{8,24},{16,0},{24,8},{1,17},{9,25},{17,1},{25,9},{2,18},{10... | collective-permute-start | bytes 466952 | tf_op jit(solution)/shard_map/ppermute | solution.py:620
  116.7 8.5 %collective-permute-start.53 = (bf16[608,128]{1,0:T(8,128)(2,1)S(1)}, bf16[608,128]{1,0:T(8,128)(2,1)S(1)}, u32[]{:S(2)}, u32[]{:S(2)}) collective-permute-start(bf16[608,128]{1,0:T(8,128)(2,1)S(1)} %get-tuple-element.160), channel_id=1, source_target_pairs={{0,24},{8,16},{16,8},{24,0},{1,25},{9,17},{17,9},{25,1},{2,26},{10... | collective-permute-start | bytes 466952 | tf_op jit(solution)/shard_map/ppermute | solution.py:620
  117.9 11.9 %collective-permute-start.50 = (bf16[1024,128]{1,0:T(8,128)(2,1)S(1)}, bf16[1024,128]{1,0:T(8,128)(2,1)S(1)}, u32[]{:S(2)}, u32[]{:S(2)}) collective-permute-start(bf16[1024,128]{1,0:T(8,128)(2,1)S(1)} %far.13), channel_id=1, source_target_pairs={{1,2},{2,1},{3,4},{4,3},{5,6},{6,5},{9,10},{10,9},{11,12},{12,11},... | collective-permute-start | bytes 786440 | tf_op jit(solution)/shard_map/ppermute | solution.py:627
  125.3 8.1 %collective-permute-start.54 = (bf16[144,128]{1,0:T(8,128)(2,1)S(1)}, bf16[144,128]{1,0:T(8,128)(2,1)S(1)}, u32[]{:S(2)}, u32[]{:S(2)}) collective-permute-start(bf16[144,128]{1,0:T(8,128)(2,1)S(1)} %get-tuple-element.165), channel_id=1, source_target_pairs={{0,2},{1,3},{2,0},{3,1},{4,6},{5,7},{6,4},{7,5},{8,10},{9,11},{10,... | collective-permute-start | bytes 110600 | tf_op jit(solution)/shard_map/ppermute | solution.py:620
  126.3 7.1 %collective-permute-start.55 = (bf16[144,128]{1,0:T(8,128)(2,1)S(1)}, bf16[144,128]{1,0:T(8,128)(2,1)S(1)}, u32[]{:S(2)}, u32[]{:S(2)}) collective-permute-start(bf16[144,128]{1,0:T(8,128)(2,1)S(1)} %get-tuple-element.166), channel_id=1, source_target_pairs={{0,4},{1,5},{2,6},{3,7},{4,0},{5,1},{6,2},{7,3},{8,12},{9,13},{10,... | collective-permute-start | bytes 110600 | tf_op jit(solution)/shard_map/ppermute | solution.py:620
  128.1 5.8 %collective-permute-start.56 = (bf16[144,128]{1,0:T(8,128)(2,1)S(1)}, bf16[144,128]{1,0:T(8,128)(2,1)S(1)}, u32[]{:S(2)}, u32[]{:S(2)}) collective-permute-start(bf16[144,128]{1,0:T(8,128)(2,1)S(1)} %get-tuple-element.167), channel_id=1, source_target_pairs={{0,6},{1,7},{2,4},{3,5},{4,2},{5,3},{6,0},{7,1},{8,14},{9,15},{10,... | collective-permute-start | bytes 110600 | tf_op jit(solution)/shard_map/ppermute | solution.py:620
